TPU v7x, 32 devices: a whole 2x2x4 slice. The times are simulated.
32 devices in a mesh: dp: 8 (over z, x), fsdp: 4 (over y, core).
Axes of the slice: x: 2, y: 2, z: 4, core: 2. Of those that a mesh axis runs over, the one named last changes fastest.
Arguments:
- queries: bfloat16 [4, 16, 128, 2048], P('fsdp', 'dp'), may hold values from -6 to 6
- response_key_value: bfloat16 [4, 16, 128, 2048], P('fsdp', 'dp'), may hold values from -6 to 6
- prompt_kv: bfloat16 [4, 1024, 2048], P('fsdp', 'dp'), may hold values from -6 to 6
- out_weight: bfloat16 [2048, 4608], P(None, 'fsdp'), may hold values from -0.125 to 0.125
- residual: bfloat16 [4, 16, 128, 4608], P('fsdp', 'dp'), may hold values from -6 to 6
- post_gain: float32 [4608], replicated, may hold values from 0.1 to 1.9
- final_gain: float32 [4608], replicated, may hold values from 0.1 to 1.9
- target_rows: bfloat16 [4, 16, 128, 4608], P('fsdp', 'dp'), may hold values from -0.046875 to 0.046875
- log_norm: float32 [4, 16, 128], P('fsdp', 'dp'), may hold values from 9.5 to 10.5
- old_logp: float32 [4, 16, 128], P('fsdp', 'dp'), may hold values from -10.5 to -9.5
- ref_logp: float32 [4, 16, 128], P('fsdp', 'dp'), may hold values from -10.5 to -9.5
- lengths: int32 [4, 16], P('fsdp', 'dp'), may hold values from 1 to 128, 682 in all within a row
- rewards: float32 [4, 16], P('fsdp', 'dp'), may hold values from -4 to 4
Outputs:
- log_ratio: float32 [4, 16, 128], P('fsdp', 'dp')
- kl_terms: float32 [4, 16, 128], P('fsdp', 'dp')
- objective: float32 [4, 16, 128], P('fsdp', 'dp')
- batch_loss: float32 [], replicated
Inputs may be any that keep to these rules, and one draw needn't show every extreme that they name: The 16 lengths of each prompt sum to 682, and the largest of each prompt is exactly 128.
All inputs are finite; a program needn't handle non-finite values.
Results may differ from a plain program's by a relative error of at most 0.0033.
Values may be sent and summed in bfloat16 or wider, within the bound.
No kernel may reach another device: no remote copies, remote signals or barrier semaphores. Data moves between devices by JAX's collectives and lax.ppermute only.
A program may use at most 128 MiB of HBM per device.

v0:
```python
import jax
import jax.numpy as jnp
from jax import lax
from jax.sharding import PartitionSpec as P

D = 4608
QUERY_HEADS = 16
KEY_VALUE_HEADS = 8
HEAD_SIZE = 128
QPRE = 144


def capped(values, limit):
    return limit * jnp.tanh(values / limit)


def rms_scaled(values, gain):
    mean_square = jnp.mean(values * values, axis=-1, keepdims=True)
    return values * lax.rsqrt(mean_square + 1e-06) * gain


def body(
    queries,
    response_key_value,
    prompt_kv,
    out_weight,
    residual,
    post_gain,
    final_gain,
    target_rows,
    log_norm,
    old_logp,
    ref_logp,
    lengths,
    rewards,
):
    cache_slots = queries.shape[1]
    token_positions = queries.shape[2]
    tokens_here = cache_slots * token_positions
    per_key_value = QUERY_HEADS // KEY_VALUE_HEADS
    key_value_width = KEY_VALUE_HEADS * HEAD_SIZE
    score_scale = QPRE ** (-0.5)
    query_result = queries[0].reshape(
        cache_slots, token_positions, KEY_VALUE_HEADS, per_key_value, HEAD_SIZE
    )
    response_keys = response_key_value[0, :, :, :key_value_width].reshape(
        cache_slots, token_positions, KEY_VALUE_HEADS, HEAD_SIZE
    )
    response_values = response_key_value[0, :, :, key_value_width:].reshape(
        cache_slots, token_positions, KEY_VALUE_HEADS, HEAD_SIZE
    )
    own_scores = capped(
        jnp.einsum(
            "rlkhd,rmkd->rlkhm", query_result, response_keys, preferred_element_type=jnp.float32
        )
        * score_scale,
        50.0,
    )
    later = lax.broadcasted_iota(jnp.int32, (token_positions, token_positions), 0)
    earlier = lax.broadcasted_iota(jnp.int32, (token_positions, token_positions), 1)
    causal = (earlier <= later)[None, :, None, None, :]
    own_weights = jnp.where(causal, jnp.exp(own_scores), 0.0)
    own_numerator = jnp.einsum(
        "rlkhm,rmkd->rlkhd",
        own_weights.astype(jnp.bfloat16),
        response_values,
        preferred_element_type=jnp.float32,
    )
    own_denominator = jnp.sum(own_weights, axis=-1)
    starting = (own_numerator, own_denominator)
    combined_key_value = lax.all_gather(prompt_kv, "dp", axis=1, tiled=True)
    key_matrix_rows = combined_key_value[0, :, :key_value_width].reshape(
        -1, KEY_VALUE_HEADS, HEAD_SIZE
    )
    value_matrix_rows = combined_key_value[0, :, key_value_width:].reshape(
        -1, KEY_VALUE_HEADS, HEAD_SIZE
    )
    scores = capped(
        jnp.einsum(
            "rlkhd,nkd->rlkhn", query_result, key_matrix_rows, preferred_element_type=jnp.float32
        )
        * score_scale,
        50.0,
    )
    weights = jnp.exp(scores)
    numerator = starting[0] + jnp.einsum(
        "rlkhn,nkd->rlkhd",
        weights.astype(jnp.bfloat16),
        value_matrix_rows,
        preferred_element_type=jnp.float32,
    )
    numerator, denominator = (numerator, starting[1] + jnp.sum(weights, axis=-1))
    attended = (
        (numerator / denominator[..., None])
        .astype(jnp.bfloat16)
        .reshape(tokens_here, QUERY_HEADS * HEAD_SIZE)
    )
    projected = jnp.dot(
        attended,
        lax.all_gather(out_weight, "fsdp", axis=1, tiled=True),
        preferred_element_type=jnp.float32,
    )
    mixed = residual[0].reshape(tokens_here, D).astype(jnp.float32) + rms_scaled(
        projected, post_gain
    )
    hidden = rms_scaled(mixed, final_gain)
    logit = capped(
        jnp.sum(hidden * target_rows[0].reshape(tokens_here, D).astype(jnp.float32), axis=-1), 30.0
    )
    logp = logit.reshape(cache_slots, token_positions) - log_norm[0]
    position_ids = lax.broadcasted_iota(jnp.int32, (cache_slots, token_positions), 1)
    live_mask = position_ids < lengths[0][:, None]
    log_ratio = jnp.where(live_mask, logp - old_logp[0], 0.0)
    drift = ref_logp[0] - logp
    kl_terms = jnp.where(live_mask, jnp.exp(drift) - drift - 1.0, 0.0)
    group_sum = lax.psum(jnp.sum(rewards[0]), "dp")
    group_mean = group_sum / (cache_slots * lax.axis_size("dp"))
    advantage = (rewards[0] - group_mean)[:, None]
    prob_ratio = jnp.exp(logp - old_logp[0])
    surrogate = jnp.minimum(prob_ratio * advantage, jnp.clip(prob_ratio, 0.8, 1.2) * advantage)
    objective = jnp.where(live_mask, 0.04 * kl_terms - surrogate, 0.0)
    totals = lax.psum((jnp.sum(objective), jnp.sum(live_mask.astype(jnp.float32))), ("dp", "fsdp"))
    batch_loss = totals[0] / totals[1]
    return (log_ratio[None], kl_terms[None], objective[None], batch_loss)


def solution(mesh):
    in_specs = (
        P("fsdp", "dp", None, None),
        P("fsdp", "dp", None, None),
        P("fsdp", "dp", None),
        P(None, "fsdp"),
        P("fsdp", "dp", None, None),
        P(),
        P(),
        P("fsdp", "dp", None, None),
        P("fsdp", "dp", None),
        P("fsdp", "dp", None),
        P("fsdp", "dp", None),
        P("fsdp", "dp"),
        P("fsdp", "dp"),
    )
    out_specs = (P("fsdp", "dp", None), P("fsdp", "dp", None), P("fsdp", "dp", None), P())
    return jax.shard_map(body, mesh=mesh, in_specs=in_specs, out_specs=out_specs, check_vma=False)
```

profile of v0, /device:TPU:0, one launch (start us, length us, event | category | flops | bytes accessed | tf_op | source)
XLA Modules:
  0.0 270.6 jit_solution(7256983199510320651)
XLA Ops:
  7.2 0.0 all-gather.3.cloned.1.call-start
  7.2 2.2 copy.54
  9.4 0.0 all-gather.3.cloned.1.call-update
  9.5 0.0 all-gather.5.cloned.1.call-start
  9.5 0.7 all-gather.5.cloned.1.call-update
  10.2 0.6 reduce_sum.77
  10.8 24.1 %psum.21 = f32[]{:T(128)} all-reduce(f32[]{:T(128)} %reduce_sum.77), channel_id=1, replica_groups=mesh['dp'=8,'fsdp'=4] {'dp'}, use_global_device_ids=true, to_apply=%region_6.7 | all-reduce | flops 1 | bytes 8 | tf_op jit(solution)/shard_map/psum | solution.py:116
  35.0 0.7 reshape_squeeze.18
  35.7 0.1 fusion.21
  35.8 0.3 copy.76
  36.1 0.3 copy.77
  37.1 2.0 fusion.22
  39.1 49.0 %all-gather.3.cloned.1.call-done = bf16[1,1024,2048]{1,2,0:T(8,128)(2,1)} async-done(((bf16[1,128,2048]{1,2,0:T(8,128)(2,1)}), bf16[1,1024,2048]{1,2,0:T(8,128)(2,1)}) %all-gather.3.cloned.1.call-update) | async-done | bytes 4194320 | tf_op jit(solution)/shard_map/all_gather | solution.py:71
  88.1 4.0 %fusion.20 = (bf16[1,1024,1024]{1,2,0:T(8,128)(2,1)S(1)}, bf16[1,1024,1024]{1,2,0:T(8,128)(2,1)}) fusion(bf16[1,1024,2048]{1,2,0:T(8,128)(2,1)} %all-gather.3.cloned.1.call-done), kind=kLoop, calls=%fused_computation.44 | loop fusion | bytes 8388608 | tf_op jit(solution)/shard_map/slice | solution.py:72
  92.0 7.6 %bitcast_convert_fusion = (bf16[2,128,8,2,1024]{1,4,3,0,2:T(8,128)(2,1)}, f32[8,1024,2,128,2]{3,1,4,2,0:T(8,128)S(1)}) fusion(bf16[1024,8,128,1,1]{0,2,4,3,1:T(8,128)(2,1)S(1)} %bitcast.87, bf16[2,128,8,2,128]{4,3,2,1,0:T(2,128)(2,1)S(1)} %reshape_squeeze.18), kind=kOutput, calls=%fused_computation.1 | convolution fusion | flops 1086324736 | bytes 28311552 | tf_op jit(solution)/shard_map/rlkhd,nkd->rlkhn/dot_general | solution.py:79
  99.6 4.8 %bitcast_reduce_fusion = f32[2,128,8,2]{1,3,0,2:T(2,128)S(1)} fusion(f32[8,1024,2,128,2]{3,1,4,2,0:T(8,128)S(1)} %get-tuple-element.16), kind=kLoop, calls=%fused_computation | loop fusion | flops 12578816 | bytes 16793600 | tf_op jit(solution)/shard_map/reduce_sum | solution.py:92
  104.5 7.0 %fusion = f32[8,2,128,2,128]{4,2,3,0,1:T(8,128)S(1)} fusion(bf16[1024,8,128,1,1]{0,2,4,1,3:T(8,128)(2,1)S(1)} %bitcast.88, bf16[2,128,8,2,1024]{1,4,3,0,2:T(8,128)(2,1)} %get-tuple-element.15), kind=kOutput, calls=%fused_computation.3 | convolution fusion | flops 1073741824 | bytes 12582912 | tf_op jit(solution)/shard_map/rlkhn,nkd->rlkhd/dot_general | solution.py:86
  111.5 1.1 fusion.4
  112.6 1.1 copy.60
  113.7 0.8 reshape.142
  114.5 0.0 copy-start
  114.5 0.0 copy-start.5
  114.5 93.3 %all-gather.5.cloned.1.call-done = bf16[2048,4608]{1,0:T(8,128)(2,1)} async-done(((bf16[2048,1152]{1,0:T(8,128)(2,1)}), bf16[2048,4608]{1,0:T(8,128)(2,1)}) %all-gather.5.cloned.1.call-update) | async-done | bytes 18874384 | tf_op jit(solution)/shard_map/all_gather | solution.py:100
  207.8 9.1 %multiply_reduce_fusion.1 = (f32[256]{0:T(256)S(1)}, f32[256,4608]{1,0:T(8,128)S(1)}) fusion(bf16[256,2048]{1,0:T(8,128)(2,1)S(1)} %reshape.142, bf16[2048,4608]{1,0:T(8,128)(2,1)} %all-gather.5.cloned.1.call-done), kind=kOutput, calls=%fused_computation.9 | convolution fusion | flops 4834197504 | bytes 24642560 | tf_op jit(solution)/shard_map/dot_general | solution.py:98
  216.9 0.0 copy-start.6
  216.9 1.2 multiply_reduce_fusion
  218.1 0.4 copy-done.1
  218.6 0.0 copy-start.10
  218.6 1.8 fusion.2
  220.4 0.8 convert_reduce_fusion
  221.2 0.6 subtract_select_fusion
  221.8 39.6 %all-reduce = (f32[]{:T(128)}, f32[]{:T(128)}) all-reduce(f32[]{:T(128)} %get-tuple-element.5, f32[]{:T(128)} %get-tuple-element.4), channel_id=1, replica_groups=mesh['dp'=8,'fsdp'=4] {'dp','fsdp'}, use_global_device_ids=true, to_apply=%region_8.9 | all-reduce | flops 2 | bytes 16 | tf_op jit(solution)/shard_map/psum | solution.py:122
  (26 shorter events, 0.1 us)
Async XLA Ops:
  7.2 3.1 %copy-start.11 = (f32[1,2]{1,0:T(1,128)S(1)}, f32[1,2]{1,0:T(1,128)}, u32[]{:S(2)}) copy-start(f32[1,2]{1,0:T(1,128)} %param.25) | copy-start | bytes 28
  7.2 27.8 %copy-start.3 = (bf16[1,2,128,2048]{3,2,1,0:T(8,128)(2,1)S(1)}, bf16[1,2,128,2048]{3,2,1,0:T(8,128)(2,1)}, u32[]{:S(2)}) copy-start(bf16[1,2,128,2048]{3,2,1,0:T(8,128)(2,1)} %param.13) | copy-start | bytes 3145732
  7.2 28.6 %copy-start.4 = (bf16[1,2,128,2048]{3,2,1,0:T(8,128)(2,1)S(1)}, bf16[1,2,128,2048]{3,2,1,0:T(8,128)(2,1)}, u32[]{:S(2)}) copy-start(bf16[1,2,128,2048]{3,2,1,0:T(8,128)(2,1)} %param.14) | copy-start | bytes 3145732
  7.2 80.9 %all-gather.3.cloned.1.call-start = ((), (), s32[]{:S(2)}) async-start(), calls=%async_computation | async-start | bytes 4718592 | tf_op jit(solution)/shard_map/all_gather | solution.py:71
  9.5 198.3 %all-gather.5.cloned.1.call-start = ((), (), s32[]{:S(2)}) async-start(), calls=%async_computation.1 | async-start | bytes 23592960 | tf_op jit(solution)/shard_map/all_gather | solution.py:100
  99.6 4.9 %copy-start.2 = (bf16[1,1024,1024]{1,2,0:T(8,128)(2,1)S(1)}, bf16[1,1024,1024]{1,2,0:T(8,128)(2,1)}, u32[]{:S(2)}) copy-start(bf16[1,1024,1024]{1,2,0:T(8,128)(2,1)} %get-tuple-element.11) | copy-start | bytes 6291460
  104.5 7.0 %copy-start.12 = (bf16[2,128,8,2,128]{1,4,3,2,0:T(8,128)(2,1)S(1)}, bf16[2,128,8,2,128]{1,4,3,2,0:T(8,128)(2,1)}, u32[]{:S(2)}) copy-start(bf16[2,128,8,2,128]{1,4,3,2,0:T(8,128)(2,1)} %get-tuple-element.18) | copy-start | bytes 3145732
  114.5 102.4 %copy-start = (bf16[1,2,128,4608]{3,2,1,0:T(8,128)(2,1)S(1)}, bf16[1,2,128,4608]{3,2,1,0:T(8,128)(2,1)}, u32[]{:S(2)}) copy-start(bf16[1,2,128,4608]{3,2,1,0:T(8,128)(2,1)} %param.17) | copy-start | bytes 7077892
  114.5 102.4 %copy-start.5 = (f32[4608]{0:T(1024)S(1)}, f32[4608]{0:T(1024)}, u32[]{:S(2)}) copy-start(f32[4608]{0:T(1024)} %param.18) | copy-start | bytes 55300
  216.9 1.7 copy-start.1
  216.9 1.7 copy-start.6
  218.6 1.8 copy-start.7
  218.6 1.8 copy-start.8
  218.6 1.9 copy-start.9
  218.6 1.9 copy-start.10
Sparse Core Ops, SparseCore 0:
  10.1 77.9 all-gather.2
  89.7 118.0 all-gather.4
where the time goes:
time: 271 us
  waiting for transfers between devices  143 us (53%)
  blocking collectives  63.7 us (24%)
  matrix products  26.7 us (10%)
  between operations  17.3 us (6%)
  local copies, waits for them, and re-layouts  9.9 us (4%)
  other arithmetic  9.88 us (4%)
    all_gather x1, waiting for transfers between devices, body(): lax.all_gather(out_weight, 'fsdp', axis=1, tiled=True)  93.3 us
    all_gather x1, waiting for transfers between devices, body(): combined_key_value = lax.all_gather(prompt_kv, 'dp', axis=1, tiled=True)  49 us
    psum x1, blocking collectives, body(): lax.psum((jnp.sum(objective), jnp.sum(live_mask.astype(jnp.float32))), ('...  39.6 us
    psum x1, blocking collectives, body(): group_sum = lax.psum(jnp.sum(rewards[0]), 'dp')  24.1 us
    dot_general x1, matrix products, body(): jnp.dot(attended, lax.all_gather(out_weight, 'fsdp', axis=1, tiled=True),...  9.1 us
    dot_general x1, matrix products, body(): jnp.einsum('rlkhd,nkd->rlkhn', query_result, key_matrix_rows, preferred_e...  7.56 us
    dot_general x1, matrix products, body(): jnp.einsum('rlkhn,nkd->rlkhd', weights.astype(jnp.bfloat16), value_matrix...  6.99 us
  transfers between devices with their start and end apart: 2, of which 2 were waited for; matrix products, arithmetic and copies ran while one was open for 11% of the time, Pallas kernels for 0%

commit v1 on v0

v1 whole, which is shorter than its diff:
```python
import functools
import math

import jax
import jax.numpy as jnp
from jax import lax
from jax.experimental import pallas as pl
from jax.experimental.pallas import tpu as pltpu
from jax.sharding import PartitionSpec as P

D = 4608
KEY_VALUE_HEADS = 8
PER_KEY_VALUE = 2
HEAD_SIZE = 128
QPRE = 144
GROUPS = 2
SUMS = 8


def swap(value, axis, bit):
    count = lax.axis_size(axis)
    return lax.ppermute(value, axis, [(i, i ^ bit) for i in range(count)])


def around(value, axis):
    half = lax.axis_size(axis) // 2
    order = list(range(0, half, 2)) + list(range(1, half, 2))[::-1]
    after = {order[i]: order[(i + 1) % half] for i in range(half)}
    return lax.ppermute(
        value, axis, [(i, after[i // 2] * 2 + i % 2) for i in range(2 * half)]
    )


def attention_kernel(count, q_ref, rk_ref, rv_ref, *refs):
    key_refs, value_refs, out_ref = refs[:count], refs[count : 2 * count], refs[-1]
    responses, length, _ = q_ref.shape
    tokens = responses * length
    inner = QPRE**-0.5 / 50.0
    outer = 50.0 * math.log2(math.e)
    q = q_ref[...].reshape(tokens, PER_KEY_VALUE * HEAD_SIZE)
    heads = [q[:, h * HEAD_SIZE : (h + 1) * HEAD_SIZE] for h in range(PER_KEY_VALUE)]
    keys = jnp.concatenate([ref[...] for ref in key_refs], axis=0)
    values = jnp.concatenate([ref[...] for ref in value_refs], axis=0)
    later = lax.broadcasted_iota(jnp.int32, (length, length), 0)
    earlier = lax.broadcasted_iota(jnp.int32, (length, length), 1)
    causal = earlier <= later
    chunk = 256

    def weigh(q_rows, k_rows):
        scores = lax.dot_general(
            q_rows, k_rows, (((1,), (1,)), ((), ())), preferred_element_type=jnp.float32
        )
        return jnp.exp2(outer * jnp.tanh(scores * inner))

    for h in range(PER_KEY_VALUE):
        for r in range(responses):
            rows = heads[h][r * length : (r + 1) * length]
            own = jnp.where(causal, weigh(rows, rk_ref[r]), 0.0)
            total = own
            numerator = jnp.dot(
                own.astype(jnp.bfloat16), rv_ref[r], preferred_element_type=jnp.float32
            )
            for start in range(0, keys.shape[0], chunk):
                weights = weigh(rows, keys[start : start + chunk])
                for lane in range(0, chunk, HEAD_SIZE):
                    total = total + weights[:, lane : lane + HEAD_SIZE]
                numerator = numerator + jnp.dot(
                    weights.astype(jnp.bfloat16),
                    values[start : start + chunk],
                    preferred_element_type=jnp.float32,
                )
            denominator = jnp.sum(total, axis=-1, keepdims=True)
            out_ref[r * length : (r + 1) * length, h * HEAD_SIZE : (h + 1) * HEAD_SIZE] = (
                numerator / denominator
            ).astype(jnp.bfloat16)


def attend(queries, response_key_value, blocks, group):
    responses, length, _ = queries.shape
    per_group = KEY_VALUE_HEADS // GROUPS
    count = len(blocks)
    rows = blocks[0].shape[0]
    width = PER_KEY_VALUE * HEAD_SIZE
    first = group * per_group
    in_specs = [
        pl.BlockSpec((responses, length, width), lambda i: (0, 0, first + i)),
        pl.BlockSpec((responses, length, HEAD_SIZE), lambda i: (0, 0, first + i)),
        pl.BlockSpec((responses, length, HEAD_SIZE), lambda i: (0, 0, KEY_VALUE_HEADS + first + i)),
    ]
    in_specs += [pl.BlockSpec((rows, HEAD_SIZE), lambda i: (0, i))] * count
    in_specs += [pl.BlockSpec((rows, HEAD_SIZE), lambda i: (0, per_group + i))] * count
    tokens = responses * length
    return pl.pallas_call(
        functools.partial(attention_kernel, count),
        grid=(per_group,),
        in_specs=in_specs,
        out_specs=pl.BlockSpec((tokens, width), lambda i: (0, i)),
        out_shape=jax.ShapeDtypeStruct((tokens, per_group * width), jnp.bfloat16),
        compiler_params=pltpu.CompilerParams(vmem_limit_bytes=32 * 1024 * 1024),
        cost_estimate=pl.CostEstimate(
            flops=2 * 2 * tokens * 2 * per_group * 1152 * 128,
            bytes_accessed=4 * 1024 * 1024,
            transcendentals=2 * tokens * 2 * per_group * 1152,
        ),
    )(queries, response_key_value, response_key_value, *blocks, *blocks)


def project_kernel(sources, weight_ref, gain_ref, *refs):
    out_ref = refs[-1]
    post = gain_ref[0:1, :]
    final = gain_ref[1:2, :]
    part = weight_ref.shape[0] // GROUPS
    for s in range(sources):
        tail_ref = refs[s * (GROUPS + 1)]
        attended = [refs[s * (GROUPS + 1) + 1 + g] for g in range(GROUPS)]
        tokens = attended[0].shape[0]
        projected = jnp.dot(
            attended[0][...], weight_ref[0:part, :], preferred_element_type=jnp.float32
        )
        for g in range(1, GROUPS):
            projected += jnp.dot(
                attended[g][...],
                weight_ref[g * part : (g + 1) * part, :],
                preferred_element_type=jnp.float32,
            )
        residual = tail_ref[0:tokens, :].astype(jnp.float32)
        target = tail_ref[tokens : 2 * tokens, :].astype(jnp.float32) * final
        scaled = projected * post
        lane = lax.broadcasted_iota(jnp.int32, (tokens, 128), 1)
        packed = jnp.zeros((tokens, 128), jnp.float32)
        terms = (
            projected * projected,
            residual * scaled,
            scaled * scaled,
            target * scaled,
            residual * residual,
            residual * target,
        )
        for k, term in enumerate(terms):
            packed = jnp.where(lane == k, jnp.sum(term, axis=-1, keepdims=True), packed)
        out_ref[s] = jnp.transpose(packed)[0:SUMS, :]


def project(weight, gains, tails, attended):
    sources = len(tails)
    tokens = attended[0][0].shape[0]
    width = weight.shape[1]
    operands = [weight, gains]
    for s in range(sources):
        operands += [tails[s]] + list(attended[s])
    return pl.pallas_call(
        functools.partial(project_kernel, sources),
        out_shape=jax.ShapeDtypeStruct((sources, SUMS, tokens), jnp.float32),
        compiler_params=pltpu.CompilerParams(vmem_limit_bytes=48 * 1024 * 1024),
        cost_estimate=pl.CostEstimate(
            flops=2 * sources * tokens * 2048 * width,
            bytes_accessed=8 * 1024 * 1024,
            transcendentals=0,
        ),
    )(*operands)


def body(
    queries,
    response_key_value,
    prompt_kv,
    out_weight,
    residual,
    post_gain,
    final_gain,
    target_rows,
    log_norm,
    old_logp,
    ref_logp,
    lengths,
    rewards,
):
    _, responses, length, _ = queries.shape
    tokens = responses * length
    fsdp = lax.axis_size("fsdp")
    dp = lax.axis_size("dp")
    here = lax.axis_index("fsdp")
    columns = D // fsdp
    key_value_width = KEY_VALUE_HEADS * HEAD_SIZE
    part = key_value_width // GROUPS

    gathered = []
    for g in range(GROUPS):
        block = jnp.concatenate(
            [
                prompt_kv[0, :, g * part : (g + 1) * part],
                prompt_kv[0, :, key_value_width + g * part : key_value_width + (g + 1) * part],
            ],
            axis=1,
        )
        blocks = [block, swap(block, "dp", 1)]
        for _ in range(dp // 2 - 1):
            block = around(block, "dp")
            blocks += [block, swap(block, "dp", 1)]
        gathered.append(blocks)

    tail = jnp.concatenate(
        [residual[0].reshape(tokens, D), target_rows[0].reshape(tokens, D)], axis=0
    )
    tails = []
    for k in range(fsdp):
        piece = lax.dynamic_slice_in_dim(tail, (here ^ k) * columns, columns, 1)
        tails.append(swap(piece, "fsdp", k) if k else piece)
    gains = lax.dynamic_slice_in_dim(
        jnp.stack([post_gain, final_gain]), here * columns, columns, 1
    )

    sums = jnp.stack([jnp.sum(rewards[0]), jnp.sum(lengths[0]).astype(jnp.float32)])
    sums = jnp.pad(sums[None], ((0, 0), (0, 126)))
    bit = 1
    while bit < dp:
        sums = sums + swap(sums, "dp", bit)
        bit *= 2
    meta = jnp.concatenate(
        [sums[0, :2], rewards[0], lengths[0].astype(jnp.float32)]
    )
    meta = jnp.pad(meta[None], ((0, 0), (0, length - meta.shape[0])))
    facts = [jnp.concatenate([log_norm[0], old_logp[0], ref_logp[0], meta], axis=0)]
    bit = 1
    while bit < fsdp:
        facts = facts + [swap(value, "fsdp", bit) for value in facts]
        bit *= 2
    facts = jnp.stack(facts)

    attended = [[None] * GROUPS for _ in range(fsdp)]
    for g in range(GROUPS):
        attended[0][g] = attend(queries[0], response_key_value[0], gathered[g], g)
        bit = fsdp // 2
        known = [0]
        while bit:
            for k in known:
                attended[k ^ bit][g] = swap(attended[k][g], "fsdp", bit)
            known = known + [k ^ bit for k in known]
            bit //= 2

    near = list(range(min(2, fsdp)))
    far = list(range(2, fsdp))
    parts = []
    for some in (near, far):
        parts.append(
            project(out_weight, gains, [tails[k] for k in some], [attended[k] for k in some])
        )
    totals = jnp.concatenate(parts, axis=0)
    bit = 1
    while bit < fsdp:
        other = swap(totals, "fsdp", bit)
        totals = totals + jnp.stack([other[k ^ bit] for k in range(fsdp)])
        bit *= 2

    totals = totals.reshape(fsdp, SUMS, responses, length)
    inverse = lax.rsqrt(totals[:, 0] / D + 1e-06)
    square = totals[:, 4] + inverse * (2.0 * totals[:, 1] + inverse * totals[:, 2])
    outer = lax.rsqrt(jnp.maximum(square, 0.0) / D + 1e-06)
    raw = outer * (totals[:, 5] + inverse * totals[:, 3])
    logit = 30.0 * jnp.tanh(raw / 30.0)
    logp = logit - facts[:, 0:responses]
    old = facts[:, responses : 2 * responses]
    ref = facts[:, 2 * responses : 3 * responses]
    meta = facts[:, 3 * responses]
    group_sum, group_count = meta[:, 0], meta[:, 1]
    reward = meta[:, 2 : 2 + responses]
    size = meta[:, 2 + responses : 2 + 2 * responses].astype(jnp.int32)
    position = lax.broadcasted_iota(jnp.int32, (fsdp, responses, length), 2)
    live = position < size[:, :, None]
    log_ratio = jnp.where(live, logp - old, 0.0)
    drift = ref - logp
    kl_terms = jnp.where(live, jnp.exp(drift) - drift - 1.0, 0.0)
    advantage = (reward - (group_sum / (responses * dp))[:, None])[:, :, None]
    ratio = jnp.exp(logp - old)
    surrogate = jnp.minimum(ratio * advantage, jnp.clip(ratio, 0.8, 1.2) * advantage)
    objective = jnp.where(live, 0.04 * kl_terms - surrogate, 0.0)
    loss = jnp.full((1, 128), jnp.sum(objective))
    bit = 1
    while bit < dp:
        loss = loss + swap(loss, "dp", bit)
        bit *= 2
    batch_loss = loss[0, 0] / jnp.sum(group_count)
    return (log_ratio[:1], kl_terms[:1], objective[:1], batch_loss)


def solution(mesh):
    rows4 = P("fsdp", "dp", None, None)
    rows3 = P("fsdp", "dp", None)
    in_specs = (
        rows4,
        rows4,
        rows3,
        P(None, "fsdp"),
        rows4,
        P(),
        P(),
        rows4,
        rows3,
        rows3,
        rows3,
        P("fsdp", "dp"),
        P("fsdp", "dp"),
    )
    out_specs = (rows3, rows3, rows3, P())
    return jax.shard_map(body, mesh=mesh, in_specs=in_specs, out_specs=out_specs, check_vma=False)
```

time: 271 us -> 178 us (0.66)
  blocking collectives: 63.7 us -> 0 us
  waiting for transfers between devices: 143 us -> 99.7 us
  starting transfers between devices: 0.08 us -> 32.9 us
  Pallas kernels: 0 us -> 29.1 us
  matrix products: 26.7 us -> 0 us
  between operations: 17.3 us -> 3.45 us
  local copies, waits for them, and re-layouts: 9.9 us -> 3.06 us
    all_gather x2 -> x0, waiting for transfers between devices: 142 us -> none  [the longest x1 93.3 us: body(): lax.all_gather(out_weight, 'fsdp', axis=1, tiled=True)]
    ppermute x0 -> x34, waiting for transfers between devices: none -> 99.7 us  [the longest x28 96.7 us: swap(): return lax.ppermute(value, axis, [(i, i ^ bit) for i in range(count)])]
    psum x2 -> x0, blocking collectives: 63.7 us -> none  [the longest x1 39.6 us: body(): lax.psum((jnp.sum(objective), jnp.sum(live_mask.astype(jnp.float32))), ('...]
    ppermute x0 -> x34, starting transfers between devices: none -> 32.9 us  [the longest x28 22.5 us: swap(): return lax.ppermute(value, axis, [(i, i ^ bit) for i in range(count)])]
    pallas_call x0 -> x4, Pallas kernels: none -> 29.1 us  [the longest x2 16.9 us: attend(): pl.pallas_call(functools.partial(attention_kernel, count), grid=(per_grou...]
    dot_general x5 -> x0, matrix products: 26.7 us -> none  [the longest x1 9.1 us: body(): jnp.dot(attended, lax.all_gather(out_weight, 'fsdp', axis=1, tiled=True),...]
    reduce_sum x5 -> x4, other arithmetic: 9.19 us -> 3.98 us  [the longest x1 1.37 us: body(): jnp.sum(lengths[0]).astype(jnp.float32)]
    unnamed x29 -> x16, local copies, waits for them, and re-layouts: 3.22 us -> 0.03 us
  transfers between devices with their start and end apart: 2 -> 34, of which waited for: 2 -> 20; matrix products, arithmetic and copies ran while one was open for 11% -> 5% of each run, Pallas kernels for 0% -> 13%
where the time goes in v1:
time: 178 us
  waiting for transfers between devices  99.7 us (56%)
  starting transfers between devices  32.9 us (18%)
  Pallas kernels  29.1 us (16%)
  other arithmetic  9.79 us (5%)
  between operations  3.45 us (2%)
  local copies, waits for them, and re-layouts  3.06 us (2%)
    ppermute x28, waiting for transfers between devices, swap(): return lax.ppermute(value, axis, [(i, i ^ bit) for i in range(count)])  96.7 us
    ppermute x28, starting transfers between devices, swap(): return lax.ppermute(value, axis, [(i, i ^ bit) for i in range(count)])  22.5 us
    pallas_call x2, Pallas kernels, attend(): pl.pallas_call(functools.partial(attention_kernel, count), grid=(per_grou...  16.9 us
    pallas_call x2, Pallas kernels, project(): pl.pallas_call(functools.partial(project_kernel, sources), out_shape=jax....  12.2 us
    ppermute x6, starting transfers between devices, around(): lax.ppermute(value, axis, [(i, after[i // 2] * 2 + i % 2) for i in range(...  10.3 us
  transfers between devices with their start and end apart: 34, of which 20 were waited for; matrix products, arithmetic and copies ran while one was open for 5% of the time, Pallas kernels for 13%

profile of v1, /device:TPU:0, one launch (start us, length us, event | category | flops | bytes accessed | tf_op | source)
XLA Modules:
  0.0 178.0 jit_solution(7102327126869120634)
XLA Ops:
  1.8 4.1 %collective-permute-start.14 = (bf16[128,1024]{1,0:T(8,128)(2,1)S(1)}, bf16[128,1024]{1,0:T(8,128)(2,1)S(1)}, u32[]{:S(2)}, u32[]{:S(2)}) collective-permute-start(bf16[128,1024]{1,0:T(8,128)(2,1)S(1)} %pad_maximum_fusion.1.refs_0_.refs_8_), channel_id=1, source_target_pairs={{0,16},{4,20},{8,0},{12,4},{16,24},{20,28},{24,8},{28,12},{1,17},{... | collective-permute-start | bytes 786440 | tf_op jit(solution)/shard_map/ppermute | solution.py:29
  5.9 1.6 collective-permute-start.7
  11.6 1.5 collective-permute-start
  13.1 2.8 %fusion.2 = (bf16[512,1152]{1,0:T(8,128)(2,1)S(1)}, bf16[512,1152]{1,0:T(8,128)(2,1)S(1)}, bf16[512,1152]{1,0:T(8,128)(2,1)S(1)}, bf16[512,1152]{1,0:T(8,128)(2,1)S(1)}) fusion(s32[]{:T(128)S(6)} %select_n.24, bf16[256,4608]{1,0:T(8,128)(2,1)} %bitcast.112, bf16[256,4608]{1,0:T(8,128)(2,1)} %bitcast.113, s32[]{:T(128)S(6)} %select_n.23, s32[]{:T(128)S(6)} %select_n.25, ...), kind=kLoop, calls=%fused_computation.10 | loop fusion | flops 9437184 | bytes 9437200 | tf_op jit(solution)/shard_map/concatenate | solution.py:202
  16.4 1.7 collective-permute-start.1
  18.2 6.6 %collective-permute-done.1 = f32[1,128]{1,0:T(1,128)S(1)} collective-permute-done((f32[1,128]{1,0:T(1,128)S(1)}, f32[1,128]{1,0:T(1,128)S(1)}, u32[]{:S(2)}, u32[]{:S(2)}) %collective-permute-start.1) | collective-permute-done | bytes 544 | tf_op jit(solution)/shard_map/ppermute | solution.py:22
  26.6 2.6 %collective-permute-done.2 = f32[1,128]{1,0:T(1,128)S(1)} collective-permute-done((f32[1,128]{1,0:T(1,128)S(1)}, f32[1,128]{1,0:T(1,128)S(1)}, u32[]{:S(2)}, u32[]{:S(2)}) %collective-permute-start.2) | collective-permute-done | bytes 544 | tf_op jit(solution)/shard_map/ppermute | solution.py:22
  32.7 1.5 collective-permute-start.4
  34.2 2.1 %collective-permute-done.4 = f32[7,128]{1,0:T(8,128)S(1)} collective-permute-done((f32[7,128]{1,0:T(8,128)S(1)}, f32[7,128]{1,0:T(8,128)S(1)}, u32[]{:S(2)}, u32[]{:S(2)}) %collective-permute-start.4) | collective-permute-done | bytes 3616 | tf_op jit(solution)/shard_map/ppermute | solution.py:22
  36.3 1.5 collective-permute-start.15
  38.6 2.2 %collective-permute-start.11 = (bf16[128,1024]{1,0:T(8,128)(2,1)S(1)}, bf16[128,1024]{1,0:T(8,128)(2,1)S(1)}, u32[]{:S(2)}, u32[]{:S(2)}) collective-permute-start(bf16[128,1024]{1,0:T(8,128)(2,1)S(1)} %collective-permute-done.9.refs_4_.refs_12_), channel_id=1, source_target_pairs={{0,16},{4,20},{8,0},{12,4},{16,24},{20,28},{24,8},{28,12},{1,17},{... | collective-permute-start | bytes 786440 | tf_op jit(solution)/shard_map/ppermute | solution.py:29
  40.7 2.7 %collective-permute-done.18.refs_6_.refs_14_ = bf16[128,1024]{1,0:T(8,128)(2,1)S(1)} collective-permute-done((bf16[128,1024]{1,0:T(8,128)(2,1)S(1)}, bf16[128,1024]{1,0:T(8,128)(2,1)S(1)}, u32[]{:S(2)}, u32[]{:S(2)}) %collective-permute-start.18) | collective-permute-done | bytes 262176 | tf_op jit(solution)/shard_map/ppermute | solution.py:29
  43.4 2.1 %collective-permute-done.15.refs_3_.refs_11_ = bf16[128,1024]{1,0:T(8,128)(2,1)S(1)} collective-permute-done((bf16[128,1024]{1,0:T(8,128)(2,1)S(1)}, bf16[128,1024]{1,0:T(8,128)(2,1)S(1)}, u32[]{:S(2)}, u32[]{:S(2)}) %collective-permute-start.15) | collective-permute-done | bytes 262176 | tf_op jit(solution)/shard_map/ppermute | solution.py:22
  45.5 1.5 collective-permute-start.6
  47.0 4.1 %collective-permute-done.17.refs_5_.refs_13_ = bf16[128,1024]{1,0:T(8,128)(2,1)S(1)} collective-permute-done((bf16[128,1024]{1,0:T(8,128)(2,1)S(1)}, bf16[128,1024]{1,0:T(8,128)(2,1)S(1)}, u32[]{:S(2)}, u32[]{:S(2)}) %collective-permute-start.17) | collective-permute-done | bytes 262176 | tf_op jit(solution)/shard_map/ppermute | solution.py:22
  53.2 3.6 %collective-permute-done.19.refs_7_.refs_15_ = bf16[128,1024]{1,0:T(8,128)(2,1)S(1)} collective-permute-done((bf16[128,1024]{1,0:T(8,128)(2,1)S(1)}, bf16[128,1024]{1,0:T(8,128)(2,1)S(1)}, u32[]{:S(2)}, u32[]{:S(2)}) %collective-permute-start.19) | collective-permute-done | bytes 262176 | tf_op jit(solution)/shard_map/ppermute | solution.py:22
  58.2 8.5 %shard_map.157.refs_2_ = bf16[256,1024]{1,0:T(8,128)(2,1)S(1)} custom-call(bf16[2,128,2048]{2,1,0:T(8,128)(2,1)S(1)} %bitcast.106, bf16[2,128,2048]{2,1,0:T(8,128)(2,1)S(1)} %bitcast.108, bf16[2,128,2048]{2,1,0:T(8,128)(2,1)S(1)} %bitcast.109, bf16[128,1024]{1,0:T(8,128)(2,1)S(1)} %pad_maximum_fusion.1.refs_0_.refs_8_, ...), custom_call_target="tpu_custom_call" | custom-call | flops 1207959552 | bytes 4194304 | tf_op jit(solution)/shard_map/pallas_call | solution.py:93
  68.0 1.5 collective-permute-start.23
  69.5 4.1 %collective-permute-done.10.refs_5_.refs_13_ = bf16[128,1024]{1,0:T(8,128)(2,1)S(1)} collective-permute-done((bf16[128,1024]{1,0:T(8,128)(2,1)S(1)}, bf16[128,1024]{1,0:T(8,128)(2,1)S(1)}, u32[]{:S(2)}, u32[]{:S(2)}) %collective-permute-start.10) | collective-permute-done | bytes 262176 | tf_op jit(solution)/shard_map/ppermute | solution.py:22
  73.6 3.9 %collective-permute-done.12.refs_7_.refs_15_ = bf16[128,1024]{1,0:T(8,128)(2,1)S(1)} collective-permute-done((bf16[128,1024]{1,0:T(8,128)(2,1)S(1)}, bf16[128,1024]{1,0:T(8,128)(2,1)S(1)}, u32[]{:S(2)}, u32[]{:S(2)}) %collective-permute-start.12) | collective-permute-done | bytes 262176 | tf_op jit(solution)/shard_map/ppermute | solution.py:22
  77.5 1.5 collective-permute-start.5
  79.0 8.5 %shard_map.156.refs_1_ = bf16[256,1024]{1,0:T(8,128)(2,1)S(1)} custom-call(bf16[2,128,2048]{2,1,0:T(8,128)(2,1)S(1)} %bitcast.107, bf16[2,128,2048]{2,1,0:T(8,128)(2,1)S(1)} %bitcast.110, bf16[2,128,2048]{2,1,0:T(8,128)(2,1)S(1)} %bitcast.111, bf16[128,1024]{1,0:T(8,128)(2,1)S(1)} %pad_maximum_fusion.refs_0_.refs_8_, ...), custom_call_target="tpu_custom_call" | custom-call | flops 1207959552 | bytes 4194304 | tf_op jit(solution)/shard_map/pallas_call | solution.py:93
  87.5 33.1 %collective-permute-done.5 = f32[7,128]{1,0:T(8,128)S(1)} collective-permute-done((f32[7,128]{1,0:T(8,128)S(1)}, f32[7,128]{1,0:T(8,128)S(1)}, u32[]{:S(2)}, u32[]{:S(2)}) %collective-permute-start.5) | collective-permute-done | bytes 3616 | tf_op jit(solution)/shard_map/ppermute | solution.py:22
  120.5 1.5 collective-permute-start.25
  122.6 12.8 %collective-permute-done.25.refs_2_ = bf16[256,1024]{1,0:T(8,128)(2,1)S(1)} collective-permute-done((bf16[256,1024]{1,0:T(8,128)(2,1)S(1)}, bf16[256,1024]{1,0:T(8,128)(2,1)S(1)}, u32[]{:S(2)}, u32[]{:S(2)}) %collective-permute-start.25) | collective-permute-done | bytes 524320 | tf_op jit(solution)/shard_map/ppermute | solution.py:22
  135.4 8.5 %collective-permute-done.24.refs_1_ = bf16[256,1024]{1,0:T(8,128)(2,1)S(1)} collective-permute-done((bf16[256,1024]{1,0:T(8,128)(2,1)S(1)}, bf16[256,1024]{1,0:T(8,128)(2,1)S(1)}, u32[]{:S(2)}, u32[]{:S(2)}) %collective-permute-start.24) | collective-permute-done | bytes 524320 | tf_op jit(solution)/shard_map/ppermute | solution.py:22
  144.0 6.1 %shard_map.158 = f32[2,8,256]{2,1,0:T(8,128)S(1)} custom-call(bf16[2048,1152]{1,0:T(8,128)(2,1)} %weight_ref.3, f32[2,1152]{1,0:T(2,128)S(1)} %fusion.4.gain_ref, bf16[512,1152]{1,0:T(8,128)(2,1)S(1)} %get-tuple-element.11.refs_0_, bf16[256,1024]{1,0:T(8,128)(2,1)S(1)} %shard_map.156.refs_1_, bf16[256,1024]{1,0:T(8,128)(2,1)S(1)} %shard_map.157.refs_2_, ...), custom_call_target="tpu_custom_call" | custom-call | flops 2415919104 | bytes 8388608 | tf_op jit(solution)/shard_map/pallas_call | solution.py:151
  150.2 6.1 %shard_map.159 = f32[2,8,256]{2,1,0:T(8,128)S(1)} custom-call(bf16[2048,1152]{1,0:T(8,128)(2,1)} %weight_ref.3, f32[2,1152]{1,0:T(2,128)S(1)} %fusion.4.gain_ref, bf16[512,1152]{1,0:T(8,128)(2,1)S(1)} %collective-permute-done.23.refs_0_, bf16[256,1024]{1,0:T(8,128)(2,1)S(1)} %collective-permute-done.24.refs_1_, ...), custom_call_target="tpu_custom_call" | custom-call | flops 2415919104 | bytes 8388608 | tf_op jit(solution)/shard_map/pallas_call | solution.py:151
  157.7 1.6 collective-permute-start.30
  159.5 2.2 %collective-permute-done.30 = f32[4,8,256]{2,1,0:T(8,128)S(1)} collective-permute-done((f32[4,8,256]{2,1,0:T(8,128)S(1)}, f32[4,8,256]{2,1,0:T(8,128)S(1)}, u32[]{:S(2)}, u32[]{:S(2)}) %collective-permute-start.30) | collective-permute-done | bytes 32800 | tf_op jit(solution)/shard_map/ppermute | solution.py:22
  163.2 3.5 %collective-permute-done.31 = f32[1,128]{1,0:T(1,128)S(1)} collective-permute-done((f32[1,128]{1,0:T(1,128)S(1)}, f32[1,128]{1,0:T(1,128)S(1)}, u32[]{:S(2)}, u32[]{:S(2)}) %collective-permute-start.31) | collective-permute-done | bytes 544 | tf_op jit(solution)/shard_map/ppermute | solution.py:22
  167.5 3.5 %collective-permute-done.32 = f32[1,128]{1,0:T(1,128)S(1)} collective-permute-done((f32[1,128]{1,0:T(1,128)S(1)}, f32[1,128]{1,0:T(1,128)S(1)}, u32[]{:S(2)}, u32[]{:S(2)}) %collective-permute-start.32) | collective-permute-done | bytes 544 | tf_op jit(solution)/shard_map/ppermute | solution.py:22
  (97 shorter events, 25.4 us)
Async XLA Ops:
  1.8 14.2 %collective-permute-start.14 = (bf16[128,1024]{1,0:T(8,128)(2,1)S(1)}, bf16[128,1024]{1,0:T(8,128)(2,1)S(1)}, u32[]{:S(2)}, u32[]{:S(2)}) collective-permute-start(bf16[128,1024]{1,0:T(8,128)(2,1)S(1)} %pad_maximum_fusion.1.refs_0_.refs_8_), channel_id=1, source_target_pairs={{0,16},{4,20},{8,0},{12,4},{16,24},{20,28},{24,8},{28,12},{1,17},{... | collective-permute-start | bytes 786440 | tf_op jit(solution)/shard_map/ppermute | solution.py:29
  5.9 23.3 %collective-permute-start.7 = (bf16[128,1024]{1,0:T(8,128)(2,1)S(1)}, bf16[128,1024]{1,0:T(8,128)(2,1)S(1)}, u32[]{:S(2)}, u32[]{:S(2)}) collective-permute-start(bf16[128,1024]{1,0:T(8,128)(2,1)S(1)} %pad_maximum_fusion.refs_0_.refs_8_), channel_id=1, source_target_pairs={{0,16},{4,20},{8,0},{12,4},{16,24},{20,28},{24,8},{28,12},{1,17},{... | collective-permute-start | bytes 786440 | tf_op jit(solution)/shard_map/ppermute | solution.py:29
  11.6 4.9 %collective-permute-start = (f32[1,128]{1,0:T(1,128)S(1)}, f32[1,128]{1,0:T(1,128)S(1)}, u32[]{:S(2)}, u32[]{:S(2)}) collective-permute-start(f32[1,128]{1,0:T(1,128)S(1)} %pad.8), channel_id=1, source_target_pairs={{0,4},{4,0},{8,12},{12,8},{16,20},{20,16},{24,28},{28,24},{1,5},{5... | collective-permute-start | bytes 1544 | tf_op jit(solution)/shard_map/ppermute | solution.py:22
  15.9 106.1 %collective-permute-start.20 = (bf16[512,1152]{1,0:T(8,128)(2,1)S(1)}, bf16[512,1152]{1,0:T(8,128)(2,1)S(1)}, u32[]{:S(2)}, u32[]{:S(2)}) collective-permute-start(bf16[512,1152]{1,0:T(8,128)(2,1)S(1)} %get-tuple-element.10), channel_id=1, source_target_pairs={{0,1},{1,0},{2,3},{3,2},{4,5},{5,4},{6,7},{7,6},{8,9},{9,8},{10,11... | collective-permute-start | bytes 3538952 | tf_op jit(solution)/shard_map/ppermute | solution.py:22
  16.0 14.5 %collective-permute-start.16 = (bf16[128,1024]{1,0:T(8,128)(2,1)S(1)}, bf16[128,1024]{1,0:T(8,128)(2,1)S(1)}, u32[]{:S(2)}, u32[]{:S(2)}) collective-permute-start(bf16[128,1024]{1,0:T(8,128)(2,1)S(1)} %collective-permute-done.14.refs_2_.refs_10_), channel_id=1, source_target_pairs={{0,16},{4,20},{8,0},{12,4},{16,24},{20,28},{24,8},{28,12},{1,17},{... | collective-permute-start | bytes 786440 | tf_op jit(solution)/shard_map/ppermute | solution.py:29
  16.4 8.4 %collective-permute-start.1 = (f32[1,128]{1,0:T(1,128)S(1)}, f32[1,128]{1,0:T(1,128)S(1)}, u32[]{:S(2)}, u32[]{:S(2)}) collective-permute-start(f32[1,128]{1,0:T(1,128)S(1)} %pad_add_fusion), channel_id=1, source_target_pairs={{0,8},{4,12},{8,0},{12,4},{16,24},{20,28},{24,16},{28,20},{1,9},{5... | collective-permute-start | bytes 1544 | tf_op jit(solution)/shard_map/ppermute | solution.py:22
  24.8 4.4 %collective-permute-start.2 = (f32[1,128]{1,0:T(1,128)S(1)}, f32[1,128]{1,0:T(1,128)S(1)}, u32[]{:S(2)}, u32[]{:S(2)}) collective-permute-start(f32[1,128]{1,0:T(1,128)S(1)} %add.63), channel_id=1, source_target_pairs={{0,16},{4,20},{8,24},{12,28},{16,0},{20,4},{24,8},{28,12},{1,17},{... | collective-permute-start | bytes 1544 | tf_op jit(solution)/shard_map/ppermute | solution.py:22
  26.1 11.7 %collective-permute-start.13 = (bf16[128,1024]{1,0:T(8,128)(2,1)S(1)}, bf16[128,1024]{1,0:T(8,128)(2,1)S(1)}, u32[]{:S(2)}, u32[]{:S(2)}) collective-permute-start(bf16[128,1024]{1,0:T(8,128)(2,1)S(1)} %pad_maximum_fusion.1.refs_0_.refs_8_), channel_id=1, source_target_pairs={{0,4},{4,0},{8,12},{12,8},{16,20},{20,16},{24,28},{28,24},{1,5},{5... | collective-permute-start | bytes 786440 | tf_op jit(solution)/shard_map/ppermute | solution.py:22
  29.3 9.3 %collective-permute-start.9 = (bf16[128,1024]{1,0:T(8,128)(2,1)S(1)}, bf16[128,1024]{1,0:T(8,128)(2,1)S(1)}, u32[]{:S(2)}, u32[]{:S(2)}) collective-permute-start(bf16[128,1024]{1,0:T(8,128)(2,1)S(1)} %collective-permute-done.7.refs_2_.refs_10_), channel_id=1, source_target_pairs={{0,16},{4,20},{8,0},{12,4},{16,24},{20,28},{24,8},{28,12},{1,17},{... | collective-permute-start | bytes 786440 | tf_op jit(solution)/shard_map/ppermute | solution.py:29
  30.6 12.8 %collective-permute-start.18 = (bf16[128,1024]{1,0:T(8,128)(2,1)S(1)}, bf16[128,1024]{1,0:T(8,128)(2,1)S(1)}, u32[]{:S(2)}, u32[]{:S(2)}) collective-permute-start(bf16[128,1024]{1,0:T(8,128)(2,1)S(1)} %collective-permute-done.16.refs_4_.refs_12_), channel_id=1, source_target_pairs={{0,16},{4,20},{8,0},{12,4},{16,24},{20,28},{24,8},{28,12},{1,17},{... | collective-permute-start | bytes 786440 | tf_op jit(solution)/shard_map/ppermute | solution.py:29
  32.7 3.6 %collective-permute-start.4 = (f32[7,128]{1,0:T(8,128)S(1)}, f32[7,128]{1,0:T(8,128)S(1)}, u32[]{:S(2)}, u32[]{:S(2)}) collective-permute-start(f32[7,128]{1,0:T(8,128)S(1)} %get-tuple-element.29), channel_id=1, source_target_pairs={{0,2},{1,3},{2,0},{3,1},{4,6},{5,7},{6,4},{7,5},{8,10},{9,11},{10,... | collective-permute-start | bytes 10760 | tf_op jit(solution)/shard_map/ppermute | solution.py:22
  36.3 9.2 %collective-permute-start.15 = (bf16[128,1024]{1,0:T(8,128)(2,1)S(1)}, bf16[128,1024]{1,0:T(8,128)(2,1)S(1)}, u32[]{:S(2)}, u32[]{:S(2)}) collective-permute-start(bf16[128,1024]{1,0:T(8,128)(2,1)S(1)} %collective-permute-done.14.refs_2_.refs_10_), channel_id=1, source_target_pairs={{0,4},{4,0},{8,12},{12,8},{16,20},{20,16},{24,28},{28,24},{1,5},{5... | collective-permute-start | bytes 786440 | tf_op jit(solution)/shard_map/ppermute | solution.py:22
  37.8 13.4 %collective-permute-start.17 = (bf16[128,1024]{1,0:T(8,128)(2,1)S(1)}, bf16[128,1024]{1,0:T(8,128)(2,1)S(1)}, u32[]{:S(2)}, u32[]{:S(2)}) collective-permute-start(bf16[128,1024]{1,0:T(8,128)(2,1)S(1)} %collective-permute-done.16.refs_4_.refs_12_), channel_id=1, source_target_pairs={{0,4},{4,0},{8,12},{12,8},{16,20},{20,16},{24,28},{28,24},{1,5},{5... | collective-permute-start | bytes 786440 | tf_op jit(solution)/shard_map/ppermute | solution.py:22
  38.6 14.1 %collective-permute-start.11 = (bf16[128,1024]{1,0:T(8,128)(2,1)S(1)}, bf16[128,1024]{1,0:T(8,128)(2,1)S(1)}, u32[]{:S(2)}, u32[]{:S(2)}) collective-permute-start(bf16[128,1024]{1,0:T(8,128)(2,1)S(1)} %collective-permute-done.9.refs_4_.refs_12_), channel_id=1, source_target_pairs={{0,16},{4,20},{8,0},{12,4},{16,24},{20,28},{24,8},{28,12},{1,17},{... | collective-permute-start | bytes 786440 | tf_op jit(solution)/shard_map/ppermute | solution.py:29
  43.4 13.3 %collective-permute-start.19 = (bf16[128,1024]{1,0:T(8,128)(2,1)S(1)}, bf16[128,1024]{1,0:T(8,128)(2,1)S(1)}, u32[]{:S(2)}, u32[]{:S(2)}) collective-permute-start(bf16[128,1024]{1,0:T(8,128)(2,1)S(1)} %collective-permute-done.18.refs_6_.refs_14_), channel_id=1, source_target_pairs={{0,4},{4,0},{8,12},{12,8},{16,20},{20,16},{24,28},{28,24},{1,5},{5... | collective-permute-start | bytes 786440 | tf_op jit(solution)/shard_map/ppermute | solution.py:22
  45.5 21.2 %collective-permute-start.6 = (bf16[128,1024]{1,0:T(8,128)(2,1)S(1)}, bf16[128,1024]{1,0:T(8,128)(2,1)S(1)}, u32[]{:S(2)}, u32[]{:S(2)}) collective-permute-start(bf16[128,1024]{1,0:T(8,128)(2,1)S(1)} %pad_maximum_fusion.refs_0_.refs_8_), channel_id=1, source_target_pairs={{0,4},{4,0},{8,12},{12,8},{16,20},{20,16},{24,28},{28,24},{1,5},{5... | collective-permute-start | bytes 786440 | tf_op jit(solution)/shard_map/ppermute | solution.py:22
  51.1 16.9 %collective-permute-start.8 = (bf16[128,1024]{1,0:T(8,128)(2,1)S(1)}, bf16[128,1024]{1,0:T(8,128)(2,1)S(1)}, u32[]{:S(2)}, u32[]{:S(2)}) collective-permute-start(bf16[128,1024]{1,0:T(8,128)(2,1)S(1)} %collective-permute-done.7.refs_2_.refs_10_), channel_id=1, source_target_pairs={{0,4},{4,0},{8,12},{12,8},{16,20},{20,16},{24,28},{28,24},{1,5},{5... | collective-permute-start | bytes 786440 | tf_op jit(solution)/shard_map/ppermute | solution.py:22
  52.6 21.0 %collective-permute-start.10 = (bf16[128,1024]{1,0:T(8,128)(2,1)S(1)}, bf16[128,1024]{1,0:T(8,128)(2,1)S(1)}, u32[]{:S(2)}, u32[]{:S(2)}) collective-permute-start(bf16[128,1024]{1,0:T(8,128)(2,1)S(1)} %collective-permute-done.9.refs_4_.refs_12_), channel_id=1, source_target_pairs={{0,4},{4,0},{8,12},{12,8},{16,20},{20,16},{24,28},{28,24},{1,5},{5... | collective-permute-start | bytes 786440 | tf_op jit(solution)/shard_map/ppermute | solution.py:22
  56.8 20.7 %collective-permute-start.12 = (bf16[128,1024]{1,0:T(8,128)(2,1)S(1)}, bf16[128,1024]{1,0:T(8,128)(2,1)S(1)}, u32[]{:S(2)}, u32[]{:S(2)}) collective-permute-start(bf16[128,1024]{1,0:T(8,128)(2,1)S(1)} %collective-permute-done.11.refs_6_.refs_14_), channel_id=1, source_target_pairs={{0,4},{4,0},{8,12},{12,8},{16,20},{20,16},{24,28},{28,24},{1,5},{5... | collective-permute-start | bytes 786440 | tf_op jit(solution)/shard_map/ppermute | solution.py:22
  66.7 55.9 %collective-permute-start.22 = (bf16[256,1024]{1,0:T(8,128)(2,1)S(1)}, bf16[256,1024]{1,0:T(8,128)(2,1)S(1)}, u32[]{:S(2)}, u32[]{:S(2)}) collective-permute-start(bf16[256,1024]{1,0:T(8,128)(2,1)S(1)} %shard_map.157.refs_2_), channel_id=1, source_target_pairs={{0,1},{1,0},{2,3},{3,2},{4,5},{5,4},{6,7},{7,6},{8,9},{9,8},{10,11... | collective-permute-start | bytes 1572872 | tf_op jit(solution)/shard_map/ppermute | solution.py:22
  68.0 82.2 %collective-permute-start.23 = (bf16[512,1152]{1,0:T(8,128)(2,1)S(1)}, bf16[512,1152]{1,0:T(8,128)(2,1)S(1)}, u32[]{:S(2)}, u32[]{:S(2)}) collective-permute-start(bf16[512,1152]{1,0:T(8,128)(2,1)S(1)} %get-tuple-element.12), channel_id=1, source_target_pairs={{0,2},{1,3},{2,0},{3,1},{4,6},{5,7},{6,4},{7,5},{8,10},{9,11},{10,... | collective-permute-start | bytes 3538952 | tf_op jit(solution)/shard_map/ppermute | solution.py:22
  73.6 76.5 %collective-permute-start.26 = (bf16[512,1152]{1,0:T(8,128)(2,1)S(1)}, bf16[512,1152]{1,0:T(8,128)(2,1)S(1)}, u32[]{:S(2)}, u32[]{:S(2)}) collective-permute-start(bf16[512,1152]{1,0:T(8,128)(2,1)S(1)} %get-tuple-element.13), channel_id=1, source_target_pairs={{0,3},{1,2},{2,1},{3,0},{4,7},{5,6},{6,5},{7,4},{8,11},{9,10},{10,... | collective-permute-start | bytes 3538952 | tf_op jit(solution)/shard_map/ppermute | solution.py:22
  77.5 43.0 %collective-permute-start.5 = (f32[7,128]{1,0:T(8,128)S(1)}, f32[7,128]{1,0:T(8,128)S(1)}, u32[]{:S(2)}, u32[]{:S(2)}) collective-permute-start(f32[7,128]{1,0:T(8,128)S(1)} %collective-permute-done.3), channel_id=1, source_target_pairs={{0,2},{1,3},{2,0},{3,1},{4,6},{5,7},{6,4},{7,5},{8,10},{9,11},{10,... | collective-permute-start | bytes 10760 | tf_op jit(solution)/shard_map/ppermute | solution.py:22
  120.5 14.9 %collective-permute-start.25 = (bf16[256,1024]{1,0:T(8,128)(2,1)S(1)}, bf16[256,1024]{1,0:T(8,128)(2,1)S(1)}, u32[]{:S(2)}, u32[]{:S(2)}) collective-permute-start(bf16[256,1024]{1,0:T(8,128)(2,1)S(1)} %shard_map.157.refs_2_), channel_id=1, source_target_pairs={{0,2},{1,3},{2,0},{3,1},{4,6},{5,7},{6,4},{7,5},{8,10},{9,11},{10,... | collective-permute-start | bytes 1572872 | tf_op jit(solution)/shard_map/ppermute | solution.py:22
  122.1 21.8 %collective-permute-start.24 = (bf16[256,1024]{1,0:T(8,128)(2,1)S(1)}, bf16[256,1024]{1,0:T(8,128)(2,1)S(1)}, u32[]{:S(2)}, u32[]{:S(2)}) collective-permute-start(bf16[256,1024]{1,0:T(8,128)(2,1)S(1)} %shard_map.156.refs_1_), channel_id=1, source_target_pairs={{0,2},{1,3},{2,0},{3,1},{4,6},{5,7},{6,4},{7,5},{8,10},{9,11},{10,... | collective-permute-start | bytes 1572872 | tf_op jit(solution)/shard_map/ppermute | solution.py:22
  122.6 21.4 %collective-permute-start.21 = (bf16[256,1024]{1,0:T(8,128)(2,1)S(1)}, bf16[256,1024]{1,0:T(8,128)(2,1)S(1)}, u32[]{:S(2)}, u32[]{:S(2)}) collective-permute-start(bf16[256,1024]{1,0:T(8,128)(2,1)S(1)} %shard_map.156.refs_1_), channel_id=1, source_target_pairs={{0,1},{1,0},{2,3},{3,2},{4,5},{5,4},{6,7},{7,6},{8,9},{9,8},{10,11... | collective-permute-start | bytes 1572872 | tf_op jit(solution)/shard_map/ppermute | solution.py:22
  135.4 14.8 %collective-permute-start.28 = (bf16[256,1024]{1,0:T(8,128)(2,1)S(1)}, bf16[256,1024]{1,0:T(8,128)(2,1)S(1)}, u32[]{:S(2)}, u32[]{:S(2)}) collective-permute-start(bf16[256,1024]{1,0:T(8,128)(2,1)S(1)} %collective-permute-done.25.refs_2_), channel_id=1, source_target_pairs={{0,1},{1,0},{2,3},{3,2},{4,5},{5,4},{6,7},{7,6},{8,9},{9,8},{10,11... | collective-permute-start | bytes 1572872 | tf_op jit(solution)/shard_map/ppermute | solution.py:22
  143.9 6.3 %collective-permute-start.27 = (bf16[256,1024]{1,0:T(8,128)(2,1)S(1)}, bf16[256,1024]{1,0:T(8,128)(2,1)S(1)}, u32[]{:S(2)}, u32[]{:S(2)}) collective-permute-start(bf16[256,1024]{1,0:T(8,128)(2,1)S(1)} %collective-permute-done.24.refs_1_), channel_id=1, source_target_pairs={{0,1},{1,0},{2,3},{3,2},{4,5},{5,4},{6,7},{7,6},{8,9},{9,8},{10,11... | collective-permute-start | bytes 1572872 | tf_op jit(solution)/shard_map/ppermute | solution.py:22
  157.7 4.0 %collective-permute-start.30 = (f32[4,8,256]{2,1,0:T(8,128)S(1)}, f32[4,8,256]{2,1,0:T(8,128)S(1)}, u32[]{:S(2)}, u32[]{:S(2)}) collective-permute-start(f32[4,8,256]{2,1,0:T(8,128)S(1)} %maximum_add_fusion), channel_id=1, source_target_pairs={{0,2},{1,3},{2,0},{3,1},{4,6},{5,7},{6,4},{7,5},{8,10},{9,11},{10,... | collective-permute-start | bytes 98312 | tf_op jit(solution)/shard_map/ppermute | solution.py:22
  163.1 3.6 %collective-permute-start.31 = (f32[1,128]{1,0:T(1,128)S(1)}, f32[1,128]{1,0:T(1,128)S(1)}, u32[]{:S(2)}, u32[]{:S(2)}) collective-permute-start(f32[1,128]{1,0:T(1,128)S(1)} %broadcast_in_dim.18), channel_id=1, source_target_pairs={{0,4},{4,0},{8,12},{12,8},{16,20},{20,16},{24,28},{28,24},{1,5},{5... | collective-permute-start | bytes 1544 | tf_op jit(solution)/shard_map/ppermute | solution.py:22
  167.3 3.6 %collective-permute-start.32 = (f32[1,128]{1,0:T(1,128)S(1)}, f32[1,128]{1,0:T(1,128)S(1)}, u32[]{:S(2)}, u32[]{:S(2)}) collective-permute-start(f32[1,128]{1,0:T(1,128)S(1)} %broadcast_add_fusion), channel_id=1, source_target_pairs={{0,8},{4,12},{8,0},{12,4},{16,24},{20,28},{24,16},{28,20},{1,9},{5... | collective-permute-start | bytes 1544 | tf_op jit(solution)/shard_map/ppermute | solution.py:22
  171.6 4.5 %collective-permute-start.33 = (f32[1,128]{1,0:T(1,128)S(1)}, f32[1,128]{1,0:T(1,128)S(1)}, u32[]{:S(2)}, u32[]{:S(2)}) collective-permute-start(f32[1,128]{1,0:T(1,128)S(1)} %fusion.26), channel_id=1, source_target_pairs={{0,16},{4,20},{8,24},{12,28},{16,0},{20,4},{24,8},{28,12},{1,17},{... | collective-permute-start | bytes 1544 | tf_op jit(solution)/shard_map/ppermute | solution.py:22
  (10 other events, 264.3 us)

commit v2 on v1

--- a/solution.py
+++ b/solution.py
@@ -44,7 +44,7 @@
     later = lax.broadcasted_iota(jnp.int32, (length, length), 0)
     earlier = lax.broadcasted_iota(jnp.int32, (length, length), 1)
     causal = earlier <= later
-    chunk = 256
+    chunk = 512
 
     def weigh(q_rows, k_rows):
         scores = lax.dot_general(
@@ -52,34 +52,36 @@
         )
         return jnp.exp2(outer * jnp.tanh(scores * inner))
 
+    stack = jnp.concatenate(heads, axis=0)
+    owned, numerators = [], []
     for h in range(PER_KEY_VALUE):
         for r in range(responses):
             rows = heads[h][r * length : (r + 1) * length]
             own = jnp.where(causal, weigh(rows, rk_ref[r]), 0.0)
-            total = own
-            numerator = jnp.dot(
-                own.astype(jnp.bfloat16), rv_ref[r], preferred_element_type=jnp.float32
+            owned.append(own)
+            numerators.append(
+                jnp.dot(own.astype(jnp.bfloat16), rv_ref[r], preferred_element_type=jnp.float32)
             )
-            for start in range(0, keys.shape[0], chunk):
-                weights = weigh(rows, keys[start : start + chunk])
-                for lane in range(0, chunk, HEAD_SIZE):
-                    total = total + weights[:, lane : lane + HEAD_SIZE]
-                numerator = numerator + jnp.dot(
-                    weights.astype(jnp.bfloat16),
-                    values[start : start + chunk],
-                    preferred_element_type=jnp.float32,
-                )
-            denominator = jnp.sum(total, axis=-1, keepdims=True)
-            out_ref[r * length : (r + 1) * length, h * HEAD_SIZE : (h + 1) * HEAD_SIZE] = (
-                numerator / denominator
-            ).astype(jnp.bfloat16)
+    total = jnp.concatenate(owned, axis=0)
+    numerator = jnp.concatenate(numerators, axis=0)
+    for start in range(0, keys.shape[0], chunk):
+        weights = weigh(stack, keys[start : start + chunk])
+        for lane in range(0, chunk, HEAD_SIZE):
+            total = total + weights[:, lane : lane + HEAD_SIZE]
+        numerator = numerator + jnp.dot(
+            weights.astype(jnp.bfloat16),
+            values[start : start + chunk],
+            preferred_element_type=jnp.float32,
+        )
+    result = (numerator / jnp.sum(total, axis=-1, keepdims=True)).astype(jnp.bfloat16)
+    for h in range(PER_KEY_VALUE):
+        out_ref[:, h * HEAD_SIZE : (h + 1) * HEAD_SIZE] = result[h * tokens : (h + 1) * tokens]
 
 
 def attend(queries, response_key_value, blocks, group):
     responses, length, _ = queries.shape
     per_group = KEY_VALUE_HEADS // GROUPS
     count = len(blocks)
-    rows = blocks[0].shape[0]
     width = PER_KEY_VALUE * HEAD_SIZE
     first = group * per_group
     in_specs = [
@@ -87,8 +89,11 @@
         pl.BlockSpec((responses, length, HEAD_SIZE), lambda i: (0, 0, first + i)),
         pl.BlockSpec((responses, length, HEAD_SIZE), lambda i: (0, 0, KEY_VALUE_HEADS + first + i)),
     ]
-    in_specs += [pl.BlockSpec((rows, HEAD_SIZE), lambda i: (0, i))] * count
-    in_specs += [pl.BlockSpec((rows, HEAD_SIZE), lambda i: (0, per_group + i))] * count
+    for offset in (first, KEY_VALUE_HEADS + first):
+        for block in blocks:
+            in_specs.append(
+                pl.BlockSpec((block.shape[0], HEAD_SIZE), lambda i, offset=offset: (0, offset + i))
+            )
     tokens = responses * length
     return pl.pallas_call(
         functools.partial(attention_kernel, count),
@@ -96,7 +101,7 @@
         in_specs=in_specs,
         out_specs=pl.BlockSpec((tokens, width), lambda i: (0, i)),
         out_shape=jax.ShapeDtypeStruct((tokens, per_group * width), jnp.bfloat16),
-        compiler_params=pltpu.CompilerParams(vmem_limit_bytes=32 * 1024 * 1024),
+        compiler_params=pltpu.CompilerParams(vmem_limit_bytes=60 * 1024 * 1024),
         cost_estimate=pl.CostEstimate(
             flops=2 * 2 * tokens * 2 * per_group * 1152 * 128,
             bytes_accessed=4 * 1024 * 1024,
@@ -111,8 +116,7 @@
     final = gain_ref[1:2, :]
     part = weight_ref.shape[0] // GROUPS
     for s in range(sources):
-        tail_ref = refs[s * (GROUPS + 1)]
-        attended = [refs[s * (GROUPS + 1) + 1 + g] for g in range(GROUPS)]
+        stream_ref, target_ref, *attended = refs[s * (GROUPS + 2) : (s + 1) * (GROUPS + 2)]
         tokens = attended[0].shape[0]
         projected = jnp.dot(
             attended[0][...], weight_ref[0:part, :], preferred_element_type=jnp.float32
@@ -123,8 +127,8 @@
                 weight_ref[g * part : (g + 1) * part, :],
                 preferred_element_type=jnp.float32,
             )
-        residual = tail_ref[0:tokens, :].astype(jnp.float32)
-        target = tail_ref[tokens : 2 * tokens, :].astype(jnp.float32) * final
+        residual = stream_ref[...].astype(jnp.float32)
+        target = target_ref[...].astype(jnp.float32) * final
         scaled = projected * post
         lane = lax.broadcasted_iota(jnp.int32, (tokens, 128), 1)
         packed = jnp.zeros((tokens, 128), jnp.float32)
@@ -147,11 +151,11 @@
     width = weight.shape[1]
     operands = [weight, gains]
     for s in range(sources):
-        operands += [tails[s]] + list(attended[s])
+        operands += list(tails[s]) + list(attended[s])
     return pl.pallas_call(
         functools.partial(project_kernel, sources),
         out_shape=jax.ShapeDtypeStruct((sources, SUMS, tokens), jnp.float32),
-        compiler_params=pltpu.CompilerParams(vmem_limit_bytes=48 * 1024 * 1024),
+        compiler_params=pltpu.CompilerParams(vmem_limit_bytes=24 * 1024 * 1024),
         cost_estimate=pl.CostEstimate(
             flops=2 * sources * tokens * 2048 * width,
             bytes_accessed=8 * 1024 * 1024,
@@ -181,70 +185,121 @@
     dp = lax.axis_size("dp")
     here = lax.axis_index("fsdp")
     columns = D // fsdp
-    key_value_width = KEY_VALUE_HEADS * HEAD_SIZE
-    part = key_value_width // GROUPS
-
-    gathered = []
-    for g in range(GROUPS):
-        block = jnp.concatenate(
-            [
-                prompt_kv[0, :, g * part : (g + 1) * part],
-                prompt_kv[0, :, key_value_width + g * part : key_value_width + (g + 1) * part],
-            ],
-            axis=1,
-        )
-        blocks = [block, swap(block, "dp", 1)]
-        for _ in range(dp // 2 - 1):
-            block = around(block, "dp")
-            blocks += [block, swap(block, "dp", 1)]
-        gathered.append(blocks)
-
-    tail = jnp.concatenate(
-        [residual[0].reshape(tokens, D), target_rows[0].reshape(tokens, D)], axis=0
-    )
-    tails = []
-    for k in range(fsdp):
-        piece = lax.dynamic_slice_in_dim(tail, (here ^ k) * columns, columns, 1)
-        tails.append(swap(piece, "fsdp", k) if k else piece)
-    gains = lax.dynamic_slice_in_dim(
-        jnp.stack([post_gain, final_gain]), here * columns, columns, 1
-    )
-
-    sums = jnp.stack([jnp.sum(rewards[0]), jnp.sum(lengths[0]).astype(jnp.float32)])
-    sums = jnp.pad(sums[None], ((0, 0), (0, 126)))
-    bit = 1
-    while bit < dp:
-        sums = sums + swap(sums, "dp", bit)
-        bit *= 2
-    meta = jnp.concatenate(
-        [sums[0, :2], rewards[0], lengths[0].astype(jnp.float32)]
-    )
+
+    streams = (residual[0].reshape(tokens, D), target_rows[0].reshape(tokens, D))
+
+    def cut(which, k):
+        return lax.dynamic_slice_in_dim(streams[which], (here ^ k) * columns, columns, 1)
+
+    tails = {(0, which): cut(which, 0) for which in (0, 1)}
+    far = [(k, which) for k in range(2, fsdp) for which in (0, 1)]
+    for which in (0, 1):
+        tails[1, which] = swap(cut(which, 1), "fsdp", 1)
+
+    meta = jnp.concatenate([rewards[0], lengths[0].astype(jnp.float32)])
     meta = jnp.pad(meta[None], ((0, 0), (0, length - meta.shape[0])))
     facts = [jnp.concatenate([log_norm[0], old_logp[0], ref_logp[0], meta], axis=0)]
     bit = 1
     while bit < fsdp:
         facts = facts + [swap(value, "fsdp", bit) for value in facts]
         bit *= 2
-    facts = jnp.stack(facts)
+
+    def group_sums(facts):
+        meta = jnp.stack([value[-1] for value in facts])
+        lane = lax.broadcasted_iota(jnp.int32, meta.shape, 1)
+        first = jnp.where(lane < responses, meta, 0.0)
+        second = jnp.where((lane >= responses) & (lane < 2 * responses), meta, 0.0)
+        pair = [jnp.sum(value, axis=1, keepdims=True) for value in (first, second)]
+        return jnp.concatenate(pair + [jnp.zeros((meta.shape[0], 126), jnp.float32)], axis=1)
+
+    block = prompt_kv[0]
+    gathered = [block]
+    rounds = dp // 2
+    share = -(-len(far) // rounds)
+    rows = block.shape[0]
+    crossed = None
+    waiting = []
+    pieces = {(k, which): cut(which, k) for k, which in far}
+    sums = None
+    bit = 1
+    for step in range(rounds):
+        keys = far[step * share : (step + 1) * share]
+        for key in keys:
+            tails[key] = swap(pieces[key], "fsdp", key[0])
+        if sums is not None and bit < dp:
+            sums = sums + swap(sums, "dp", bit)
+            bit *= 2
+        if step == rounds - 1:
+            gathered.append(swap(block[: rows // 2], "dp", 1))
+            if crossed is None:
+                gathered.append(swap(block[rows // 2 :], "dp", 1))
+            else:
+                gathered.append(around(crossed[rows // 2 :], "dp"))
+            waiting = keys
+            break
+        block, crossed = around(block, "dp"), swap(block, "dp", 1)
+        later = far[(step + 1) * share : (step + 2) * share]
+        held = [tails[key] for key in keys] + [pieces[key] for key in later]
+        held += facts if sums is None else [sums]
+        block, crossed, *held = lax.optimization_barrier((block, crossed, *held))
+        tails.update(zip(keys, held))
+        held = held[len(keys) :]
+        pieces.update(zip(later, held))
+        held = held[len(later) :]
+        if sums is None:
+            facts = held
+            sums = group_sums(facts)
+        else:
+            (sums,) = held
+        gathered += [block, crossed]
+    if sums is None:
+        sums = group_sums(facts)
+    while bit < dp:
+        sums = sums + swap(sums, "dp", bit)
+        bit *= 2
+    gains = lax.dynamic_slice_in_dim(
+        jnp.stack([post_gain, final_gain]), here * columns, columns, 1
+    )
 
     attended = [[None] * GROUPS for _ in range(fsdp)]
+    asked = queries[0]
     for g in range(GROUPS):
-        attended[0][g] = attend(queries[0], response_key_value[0], gathered[g], g)
+        attended[0][g] = attend(asked, response_key_value[0], gathered, g)
+        last = [tails[key] for key in waiting] + [sums]
+        asked, attended[0][g], *last = lax.optimization_barrier((asked, attended[0][g], *last))
+        tails.update(zip(waiting, last))
+        sums = last[-1]
+        if g and fsdp > 2:
+            attended[0][g], attended[fsdp // 2][g - 1] = lax.optimization_barrier(
+                (attended[0][g], attended[fsdp // 2][g - 1])
+            )
         bit = fsdp // 2
         known = [0]
-        while bit:
+        while bit > 1:
             for k in known:
                 attended[k ^ bit][g] = swap(attended[k][g], "fsdp", bit)
             known = known + [k ^ bit for k in known]
             bit //= 2
 
-    near = list(range(min(2, fsdp)))
-    far = list(range(2, fsdp))
-    parts = []
-    for some in (near, far):
-        parts.append(
-            project(out_weight, gains, [tails[k] for k in some], [attended[k] for k in some])
-        )
+    facts = jnp.stack(facts)
+
+    def project_some(some):
+        for k in some:
+            if k & 1:
+                attended[k] = [swap(value, "fsdp", 1) for value in attended[k ^ 1]]
+        return project(
+            out_weight,
+            gains,
+            [(tails[k, 0], tails[k, 1]) for k in some],
+            [attended[k] for k in some],
+        )
+
+    near = project_some(list(range(min(2, fsdp))))
+    flat = [attended[k][g] for k in range(2, fsdp, 2) for g in range(GROUPS)]
+    near, *flat = lax.optimization_barrier((near, *flat))
+    for i, k in enumerate(range(2, fsdp, 2)):
+        attended[k] = flat[i * GROUPS : (i + 1) * GROUPS]
+    parts = [near, project_some(list(range(2, fsdp)))]
     totals = jnp.concatenate(parts, axis=0)
     bit = 1
     while bit < fsdp:
@@ -262,9 +317,9 @@
     old = facts[:, responses : 2 * responses]
     ref = facts[:, 2 * responses : 3 * responses]
     meta = facts[:, 3 * responses]
-    group_sum, group_count = meta[:, 0], meta[:, 1]
-    reward = meta[:, 2 : 2 + responses]
-    size = meta[:, 2 + responses : 2 + 2 * responses].astype(jnp.int32)
+    group_sum, group_count = sums[:, 0], sums[:, 1]
+    reward = meta[:, :responses]
+    size = meta[:, responses : 2 * responses].astype(jnp.int32)
     position = lax.broadcasted_iota(jnp.int32, (fsdp, responses, length), 2)
     live = position < size[:, :, None]
     log_ratio = jnp.where(live, logp - old, 0.0)

time: 178 us -> 133 us (0.75)
  waiting for transfers between devices: 99.7 us -> 57.4 us
  local copies, waits for them, and re-layouts: 3.06 us -> 13.8 us
  other arithmetic: 9.79 us -> 3.87 us
  Pallas kernels: 29.1 us -> 25.3 us
  starting transfers between devices: 32.9 us -> 29.7 us
    ppermute x28 -> x27, waiting for transfers between devices: 96.7 us -> 56.8 us  [swap(): return lax.ppermute(value, axis, [(i, i ^ bit) for i in range(count)])]
    unnamed x16 -> x32, local copies, waits for them, and re-layouts: 0.03 us -> 6.56 us
    dynamic_slice x0 -> x2, local copies, waits for them, and re-layouts: none -> 4.3 us  [cut(): lax.dynamic_slice_in_dim(streams[which], (here ^ k) * columns, columns, 1)]
    concatenate x3 -> x2, other arithmetic: 2.88 us -> 0.09 us  [the longest x1 0.08 us: group_sums(): jnp.concatenate(pair + [jnp.zeros((meta.shape[0], 126), jnp.float32)], ax...]
    ppermute x6 -> x4, starting transfers between devices: 10.3 us -> 7.62 us  [around(): lax.ppermute(value, axis, [(i, after[i // 2] * 2 + i % 2) for i in range(...]
    reduce_sum x2 -> x1, other arithmetic: 2.63 us -> 0.15 us  [group_sums(): pair = [jnp.sum(value, axis=1, keepdims=True) for value in (first, second)]]
    ppermute x6 -> x4, waiting for transfers between devices: 2.95 us -> 0.56 us  [around(): lax.ppermute(value, axis, [(i, after[i // 2] * 2 + i % 2) for i in range(...]
    pallas_call x2, Pallas kernels: 12.2 us -> 10.1 us  [project(): pl.pallas_call(functools.partial(project_kernel, sources), out_shape=jax....]
  transfers between devices with their start and end apart: 34 -> 31, of which waited for: 20 -> 16; matrix products, arithmetic and copies ran while one was open for 5% -> 6% of each run, Pallas kernels for 13% -> 15%
where the time goes in v2:
time: 133 us
  waiting for transfers between devices  57.4 us (43%)
  starting transfers between devices  29.7 us (22%)
  Pallas kernels  25.3 us (19%)
  local copies, waits for them, and re-layouts  13.8 us (10%)
  other arithmetic  3.87 us (3%)
  between operations  2.79 us (2%)
    ppermute x27, waiting for transfers between devices, swap(): return lax.ppermute(value, axis, [(i, i ^ bit) for i in range(count)])  56.8 us
    ppermute x27, starting transfers between devices, swap(): return lax.ppermute(value, axis, [(i, i ^ bit) for i in range(count)])  22.1 us
    pallas_call x2, Pallas kernels, attend(): pl.pallas_call(functools.partial(attention_kernel, count), grid=(per_grou...  15.2 us
    pallas_call x2, Pallas kernels, project(): pl.pallas_call(functools.partial(project_kernel, sources), out_shape=jax....  10.1 us
    ppermute x4, starting transfers between devices, around(): lax.ppermute(value, axis, [(i, after[i // 2] * 2 + i % 2) for i in range(...  7.62 us
    unnamed x32, local copies, waits for them, and re-layouts  6.56 us
    dynamic_slice x2, local copies, waits for them, and re-layouts, cut(): lax.dynamic_slice_in_dim(streams[which], (here ^ k) * columns, columns, 1)  4.3 us
  transfers between devices with their start and end apart: 31, of which 16 were waited for; matrix products, arithmetic and copies ran while one was open for 6% of the time, Pallas kernels for 15%

profile of v2, /device:TPU:0, one launch (start us, length us, event | category | flops | bytes accessed | tf_op | source)
XLA Modules:
  0.0 132.8 jit_solution(11947088030900746689)
XLA Ops:
  0.6 4.1 %collective-permute-start = (bf16[128,2048]{1,0:T(8,128)(2,1)}, bf16[128,2048]{1,0:T(8,128)(2,1)S(1)}, u32[]{:S(2)}, u32[]{:S(2)}) collective-permute-start(bf16[128,2048]{1,0:T(8,128)(2,1)} %bitcast.98), channel_id=1, source_target_pairs={{0,16},{4,20},{8,0},{12,4},{16,24},{20,28},{24,8},{28,12},{1,17},{... | collective-permute-start | bytes 1572872 | tf_op jit(solution)/shard_map/ppermute | solution.py:29
  4.7 1.5 %collective-permute-start.1 = (bf16[128,2048]{1,0:T(8,128)(2,1)}, bf16[128,2048]{1,0:T(8,128)(2,1)S(1)}, u32[]{:S(2)}, u32[]{:S(2)}) collective-permute-start(bf16[128,2048]{1,0:T(8,128)(2,1)} %bitcast.99), channel_id=1, source_target_pairs={{0,4},{4,0},{8,12},{12,8},{16,20},{20,16},{24,28},{28,24},{1,5},{5... | collective-permute-start | bytes 1572872 | tf_op jit(solution)/shard_map/ppermute | solution.py:22
  6.2 3.0 %constant_dynamic-slice_fusion.1 = (bf16[256,1152]{1,0:T(8,128)(2,1)}, bf16[256,1152]{1,0:T(8,128)(2,1)}, bf16[256,1152]{1,0:T(8,128)(2,1)S(1)}, bf16[256,1152]{1,0:T(8,128)(2,1)S(1)}) fusion(bf16[256,4608]{1,0:T(8,128)(2,1)} %bitcast.106, s32[]{:T(128)S(6)} %select_n.39, s32[]{:T(128)S(6)} %select_n.36, s32[]{:T(128)S(6)} %select_n.35, s32[]{:T(128)S(6)} %select_n.34), kind=kLoop, calls=%fused_computation.50 | loop fusion | bytes 4718608 | tf_op jit(solution)/shard_map/dynamic_slice | solution.py:192
  9.2 1.5 %collective-permute-start.2 = (bf16[256,1152]{1,0:T(8,128)(2,1)S(1)}, bf16[256,1152]{1,0:T(8,128)(2,1)S(1)}, u32[]{:S(2)}, u32[]{:S(2)}) collective-permute-start(bf16[256,1152]{1,0:T(8,128)(2,1)S(1)} %get-tuple-element.79), channel_id=1, source_target_pairs={{0,2},{1,3},{2,0},{3,1},{4,6},{5,7},{6,4},{7,5},{8,10},{9,11},{10,... | collective-permute-start | bytes 1769480 | tf_op jit(solution)/shard_map/ppermute | solution.py:22
  13.0 1.3 %constant_dynamic-slice_fusion = (bf16[256,1152]{1,0:T(8,128)(2,1)}, bf16[256,1152]{1,0:T(8,128)(2,1)}, bf16[256,1152]{1,0:T(8,128)(2,1)S(1)}, bf16[256,1152]{1,0:T(8,128)(2,1)}) fusion(bf16[256,4608]{1,0:T(8,128)(2,1)S(1)} %bitcast.107, s32[]{:T(128)S(6)} %select_n.39, s32[]{:T(128)S(6)} %select_n.36, s32[]{:T(128)S(6)} %select_n.35, s32[]{:T(128)S(6)} %select_n.34), kind=kLoop, calls=%fused_computation.49 | loop fusion | bytes 4718608 | tf_op jit(solution)/shard_map/dynamic_slice | solution.py:192
  14.3 9.5 %collective-permute-done.4 = f32[7,128]{1,0:T(8,128)S(1)} collective-permute-done((f32[7,128]{1,0:T(8,128)S(1)}, f32[7,128]{1,0:T(8,128)S(1)}, u32[]{:S(2)}, u32[]{:S(2)}) %collective-permute-start.4) | collective-permute-done | bytes 3616 | tf_op jit(solution)/shard_map/ppermute | solution.py:22
  24.7 1.5 %collective-permute-start.8 = (bf16[256,1152]{1,0:T(8,128)(2,1)}, bf16[256,1152]{1,0:T(8,128)(2,1)S(1)}, u32[]{:S(2)}, u32[]{:S(2)}) collective-permute-start(bf16[256,1152]{1,0:T(8,128)(2,1)} %get-tuple-element.40), channel_id=1, source_target_pairs={{0,2},{1,3},{2,0},{3,1},{4,6},{5,7},{6,4},{7,5},{8,10},{9,11},{10,... | collective-permute-start | bytes 1769480 | tf_op jit(solution)/shard_map/ppermute | solution.py:22
  26.3 1.6 %collective-permute-start.6 = (bf16[128,2048]{1,0:T(8,128)(2,1)S(1)}, bf16[128,2048]{1,0:T(8,128)(2,1)S(1)}, u32[]{:S(2)}, u32[]{:S(2)}) collective-permute-start(bf16[128,2048]{1,0:T(8,128)(2,1)S(1)} %collective-permute-done.refs_1_.refs_10_), channel_id=1, source_target_pairs={{0,16},{4,20},{8,0},{12,4},{16,24},{20,28},{24,8},{28,12},{1,17},{... | collective-permute-start | bytes 1572872 | tf_op jit(solution)/shard_map/ppermute | solution.py:29
  28.9 1.5 %collective-permute-start.9 = (f32[4,128]{1,0:T(4,128)S(1)}, f32[4,128]{1,0:T(4,128)S(1)}, u32[]{:S(2)}, u32[]{:S(2)}) collective-permute-start(f32[4,128]{1,0:T(4,128)S(1)} %maximum_maximum_fusion), channel_id=1, source_target_pairs={{0,4},{4,0},{8,12},{12,8},{16,20},{20,16},{24,28},{28,24},{1,5},{5... | collective-permute-start | bytes 6152 | tf_op jit(solution)/shard_map/ppermute | solution.py:22
  30.4 9.3 %collective-permute-done.9 = f32[4,128]{1,0:T(4,128)S(1)} collective-permute-done((f32[4,128]{1,0:T(4,128)S(1)}, f32[4,128]{1,0:T(4,128)S(1)}, u32[]{:S(2)}, u32[]{:S(2)}) %collective-permute-start.9) | collective-permute-done | bytes 2080 | tf_op jit(solution)/shard_map/ppermute | solution.py:22
  41.4 1.1 collective-permute-start.13
  42.5 11.9 %collective-permute-done.13 = f32[4,128]{1,0:T(4,128)S(1)} collective-permute-done((f32[4,128]{1,0:T(4,128)S(1)}, f32[4,128]{1,0:T(4,128)S(1)}, u32[]{:S(2)}, u32[]{:S(2)}) %collective-permute-start.13) | collective-permute-done | bytes 2080 | tf_op jit(solution)/shard_map/ppermute | solution.py:22
  57.7 1.2 collective-permute-start.17
  59.0 4.7 %collective-permute-done.17 = f32[4,128]{1,0:T(4,128)S(1)} collective-permute-done((f32[4,128]{1,0:T(4,128)S(1)}, f32[4,128]{1,0:T(4,128)S(1)}, u32[]{:S(2)}, u32[]{:S(2)}) %collective-permute-start.17) | collective-permute-done | bytes 2080 | tf_op jit(solution)/shard_map/ppermute | solution.py:22
  63.7 1.3 collective-permute-done.14.refs_7_.refs_16_
  65.5 7.6 %shard_map.156.refs_2_ = bf16[256,1024]{1,0:T(8,128)(2,1)} custom-call(bf16[2,128,2048]{2,1,0:T(8,128)(2,1)} %bitcast.104, bf16[2,128,2048]{2,1,0:T(8,128)(2,1)} %bitcast.94, bf16[2,128,2048]{2,1,0:T(8,128)(2,1)} %bitcast.95, bf16[128,2048]{1,0:T(8,128)(2,1)} %bitcast.100, bf16[128,2048]{1,0:T(8,128)(2,1)} %copy-done.6, bf16[128,2048]{1,0:T(8,128)(2,1)} %copy-done.7, ...), custom_call_target="tpu_custom_call" | custom-call | flops 1207959552 | bytes 4194304 | tf_op jit(solution)/shard_map/pallas_call | solution.py:98
  74.7 7.6 %shard_map.157.refs_3_ = bf16[256,1024]{1,0:T(8,128)(2,1)} custom-call(bf16[2,128,2048]{2,1,0:T(8,128)(2,1)} %bitcast.105, bf16[2,128,2048]{2,1,0:T(8,128)(2,1)} %bitcast.96, bf16[2,128,2048]{2,1,0:T(8,128)(2,1)} %bitcast.97, bf16[128,2048]{1,0:T(8,128)(2,1)} %bitcast.102, bf16[128,2048]{1,0:T(8,128)(2,1)} %copy-done.6, bf16[128,2048]{1,0:T(8,128)(2,1)} %copy-done.7, ...), custom_call_target="tpu_custom_call" | custom-call | flops 1207959552 | bytes 4194304 | tf_op jit(solution)/shard_map/pallas_call | solution.py:98
  82.3 4.4 %collective-permute-done.18.refs_2_ = bf16[256,1024]{1,0:T(8,128)(2,1)} collective-permute-done((bf16[256,1024]{1,0:T(8,128)(2,1)}, bf16[256,1024]{1,0:T(8,128)(2,1)}, u32[]{:S(2)}, u32[]{:S(2)}) %collective-permute-start.18) | collective-permute-done | bytes 524320 | tf_op jit(solution)/shard_map/ppermute | solution.py:22
  86.7 1.2 collective-permute-start.23
  88.9 2.3 %copy-done = bf16[2048,1152]{1,0:T(8,128)(2,1)S(1)} copy-done((bf16[2048,1152]{1,0:T(8,128)(2,1)S(1)}, bf16[2048,1152]{1,0:T(8,128)(2,1)}, u32[]{:S(2)}) %copy-start) | copy-done | bytes 4718616
  92.3 5.2 %shard_map.158 = f32[2,8,256]{2,1,0:T(8,128)S(1)} custom-call(bf16[2048,1152]{1,0:T(8,128)(2,1)S(1)} %copy-done, f32[2,1152]{1,0:T(2,128)S(1)} %fusion.gain_ref, bf16[256,1152]{1,0:T(8,128)(2,1)S(1)} %get-tuple-element.78.refs_0_, bf16[256,1152]{1,0:T(8,128)(2,1)S(1)} %get-tuple-element.74.refs_1_, bf16[256,1024]{1,0:T(8,128)(2,1)S(1)} %copy-done.2, ...), custom_call_target="tpu_custom_call" | custom-call | flops 2415919104 | bytes 8388608 | tf_op jit(solution)/shard_map/pallas_call | solution.py:155
  97.5 3.8 %collective-permute-done.23.refs_3_ = bf16[256,1024]{1,0:T(8,128)(2,1)S(1)} collective-permute-done((bf16[256,1024]{1,0:T(8,128)(2,1)}, bf16[256,1024]{1,0:T(8,128)(2,1)S(1)}, u32[]{:S(2)}, u32[]{:S(2)}) %collective-permute-start.23) | collective-permute-done | bytes 524320 | tf_op jit(solution)/shard_map/ppermute | solution.py:22
  101.8 2.3 %collective-permute-done.24.refs_6_ = bf16[256,1024]{1,0:T(8,128)(2,1)S(1)} collective-permute-done((bf16[256,1024]{1,0:T(8,128)(2,1)}, bf16[256,1024]{1,0:T(8,128)(2,1)S(1)}, u32[]{:S(2)}, u32[]{:S(2)}) %collective-permute-start.24) | collective-permute-done | bytes 524320 | tf_op jit(solution)/shard_map/ppermute | solution.py:22
  104.1 2.3 %copy-done.1 = bf16[2048,1152]{1,0:T(8,128)(2,1)S(1)} copy-done((bf16[2048,1152]{1,0:T(8,128)(2,1)S(1)}, bf16[2048,1152]{1,0:T(8,128)(2,1)}, u32[]{:S(2)}) %copy-start.1) | copy-done | bytes 4718616
  106.4 4.8 %shard_map.159 = f32[2,8,256]{2,1,0:T(8,128)S(1)} custom-call(bf16[2048,1152]{1,0:T(8,128)(2,1)S(1)} %copy-done.1, f32[2,1152]{1,0:T(2,128)S(1)} %fusion.gain_ref, bf16[256,1152]{1,0:T(8,128)(2,1)S(1)} %collective-permute-done.2.refs_0_, bf16[256,1152]{1,0:T(8,128)(2,1)S(1)} %collective-permute-done.8.refs_1_, ...), custom_call_target="tpu_custom_call" | custom-call | flops 2415919104 | bytes 8388608 | tf_op jit(solution)/shard_map/pallas_call | solution.py:155
  112.6 1.3 collective-permute-start.27
  114.0 2.5 %collective-permute-done.27 = f32[4,8,256]{2,1,0:T(8,128)S(1)} collective-permute-done((f32[4,8,256]{2,1,0:T(8,128)S(1)}, f32[4,8,256]{2,1,0:T(8,128)S(1)}, u32[]{:S(2)}, u32[]{:S(2)}) %collective-permute-start.27) | collective-permute-done | bytes 32800 | tf_op jit(solution)/shard_map/ppermute | solution.py:22
  117.9 1.6 %collective-permute-start.28 = (f32[1,128]{1,0:T(1,128)S(1)}, f32[1,128]{1,0:T(1,128)S(1)}, u32[]{:S(2)}, u32[]{:S(2)}) collective-permute-start(f32[1,128]{1,0:T(1,128)S(1)} %broadcast_in_dim.32), channel_id=1, source_target_pairs={{0,4},{4,0},{8,12},{12,8},{16,20},{20,16},{24,28},{28,24},{1,5},{5... | collective-permute-start | bytes 1544 | tf_op jit(solution)/shard_map/ppermute | solution.py:22
  119.5 2.0 %collective-permute-done.28 = f32[1,128]{1,0:T(1,128)S(1)} collective-permute-done((f32[1,128]{1,0:T(1,128)S(1)}, f32[1,128]{1,0:T(1,128)S(1)}, u32[]{:S(2)}, u32[]{:S(2)}) %collective-permute-start.28) | collective-permute-done | bytes 544 | tf_op jit(solution)/shard_map/ppermute | solution.py:22
  122.2 1.4 %collective-permute-start.29 = (f32[1,128]{1,0:T(1,128)S(1)}, f32[1,128]{1,0:T(1,128)S(1)}, u32[]{:S(2)}, u32[]{:S(2)}) collective-permute-start(f32[1,128]{1,0:T(1,128)S(1)} %broadcast_add_fusion), channel_id=1, source_target_pairs={{0,8},{4,12},{8,0},{12,4},{16,24},{20,28},{24,16},{28,20},{1,9},{5... | collective-permute-start | bytes 1544 | tf_op jit(solution)/shard_map/ppermute | solution.py:22
  123.7 2.1 %collective-permute-done.29 = f32[1,128]{1,0:T(1,128)S(1)} collective-permute-done((f32[1,128]{1,0:T(1,128)S(1)}, f32[1,128]{1,0:T(1,128)S(1)}, u32[]{:S(2)}, u32[]{:S(2)}) %collective-permute-start.29) | collective-permute-done | bytes 544 | tf_op jit(solution)/shard_map/ppermute | solution.py:22
  126.4 1.8 %collective-permute-start.30 = (f32[1,128]{1,0:T(1,128)S(1)}, f32[1,128]{1,0:T(1,128)S(1)}, u32[]{:S(2)}, u32[]{:S(2)}) collective-permute-start(f32[1,128]{1,0:T(1,128)S(1)} %fusion.20), channel_id=1, source_target_pairs={{0,16},{4,20},{8,24},{12,28},{16,0},{20,4},{24,8},{28,12},{1,17},{... | collective-permute-start | bytes 1544 | tf_op jit(solution)/shard_map/ppermute | solution.py:22
  (114 shorter events, 20.6 us)
Async XLA Ops:
  0.6 23.3 %collective-permute-start = (bf16[128,2048]{1,0:T(8,128)(2,1)}, bf16[128,2048]{1,0:T(8,128)(2,1)S(1)}, u32[]{:S(2)}, u32[]{:S(2)}) collective-permute-start(bf16[128,2048]{1,0:T(8,128)(2,1)} %bitcast.98), channel_id=1, source_target_pairs={{0,16},{4,20},{8,0},{12,4},{16,24},{20,28},{24,8},{28,12},{1,17},{... | collective-permute-start | bytes 1572872 | tf_op jit(solution)/shard_map/ppermute | solution.py:29
  4.7 19.2 %collective-permute-start.1 = (bf16[128,2048]{1,0:T(8,128)(2,1)}, bf16[128,2048]{1,0:T(8,128)(2,1)S(1)}, u32[]{:S(2)}, u32[]{:S(2)}) collective-permute-start(bf16[128,2048]{1,0:T(8,128)(2,1)} %bitcast.99), channel_id=1, source_target_pairs={{0,4},{4,0},{8,12},{12,8},{16,20},{20,16},{24,28},{28,24},{1,5},{5... | collective-permute-start | bytes 1572872 | tf_op jit(solution)/shard_map/ppermute | solution.py:22
  9.2 14.7 %collective-permute-start.2 = (bf16[256,1152]{1,0:T(8,128)(2,1)S(1)}, bf16[256,1152]{1,0:T(8,128)(2,1)S(1)}, u32[]{:S(2)}, u32[]{:S(2)}) collective-permute-start(bf16[256,1152]{1,0:T(8,128)(2,1)S(1)} %get-tuple-element.79), channel_id=1, source_target_pairs={{0,2},{1,3},{2,0},{3,1},{4,6},{5,7},{6,4},{7,5},{8,10},{9,11},{10,... | collective-permute-start | bytes 1769480 | tf_op jit(solution)/shard_map/ppermute | solution.py:22
  10.8 1.2 collective-permute-start.3
  10.9 12.9 %collective-permute-start.4 = (f32[7,128]{1,0:T(8,128)S(1)}, f32[7,128]{1,0:T(8,128)S(1)}, u32[]{:S(2)}, u32[]{:S(2)}) collective-permute-start(f32[7,128]{1,0:T(8,128)S(1)} %select_maximum_fusion), channel_id=1, source_target_pairs={{0,2},{1,3},{2,0},{3,1},{4,6},{5,7},{6,4},{7,5},{8,10},{9,11},{10,... | collective-permute-start | bytes 10760 | tf_op jit(solution)/shard_map/ppermute | solution.py:22
  12.1 11.8 %collective-permute-start.5 = (f32[7,128]{1,0:T(8,128)S(1)}, f32[7,128]{1,0:T(8,128)S(1)}, u32[]{:S(2)}, u32[]{:S(2)}) collective-permute-start(f32[7,128]{1,0:T(8,128)S(1)} %collective-permute-done.3), channel_id=1, source_target_pairs={{0,2},{1,3},{2,0},{3,1},{4,6},{5,7},{6,4},{7,5},{8,10},{9,11},{10,... | collective-permute-start | bytes 10760 | tf_op jit(solution)/shard_map/ppermute | solution.py:22
  23.9 15.9 %copy-start.6 = (bf16[128,2048]{1,0:T(8,128)(2,1)}, bf16[128,2048]{1,0:T(8,128)(2,1)S(1)}, u32[]{:S(2)}) copy-start(bf16[128,2048]{1,0:T(8,128)(2,1)S(1)} %collective-permute-done.refs_1_.refs_10_) | copy-start | bytes 1572868
  24.7 15.0 %collective-permute-start.8 = (bf16[256,1152]{1,0:T(8,128)(2,1)}, bf16[256,1152]{1,0:T(8,128)(2,1)S(1)}, u32[]{:S(2)}, u32[]{:S(2)}) collective-permute-start(bf16[256,1152]{1,0:T(8,128)(2,1)} %get-tuple-element.40), channel_id=1, source_target_pairs={{0,2},{1,3},{2,0},{3,1},{4,6},{5,7},{6,4},{7,5},{8,10},{9,11},{10,... | collective-permute-start | bytes 1769480 | tf_op jit(solution)/shard_map/ppermute | solution.py:22
  26.3 13.4 %collective-permute-start.6 = (bf16[128,2048]{1,0:T(8,128)(2,1)S(1)}, bf16[128,2048]{1,0:T(8,128)(2,1)S(1)}, u32[]{:S(2)}, u32[]{:S(2)}) collective-permute-start(bf16[128,2048]{1,0:T(8,128)(2,1)S(1)} %collective-permute-done.refs_1_.refs_10_), channel_id=1, source_target_pairs={{0,16},{4,20},{8,0},{12,4},{16,24},{20,28},{24,8},{28,12},{1,17},{... | collective-permute-start | bytes 1572872 | tf_op jit(solution)/shard_map/ppermute | solution.py:29
  27.9 11.8 %collective-permute-start.7 = (bf16[128,2048]{1,0:T(8,128)(2,1)S(1)}, bf16[128,2048]{1,0:T(8,128)(2,1)}, u32[]{:S(2)}, u32[]{:S(2)}) collective-permute-start(bf16[128,2048]{1,0:T(8,128)(2,1)S(1)} %collective-permute-done.refs_1_.refs_10_), channel_id=1, source_target_pairs={{0,4},{4,0},{8,12},{12,8},{16,20},{20,16},{24,28},{28,24},{1,5},{5... | collective-permute-start | bytes 1572872 | tf_op jit(solution)/shard_map/ppermute | solution.py:22
  28.9 10.8 %collective-permute-start.9 = (f32[4,128]{1,0:T(4,128)S(1)}, f32[4,128]{1,0:T(4,128)S(1)}, u32[]{:S(2)}, u32[]{:S(2)}) collective-permute-start(f32[4,128]{1,0:T(4,128)S(1)} %maximum_maximum_fusion), channel_id=1, source_target_pairs={{0,4},{4,0},{8,12},{12,8},{16,20},{20,16},{24,28},{28,24},{1,5},{5... | collective-permute-start | bytes 6152 | tf_op jit(solution)/shard_map/ppermute | solution.py:22
  39.8 15.5 %collective-permute-start.12 = (bf16[256,1152]{1,0:T(8,128)(2,1)}, bf16[256,1152]{1,0:T(8,128)(2,1)S(1)}, u32[]{:S(2)}, u32[]{:S(2)}) collective-permute-start(bf16[256,1152]{1,0:T(8,128)(2,1)} %get-tuple-element.43), channel_id=1, source_target_pairs={{0,3},{1,2},{2,1},{3,0},{4,7},{5,6},{6,5},{7,4},{8,11},{9,10},{10,... | collective-permute-start | bytes 1769480 | tf_op jit(solution)/shard_map/ppermute | solution.py:22
  39.8 14.5 %collective-permute-start.10 = (bf16[128,2048]{1,0:T(8,128)(2,1)S(1)}, bf16[128,2048]{1,0:T(8,128)(2,1)S(1)}, u32[]{:S(2)}, u32[]{:S(2)}) collective-permute-start(bf16[128,2048]{1,0:T(8,128)(2,1)S(1)} %collective-permute-done.6.refs_3_.refs_12_), channel_id=1, source_target_pairs={{0,16},{4,20},{8,0},{12,4},{16,24},{20,28},{24,8},{28,12},{1,17},{... | collective-permute-start | bytes 1572872 | tf_op jit(solution)/shard_map/ppermute | solution.py:29
  40.9 14.4 %collective-permute-start.11 = (bf16[128,2048]{1,0:T(8,128)(2,1)S(1)}, bf16[128,2048]{1,0:T(8,128)(2,1)S(1)}, u32[]{:S(2)}, u32[]{:S(2)}) collective-permute-start(bf16[128,2048]{1,0:T(8,128)(2,1)S(1)} %collective-permute-done.6.refs_3_.refs_12_), channel_id=1, source_target_pairs={{0,4},{4,0},{8,12},{12,8},{16,20},{20,16},{24,28},{28,24},{1,5},{5... | collective-permute-start | bytes 1572872 | tf_op jit(solution)/shard_map/ppermute | solution.py:22
  41.4 12.9 %collective-permute-start.13 = (f32[4,128]{1,0:T(4,128)S(1)}, f32[4,128]{1,0:T(4,128)S(1)}, u32[]{:S(2)}, u32[]{:S(2)}) collective-permute-start(f32[4,128]{1,0:T(4,128)S(1)} %fusion.21), channel_id=1, source_target_pairs={{0,8},{4,12},{8,0},{12,4},{16,24},{20,28},{24,16},{28,20},{1,9},{5... | collective-permute-start | bytes 6152 | tf_op jit(solution)/shard_map/ppermute | solution.py:22
  55.3 17.9 %collective-permute-start.16 = (bf16[256,1152]{1,0:T(8,128)(2,1)}, bf16[256,1152]{1,0:T(8,128)(2,1)S(1)}, u32[]{:S(2)}, u32[]{:S(2)}) collective-permute-start(bf16[256,1152]{1,0:T(8,128)(2,1)} %get-tuple-element.47), channel_id=1, source_target_pairs={{0,3},{1,2},{2,1},{3,0},{4,7},{5,6},{6,5},{7,4},{8,11},{9,10},{10,... | collective-permute-start | bytes 1769480 | tf_op jit(solution)/shard_map/ppermute | solution.py:22
  56.2 8.8 %collective-permute-start.14 = (bf16[64,2048]{1,0:T(8,128)(2,1)S(1)}, bf16[64,2048]{1,0:T(8,128)(2,1)}, u32[]{:S(2)}, u32[]{:S(2)}) collective-permute-start(bf16[64,2048]{1,0:T(8,128)(2,1)S(1)} %slice.100), channel_id=1, source_target_pairs={{0,4},{4,0},{8,12},{12,8},{16,20},{20,16},{24,28},{28,24},{1,5},{5... | collective-permute-start | bytes 786440 | tf_op jit(solution)/shard_map/ppermute | solution.py:22
  56.8 8.7 %collective-permute-start.15 = (bf16[64,2048]{1,0:T(8,128)(2,1)S(1)}, bf16[64,2048]{1,0:T(8,128)(2,1)}, u32[]{:S(2)}, u32[]{:S(2)}) collective-permute-start(bf16[64,2048]{1,0:T(8,128)(2,1)S(1)} %slice.101), channel_id=1, source_target_pairs={{0,16},{4,20},{8,0},{12,4},{16,24},{20,28},{24,8},{28,12},{1,17},{... | collective-permute-start | bytes 786440 | tf_op jit(solution)/shard_map/ppermute | solution.py:29
  57.7 6.0 %collective-permute-start.17 = (f32[4,128]{1,0:T(4,128)S(1)}, f32[4,128]{1,0:T(4,128)S(1)}, u32[]{:S(2)}, u32[]{:S(2)}) collective-permute-start(f32[4,128]{1,0:T(4,128)S(1)} %add.68), channel_id=1, source_target_pairs={{0,16},{4,20},{8,24},{12,28},{16,0},{20,4},{24,8},{28,12},{1,17},{... | collective-permute-start | bytes 6152 | tf_op jit(solution)/shard_map/ppermute | solution.py:22
  73.2 13.5 %collective-permute-start.18 = (bf16[256,1024]{1,0:T(8,128)(2,1)}, bf16[256,1024]{1,0:T(8,128)(2,1)}, u32[]{:S(2)}, u32[]{:S(2)}) collective-permute-start(bf16[256,1024]{1,0:T(8,128)(2,1)} %shard_map.156.refs_2_), channel_id=1, source_target_pairs={{0,2},{1,3},{2,0},{3,1},{4,6},{5,7},{6,4},{7,5},{8,10},{9,11},{10,... | collective-permute-start | bytes 1572872 | tf_op jit(solution)/shard_map/ppermute | solution.py:22
  74.2 14.6 %collective-permute-start.19 = (bf16[256,1152]{1,0:T(8,128)(2,1)}, bf16[256,1152]{1,0:T(8,128)(2,1)}, u32[]{:S(2)}, u32[]{:S(2)}) collective-permute-start(bf16[256,1152]{1,0:T(8,128)(2,1)} %get-tuple-element.76), channel_id=1, source_target_pairs={{0,1},{1,0},{2,3},{3,2},{4,5},{5,4},{6,7},{7,6},{8,9},{9,8},{10,11... | collective-permute-start | bytes 1769480 | tf_op jit(solution)/shard_map/ppermute | solution.py:22
  74.2 14.6 %collective-permute-start.20 = (bf16[256,1152]{1,0:T(8,128)(2,1)}, bf16[256,1152]{1,0:T(8,128)(2,1)}, u32[]{:S(2)}, u32[]{:S(2)}) collective-permute-start(bf16[256,1152]{1,0:T(8,128)(2,1)} %get-tuple-element.72), channel_id=1, source_target_pairs={{0,1},{1,0},{2,3},{3,2},{4,5},{5,4},{6,7},{7,6},{8,9},{9,8},{10,11... | collective-permute-start | bytes 1769480 | tf_op jit(solution)/shard_map/ppermute | solution.py:22
  74.7 14.1 %collective-permute-start.21 = (bf16[256,1024]{1,0:T(8,128)(2,1)}, bf16[256,1024]{1,0:T(8,128)(2,1)}, u32[]{:S(2)}, u32[]{:S(2)}) collective-permute-start(bf16[256,1024]{1,0:T(8,128)(2,1)} %shard_map.156.refs_2_), channel_id=1, source_target_pairs={{0,1},{1,0},{2,3},{3,2},{4,5},{5,4},{6,7},{7,6},{8,9},{9,8},{10,11... | collective-permute-start | bytes 1572872 | tf_op jit(solution)/shard_map/ppermute | solution.py:22
  86.7 2.1 %collective-permute-start.22 = (bf16[256,1024]{1,0:T(8,128)(2,1)}, bf16[256,1024]{1,0:T(8,128)(2,1)S(1)}, u32[]{:S(2)}, u32[]{:S(2)}) collective-permute-start(bf16[256,1024]{1,0:T(8,128)(2,1)} %shard_map.157.refs_3_), channel_id=1, source_target_pairs={{0,1},{1,0},{2,3},{3,2},{4,5},{5,4},{6,7},{7,6},{8,9},{9,8},{10,11... | collective-permute-start | bytes 1572872 | tf_op jit(solution)/shard_map/ppermute | solution.py:22
  86.7 14.5 %collective-permute-start.23 = (bf16[256,1024]{1,0:T(8,128)(2,1)}, bf16[256,1024]{1,0:T(8,128)(2,1)S(1)}, u32[]{:S(2)}, u32[]{:S(2)}) collective-permute-start(bf16[256,1024]{1,0:T(8,128)(2,1)} %shard_map.157.refs_3_), channel_id=1, source_target_pairs={{0,2},{1,3},{2,0},{3,1},{4,6},{5,7},{6,4},{7,5},{8,10},{9,11},{10,... | collective-permute-start | bytes 1572872 | tf_op jit(solution)/shard_map/ppermute | solution.py:22
  101.3 2.8 %collective-permute-start.24 = (bf16[256,1024]{1,0:T(8,128)(2,1)}, bf16[256,1024]{1,0:T(8,128)(2,1)S(1)}, u32[]{:S(2)}, u32[]{:S(2)}) collective-permute-start(bf16[256,1024]{1,0:T(8,128)(2,1)} %collective-permute-done.18.refs_2_), channel_id=1, source_target_pairs={{0,1},{1,0},{2,3},{3,2},{4,5},{5,4},{6,7},{7,6},{8,9},{9,8},{10,11... | collective-permute-start | bytes 1572872 | tf_op jit(solution)/shard_map/ppermute | solution.py:22
  101.3 2.8 %collective-permute-start.25 = (bf16[256,1024]{1,0:T(8,128)(2,1)S(1)}, bf16[256,1024]{1,0:T(8,128)(2,1)S(1)}, u32[]{:S(2)}, u32[]{:S(2)}) collective-permute-start(bf16[256,1024]{1,0:T(8,128)(2,1)S(1)} %collective-permute-done.23.refs_3_), channel_id=1, source_target_pairs={{0,1},{1,0},{2,3},{3,2},{4,5},{5,4},{6,7},{7,6},{8,9},{9,8},{10,11... | collective-permute-start | bytes 1572872 | tf_op jit(solution)/shard_map/ppermute | solution.py:22
  111.3 1.3 collective-permute-start.26
  112.6 4.0 %collective-permute-start.27 = (f32[4,8,256]{2,1,0:T(8,128)S(1)}, f32[4,8,256]{2,1,0:T(8,128)S(1)}, u32[]{:S(2)}, u32[]{:S(2)}) collective-permute-start(f32[4,8,256]{2,1,0:T(8,128)S(1)} %maximum_add_fusion), channel_id=1, source_target_pairs={{0,2},{1,3},{2,0},{3,1},{4,6},{5,7},{6,4},{7,5},{8,10},{9,11},{10,... | collective-permute-start | bytes 98312 | tf_op jit(solution)/shard_map/ppermute | solution.py:22
  117.9 3.6 %collective-permute-start.28 = (f32[1,128]{1,0:T(1,128)S(1)}, f32[1,128]{1,0:T(1,128)S(1)}, u32[]{:S(2)}, u32[]{:S(2)}) collective-permute-start(f32[1,128]{1,0:T(1,128)S(1)} %broadcast_in_dim.32), channel_id=1, source_target_pairs={{0,4},{4,0},{8,12},{12,8},{16,20},{20,16},{24,28},{28,24},{1,5},{5... | collective-permute-start | bytes 1544 | tf_op jit(solution)/shard_map/ppermute | solution.py:22
  122.2 3.6 %collective-permute-start.29 = (f32[1,128]{1,0:T(1,128)S(1)}, f32[1,128]{1,0:T(1,128)S(1)}, u32[]{:S(2)}, u32[]{:S(2)}) collective-permute-start(f32[1,128]{1,0:T(1,128)S(1)} %broadcast_add_fusion), channel_id=1, source_target_pairs={{0,8},{4,12},{8,0},{12,4},{16,24},{20,28},{24,16},{28,20},{1,9},{5... | collective-permute-start | bytes 1544 | tf_op jit(solution)/shard_map/ppermute | solution.py:22
  126.4 4.5 %collective-permute-start.30 = (f32[1,128]{1,0:T(1,128)S(1)}, f32[1,128]{1,0:T(1,128)S(1)}, u32[]{:S(2)}, u32[]{:S(2)}) collective-permute-start(f32[1,128]{1,0:T(1,128)S(1)} %fusion.20), channel_id=1, source_target_pairs={{0,16},{4,20},{8,24},{12,28},{16,0},{20,4},{24,8},{28,12},{1,17},{... | collective-permute-start | bytes 1544 | tf_op jit(solution)/shard_map/ppermute | solution.py:22
  (15 other events, 92.8 us)

commit v3 on v2

v3 whole, which is shorter than its diff:
```python
import functools
import math

import jax
import jax.numpy as jnp
from jax import lax
from jax.experimental import pallas as pl
from jax.experimental.pallas import tpu as pltpu
from jax.sharding import PartitionSpec as P

D = 4608
KEY_VALUE_HEADS = 8
PER_KEY_VALUE = 2
HEAD_SIZE = 128
QPRE = 144
GROUPS = 2
CHUNK = 512
SUMS = 8


def swap(value, axis, bit):
    count = lax.axis_size(axis)
    return lax.ppermute(value, axis, [(i, i ^ bit) for i in range(count)])


def around(value, axis):
    half = lax.axis_size(axis) // 2
    order = list(range(0, half, 2)) + list(range(1, half, 2))[::-1]
    after = {order[i]: order[(i + 1) % half] for i in range(half)}
    return lax.ppermute(
        value, axis, [(i, after[i // 2] * 2 + i % 2) for i in range(2 * half)]
    )


def weigh(q_rows, k_rows):
    scores = lax.dot_general(
        q_rows, k_rows, (((1,), (1,)), ((), ())), preferred_element_type=jnp.float32
    )
    return jnp.exp2(50.0 * math.log2(math.e) * jnp.tanh(scores * (QPRE**-0.5 / 50.0)))


def stacked(q_ref):
    responses, length, _ = q_ref.shape
    q = q_ref[...].reshape(responses * length, PER_KEY_VALUE * HEAD_SIZE)
    return jnp.concatenate(
        [q[:, h * HEAD_SIZE : (h + 1) * HEAD_SIZE] for h in range(PER_KEY_VALUE)], axis=0
    )


def gather_in(stack, key_refs, value_refs, numerator, total):
    keys = jnp.concatenate([ref[...] for ref in key_refs], axis=0)
    values = jnp.concatenate([ref[...] for ref in value_refs], axis=0)
    count = keys.shape[0]
    for start in range(0, count, CHUNK):
        stop = min(start + CHUNK, count)
        weights = weigh(stack, keys[start:stop])
        for lane in range(0, stop - start, HEAD_SIZE):
            piece = weights[:, lane : lane + HEAD_SIZE]
            if piece.shape[1] < HEAD_SIZE:
                piece = jnp.pad(piece, ((0, 0), (0, HEAD_SIZE - piece.shape[1])))
            total = total + piece
        numerator = numerator + jnp.dot(
            weights.astype(jnp.bfloat16), values[start:stop], preferred_element_type=jnp.float32
        )
    return numerator, total


def begin(q_ref, rk_ref, rv_ref, key_refs, value_refs):
    responses, length, _ = q_ref.shape
    later = lax.broadcasted_iota(jnp.int32, (length, length), 0)
    earlier = lax.broadcasted_iota(jnp.int32, (length, length), 1)
    causal = earlier <= later
    stack = stacked(q_ref)
    owned, numerators = [], []
    for i in range(PER_KEY_VALUE * responses):
        r = i % responses
        own = jnp.where(causal, weigh(stack[i * length : (i + 1) * length], rk_ref[r]), 0.0)
        owned.append(own)
        numerators.append(
            jnp.dot(own.astype(jnp.bfloat16), rv_ref[r], preferred_element_type=jnp.float32)
        )
    return gather_in(
        stack,
        key_refs,
        value_refs,
        jnp.concatenate(numerators, axis=0),
        jnp.concatenate(owned, axis=0),
    )


def finish(tokens, numerator, total, out_ref):
    result = (numerator / jnp.sum(total, axis=-1, keepdims=True)).astype(jnp.bfloat16)
    for h in range(PER_KEY_VALUE):
        out_ref[:, h * HEAD_SIZE : (h + 1) * HEAD_SIZE] = result[h * tokens : (h + 1) * tokens]


def first_kernel(count, q_ref, rk_ref, rv_ref, *refs):
    numerator, total = begin(q_ref, rk_ref, rv_ref, refs[:count], refs[count : 2 * count])
    refs[-2][...] = numerator
    refs[-1][...] = total


def whole_kernel(count, q_ref, rk_ref, rv_ref, *refs):
    tokens = q_ref.shape[0] * q_ref.shape[1]
    numerator, total = begin(q_ref, rk_ref, rv_ref, refs[:count], refs[count : 2 * count])
    finish(tokens, numerator, total, refs[-1])


def last_kernel(count, q_ref, numerator_ref, total_ref, *refs):
    key_refs, value_refs, out_ref = refs[:count], refs[count : 2 * count], refs[-1]
    tokens = q_ref.shape[0] * q_ref.shape[1]
    numerator, total = gather_in(
        stacked(q_ref), key_refs, value_refs, numerator_ref[...], total_ref[...]
    )
    finish(tokens, numerator, total, out_ref)


def block_specs(blocks, first):
    return [
        pl.BlockSpec((block.shape[0], HEAD_SIZE), lambda i, offset=offset: (0, offset + i))
        for offset in (first, KEY_VALUE_HEADS + first)
        for block in blocks
    ]


def attention_cost(tokens, heads, positions):
    return pl.CostEstimate(
        flops=2 * 2 * tokens * PER_KEY_VALUE * heads * positions * HEAD_SIZE,
        bytes_accessed=4 * 1024 * 1024,
        transcendentals=2 * tokens * PER_KEY_VALUE * heads * positions,
    )


def attend(queries, response_key_value, state, blocks, group, partial=False):
    responses, length, _ = queries.shape
    per_group = KEY_VALUE_HEADS // GROUPS
    tokens = responses * length
    width = PER_KEY_VALUE * HEAD_SIZE
    first = group * per_group
    in_specs = [pl.BlockSpec((responses, length, width), lambda i: (0, 0, first + i))]
    state_spec = pl.BlockSpec((PER_KEY_VALUE * tokens, HEAD_SIZE), lambda i: (i, 0))
    if state:
        kernel = last_kernel
        operands = state
        in_specs += [state_spec] * 2
    else:
        kernel = first_kernel if partial else whole_kernel
        operands = [response_key_value] * 2
        own = (responses, length, HEAD_SIZE)
        in_specs += [
            pl.BlockSpec(own, lambda i: (0, 0, first + i)),
            pl.BlockSpec(own, lambda i: (0, 0, KEY_VALUE_HEADS + first + i)),
        ]
    if partial:
        out_specs = [state_spec] * 2
        shape = (per_group * PER_KEY_VALUE * tokens, HEAD_SIZE)
        out_shape = [jax.ShapeDtypeStruct(shape, jnp.float32)] * 2
    else:
        out_specs = pl.BlockSpec((tokens, width), lambda i: (0, i))
        out_shape = jax.ShapeDtypeStruct((tokens, per_group * width), jnp.bfloat16)
    return pl.pallas_call(
        functools.partial(kernel, len(blocks)),
        grid=(per_group,),
        in_specs=in_specs + block_specs(blocks, first),
        out_specs=out_specs,
        out_shape=out_shape,
        compiler_params=pltpu.CompilerParams(vmem_limit_bytes=60 * 1024 * 1024),
        cost_estimate=attention_cost(
            tokens, per_group, sum(block.shape[0] for block in blocks) + (0 if state else length)
        ),
    )(queries, *operands, *blocks, *blocks)


def project_kernel(sources, weight_ref, gain_ref, *refs):
    out_ref = refs[-1]
    post = gain_ref[0:1, :]
    final = gain_ref[1:2, :]
    part = weight_ref.shape[0] // GROUPS
    count = GROUPS + 2
    tokens = refs[2].shape[0]
    everything = None
    for g in range(GROUPS):
        rows = jnp.concatenate([refs[s * count + 2 + g][...] for s in range(sources)], axis=0)
        product = jnp.dot(
            rows, weight_ref[g * part : (g + 1) * part, :], preferred_element_type=jnp.float32
        )
        everything = product if g == 0 else everything + product
    for s in range(sources):
        stream_ref, target_ref = refs[s * count : s * count + 2]
        projected = everything[s * tokens : (s + 1) * tokens]
        residual = stream_ref[...].astype(jnp.float32)
        target = target_ref[...].astype(jnp.float32) * final
        scaled = projected * post
        lane = lax.broadcasted_iota(jnp.int32, (tokens, 128), 1)
        packed = jnp.zeros((tokens, 128), jnp.float32)
        terms = (
            projected * projected,
            residual * scaled,
            scaled * scaled,
            target * scaled,
            residual * residual,
            residual * target,
        )
        for k, term in enumerate(terms):
            packed = jnp.where(lane == k, jnp.sum(term, axis=-1, keepdims=True), packed)
        out_ref[s] = jnp.transpose(packed)[0:SUMS, :]


def project(weight, gains, tails, attended):
    sources = len(tails)
    tokens = attended[0][0].shape[0]
    width = weight.shape[1]
    operands = [weight, gains]
    for s in range(sources):
        operands += list(tails[s]) + list(attended[s])
    return pl.pallas_call(
        functools.partial(project_kernel, sources),
        out_shape=jax.ShapeDtypeStruct((sources, SUMS, tokens), jnp.float32),
        compiler_params=pltpu.CompilerParams(vmem_limit_bytes=24 * 1024 * 1024),
        cost_estimate=pl.CostEstimate(
            flops=2 * sources * tokens * 2048 * width,
            bytes_accessed=8 * 1024 * 1024,
            transcendentals=0,
        ),
    )(*operands)


def body(
    queries,
    response_key_value,
    prompt_kv,
    out_weight,
    residual,
    post_gain,
    final_gain,
    target_rows,
    log_norm,
    old_logp,
    ref_logp,
    lengths,
    rewards,
):
    _, responses, length, _ = queries.shape
    tokens = responses * length
    fsdp = lax.axis_size("fsdp")
    dp = lax.axis_size("dp")
    here = lax.axis_index("fsdp")
    columns = D // fsdp

    lane = lax.broadcasted_iota(jnp.int32, (1, length), 1)
    sums = jnp.where(
        lane == 0,
        jnp.sum(rewards[0]),
        jnp.where(lane == 1, jnp.sum(lengths[0]).astype(jnp.float32), 0.0),
    )
    bit = 1

    streams = (residual[0].reshape(tokens, D), target_rows[0].reshape(tokens, D))

    def cut(which, k):
        return lax.dynamic_slice_in_dim(streams[which], (here ^ k) * columns, columns, 1)

    tails = {}
    far = [(k, which) for k in range(2, fsdp) for which in (0, 1)]

    block = prompt_kv[0]
    gathered = [block]
    rounds = dp // 2
    share = -(-len(far) // rounds)
    rows = block.shape[0]
    pieces = {key: cut(key[1], key[0]) for key in far[:share]}
    sums, streams, pieces = lax.optimization_barrier((sums, streams, pieces))
    behind = []
    state = None
    for step in range(rounds):
        keys = far[step * share : (step + 1) * share]
        later = far[(step + 1) * share : (step + 2) * share]
        for key in keys:
            tails[key] = swap(pieces[key], "fsdp", key[0])
        if bit < dp:
            sums = sums + swap(sums, "dp", bit)
            bit *= 2
        if step == rounds - 1:
            final_blocks = [block, crossed]
            final_blocks.append(swap(block[: rows // 2], "dp", 1))
            final_blocks.append(around(crossed[rows // 2 :], "dp"))
            break
        pieces.update({key: cut(key[1], key[0]) for key in later})
        if step == rounds - 2:
            known_blocks = list(gathered)
            state = attend(queries[0], response_key_value[0], None, gathered, 0, True)
        block, crossed = around(block, "dp"), swap(block, "dp", 1)
        held = [tails[key] for key in behind] + [pieces[key] for key in later] + [sums]
        held += state or []
        block, crossed, *held = lax.optimization_barrier((block, crossed, *held))
        if state:
            state = held[-2:]
            held = held[:-2]
        tails.update(zip(behind, held))
        held = held[len(behind) :]
        behind = keys
        pieces.update(zip(later, held))
        sums = held[len(later)]
        gathered += [block, crossed]
        streams, _ = lax.optimization_barrier((streams, sums))
    waiting = far[(rounds - 2) * share :]
    while bit < dp:
        sums = sums + swap(sums, "dp", bit)
        bit *= 2
    for which in (0, 1):
        tails[0, which] = cut(which, 0)
        tails[1, which] = swap(cut(which, 1), "fsdp", 1)

    meta = jnp.concatenate([rewards[0], lengths[0].astype(jnp.float32), sums[0, :2]])
    meta = jnp.pad(meta[None], ((0, 0), (0, length - meta.shape[0])))
    facts = [jnp.concatenate([log_norm[0], old_logp[0], ref_logp[0], meta], axis=0)]
    bit = 1
    while bit < fsdp:
        facts = facts + [swap(value, "fsdp", bit) for value in facts]
        bit *= 2
    gains = lax.dynamic_slice_in_dim(
        jnp.stack([post_gain, final_gain]), here * columns, columns, 1
    )

    attended = [[None] * GROUPS for _ in range(fsdp)]
    asked = queries[0]
    for g in range(GROUPS):
        if g == 0:
            attended[0][g] = attend(asked, response_key_value[0], state, final_blocks, g)
        else:
            attended[0][g] = attend(
                asked, response_key_value[0], None, known_blocks + final_blocks, g
            )
        last = [tails[key] for key in waiting]
        asked, attended[0][g], *last = lax.optimization_barrier((asked, attended[0][g], *last))
        tails.update(zip(waiting, last))
        if g and fsdp > 2:
            attended[0][g], attended[fsdp // 2][g - 1], facts = lax.optimization_barrier(
                (attended[0][g], attended[fsdp // 2][g - 1], facts)
            )
        bit = fsdp // 2
        known = [0]
        while bit > 1:
            for k in known:
                attended[k ^ bit][g] = swap(attended[k][g], "fsdp", bit)
            known = known + [k ^ bit for k in known]
            bit //= 2


    def project_some(some):
        for k in some:
            if k & 1:
                attended[k] = [swap(value, "fsdp", 1) for value in attended[k ^ 1]]
        return project(
            out_weight,
            gains,
            [(tails[k, 0], tails[k, 1]) for k in some],
            [attended[k] for k in some],
        )

    near = project_some(list(range(min(2, fsdp))))
    flat = [attended[k][-1] for k in range(2, fsdp, 2)]
    near, *flat = lax.optimization_barrier((near, *flat))
    for k, value in zip(range(2, fsdp, 2), flat):
        attended[k][-1] = value
    facts = jnp.stack(facts)
    parts = [near, project_some(list(range(2, fsdp)))]
    totals = jnp.concatenate(parts, axis=0)
    bit = 1
    while bit < fsdp:
        other = swap(totals, "fsdp", bit)
        totals = totals + jnp.stack([other[k ^ bit] for k in range(fsdp)])
        bit *= 2

    totals = totals.reshape(fsdp, SUMS, responses, length)
    inverse = lax.rsqrt(totals[:, 0] / D + 1e-06)
    square = totals[:, 4] + inverse * (2.0 * totals[:, 1] + inverse * totals[:, 2])
    outer = lax.rsqrt(jnp.maximum(square, 0.0) / D + 1e-06)
    raw = outer * (totals[:, 5] + inverse * totals[:, 3])
    logit = 30.0 * jnp.tanh(raw / 30.0)
    logp = logit - facts[:, 0:responses]
    old = facts[:, responses : 2 * responses]
    ref = facts[:, 2 * responses : 3 * responses]
    meta = facts[:, 3 * responses]
    group_sum = meta[:, 2 * responses]
    group_count = meta[:, 2 * responses + 1]
    reward = meta[:, :responses]
    size = meta[:, responses : 2 * responses].astype(jnp.int32)
    position = lax.broadcasted_iota(jnp.int32, (fsdp, responses, length), 2)
    live = position < size[:, :, None]
    log_ratio = jnp.where(live, logp - old, 0.0)
    drift = ref - logp
    kl_terms = jnp.where(live, jnp.exp(drift) - drift - 1.0, 0.0)
    advantage = (reward - (group_sum / (responses * dp))[:, None])[:, :, None]
    ratio = jnp.exp(logp - old)
    surrogate = jnp.minimum(ratio * advantage, jnp.clip(ratio, 0.8, 1.2) * advantage)
    objective = jnp.where(live, 0.04 * kl_terms - surrogate, 0.0)
    loss = jnp.full((1, 128), jnp.sum(objective))
    bit = 1
    while bit < dp:
        loss = loss + swap(loss, "dp", bit)
        bit *= 2
    batch_loss = loss[0, 0] / jnp.sum(group_count)
    return (log_ratio[:1], kl_terms[:1], objective[:1], batch_loss)


def solution(mesh):
    rows4 = P("fsdp", "dp", None, None)
    rows3 = P("fsdp", "dp", None)
    in_specs = (
        rows4,
        rows4,
        rows3,
        P(None, "fsdp"),
        rows4,
        P(),
        P(),
        rows4,
        rows3,
        rows3,
        rows3,
        P("fsdp", "dp"),
        P("fsdp", "dp"),
    )
    out_specs = (rows3, rows3, rows3, P())
    return jax.shard_map(body, mesh=mesh, in_specs=in_specs, out_specs=out_specs, check_vma=False)
```

time: 133 us -> 124 us (0.932)
  waiting for transfers between devices: 57.4 us -> 32.3 us
  local copies, waits for them, and re-layouts: 13.8 us -> 18.4 us
  Pallas kernels: 25.3 us -> 29.3 us
  starting transfers between devices: 29.7 us -> 33 us
  other arithmetic: 3.87 us -> 6.89 us
    ppermute x27, waiting for transfers between devices: 56.8 us -> 31.4 us  [swap(): return lax.ppermute(value, axis, [(i, i ^ bit) for i in range(count)])]
    dynamic_slice x2 -> x6, local copies, waits for them, and re-layouts: 4.3 us -> 10 us  [cut(): lax.dynamic_slice_in_dim(streams[which], (here ^ k) * columns, columns, 1)]
    pallas_call x2 -> x3, Pallas kernels: 15.2 us -> 19.6 us  [attend(): pl.pallas_call(functools.partial(kernel, len(blocks)), grid=(per_group,),...]
    ppermute x4, starting transfers between devices: 7.62 us -> 9.77 us  [around(): lax.ppermute(value, axis, [(i, after[i // 2] * 2 + i % 2) for i in range(...]
    convert_element_type x1, other arithmetic: 0.01 us -> 1.37 us  [body(): lengths[0].astype(jnp.float32)]
    unnamed x32 -> x36, local copies, waits for them, and re-layouts: 6.56 us -> 6.46 us
  transfers between devices with their start and end apart: 31 -> 31, of which waited for: 16 -> 16; matrix products, arithmetic and copies ran while one was open for 6% -> 13% of each run, Pallas kernels for 15% -> 20%
where the time goes in v3:
time: 124 us; the launch traced here: 123 us
  starting transfers between devices  33 us (27%)
  waiting for transfers between devices  32.3 us (26%)
  Pallas kernels  29.3 us (24%)
  local copies, waits for them, and re-layouts  18.4 us (15%)
  other arithmetic  6.89 us (6%)
  between operations  3.5 us (3%)
    ppermute x27, waiting for transfers between devices, swap(): return lax.ppermute(value, axis, [(i, i ^ bit) for i in range(count)])  31.4 us
    ppermute x27, starting transfers between devices, swap(): return lax.ppermute(value, axis, [(i, i ^ bit) for i in range(count)])  23.2 us
    pallas_call x3, Pallas kernels, attend(): pl.pallas_call(functools.partial(kernel, len(blocks)), grid=(per_group,),...  19.6 us
    dynamic_slice x6, local copies, waits for them, and re-layouts, cut(): lax.dynamic_slice_in_dim(streams[which], (here ^ k) * columns, columns, 1)  10 us
    ppermute x4, starting transfers between devices, around(): lax.ppermute(value, axis, [(i, after[i // 2] * 2 + i % 2) for i in range(...  9.77 us
    pallas_call x2, Pallas kernels, project(): pl.pallas_call(functools.partial(project_kernel, sources), out_shape=jax....  9.71 us
    unnamed x36, local copies, waits for them, and re-layouts  6.46 us
  transfers between devices with their start and end apart: 31, of which 16 were waited for; matrix products, arithmetic and copies ran while one was open for 13% of the time, Pallas kernels for 20%

profile of v3, /device:TPU:0, one launch (start us, length us, event | category | flops | bytes accessed | tf_op | source)
XLA Modules:
  0.0 123.4 jit_solution(14432263261823786341)
XLA Ops:
  0.6 4.1 %collective-permute-start = (bf16[128,2048]{1,0:T(8,128)(2,1)}, bf16[128,2048]{1,0:T(8,128)(2,1)S(1)}, u32[]{:S(2)}, u32[]{:S(2)}) collective-permute-start(bf16[128,2048]{1,0:T(8,128)(2,1)} %bitcast.101), channel_id=1, source_target_pairs={{0,16},{4,20},{8,0},{12,4},{16,24},{20,28},{24,8},{28,12},{1,17},{... | collective-permute-start | bytes 1572872 | tf_op jit(solution)/shard_map/ppermute | solution.py:30
  4.7 1.5 %collective-permute-start.1 = (bf16[128,2048]{1,0:T(8,128)(2,1)}, bf16[128,2048]{1,0:T(8,128)(2,1)S(1)}, u32[]{:S(2)}, u32[]{:S(2)}) collective-permute-start(bf16[128,2048]{1,0:T(8,128)(2,1)} %bitcast.102), channel_id=1, source_target_pairs={{0,4},{4,0},{8,12},{12,8},{16,20},{20,16},{24,28},{28,24},{1,5},{5... | collective-permute-start | bytes 1572872 | tf_op jit(solution)/shard_map/ppermute | solution.py:23
  11.9 1.5 %collective-permute-start.5 = (bf16[256,1152]{1,0:T(8,128)(2,1)S(1)}, bf16[256,1152]{1,0:T(8,128)(2,1)S(1)}, u32[]{:S(2)}, u32[]{:S(2)}) collective-permute-start(bf16[256,1152]{1,0:T(8,128)(2,1)S(1)} %constant_dynamic-slice_fusion.7), channel_id=1, source_target_pairs={{0,2},{1,3},{2,0},{3,1},{4,6},{5,7},{6,4},{7,5},{8,10},{9,11},{10,... | collective-permute-start | bytes 1769480 | tf_op jit(solution)/shard_map/ppermute | solution.py:23
  13.4 1.9 %constant_dynamic-slice_fusion.6 = bf16[256,1152]{1,0:T(8,128)(2,1)} fusion(bf16[256,4608]{1,0:T(8,128)(2,1)} %bitcast.110, s32[]{:T(128)S(6)} %select_n.53), kind=kLoop, calls=%fused_computation.55 | loop fusion | bytes 1179652 | tf_op jit(solution)/shard_map/dynamic_slice | solution.py:261
  15.3 3.0 %collective-permute-done.2 = f32[1,128]{1,0:T(1,128)S(1)} collective-permute-done((f32[1,128]{1,0:T(1,128)S(1)}, f32[1,128]{1,0:T(1,128)S(1)}, u32[]{:S(2)}, u32[]{:S(2)}) %collective-permute-start.2) | collective-permute-done | bytes 544 | tf_op jit(solution)/shard_map/ppermute | solution.py:23
  18.4 1.6 %collective-permute-start.3 = (bf16[128,2048]{1,0:T(8,128)(2,1)S(1)}, bf16[128,2048]{1,0:T(8,128)(2,1)}, u32[]{:S(2)}, u32[]{:S(2)}) collective-permute-start(bf16[128,2048]{1,0:T(8,128)(2,1)S(1)} %collective-permute-done.refs_1_.refs_6_.refs_10_), channel_id=1, source_target_pairs={{0,16},{4,20},{8,0},{12,4},{16,24},{20,28},{24,8},{28,12},{1,17},{... | collective-permute-start | bytes 1572872 | tf_op jit(solution)/shard_map/ppermute | solution.py:30
  22.0 1.5 %collective-permute-start.9 = (bf16[256,1152]{1,0:T(8,128)(2,1)}, bf16[256,1152]{1,0:T(8,128)(2,1)S(1)}, u32[]{:S(2)}, u32[]{:S(2)}) collective-permute-start(bf16[256,1152]{1,0:T(8,128)(2,1)} %constant_dynamic-slice_fusion.6), channel_id=1, source_target_pairs={{0,2},{1,3},{2,0},{3,1},{4,6},{5,7},{6,4},{7,5},{8,10},{9,11},{10,... | collective-permute-start | bytes 1769480 | tf_op jit(solution)/shard_map/ppermute | solution.py:23
  23.5 2.0 %constant_dynamic-slice_fusion.5 = bf16[256,1152]{1,0:T(8,128)(2,1)} fusion(bf16[256,4608]{1,0:T(8,128)(2,1)} %bitcast.108, s32[]{:T(128)S(6)} %select_n.54), kind=kLoop, calls=%fused_computation.54 | loop fusion | bytes 1179652 | tf_op jit(solution)/shard_map/dynamic_slice | solution.py:261
  25.5 5.5 %collective-permute-done.6 = f32[1,128]{1,0:T(1,128)S(1)} collective-permute-done((f32[1,128]{1,0:T(1,128)S(1)}, f32[1,128]{1,0:T(1,128)S(1)}, u32[]{:S(2)}, u32[]{:S(2)}) %collective-permute-start.6) | collective-permute-done | bytes 544 | tf_op jit(solution)/shard_map/ppermute | solution.py:23
  35.5 1.9 %constant_dynamic-slice_fusion.4 = bf16[256,1152]{1,0:T(8,128)(2,1)} fusion(bf16[256,4608]{1,0:T(8,128)(2,1)} %bitcast.111, s32[]{:T(128)S(6)} %select_n.54), kind=kLoop, calls=%fused_computation.53 | loop fusion | bytes 1179652 | tf_op jit(solution)/shard_map/dynamic_slice | solution.py:261
  37.4 7.2 %shard_map.156 = (f32[2048,128]{1,0:T(8,128)}, f32[2048,128]{1,0:T(8,128)}) custom-call(bf16[2,128,2048]{2,1,0:T(8,128)(2,1)} %bitcast.98, bf16[2,128,2048]{2,1,0:T(8,128)(2,1)} %bitcast.94, bf16[2,128,2048]{2,1,0:T(8,128)(2,1)} %bitcast.95, bf16[128,2048]{1,0:T(8,128)(2,1)} %bitcast.103, bf16[128,2048]{1,0:T(8,128)(2,1)} %copy-done.6, ...), custom_call_target="tpu_custom_call" | custom-call | flops 805306368 | bytes 4194304 | tf_op jit(solution)/shard_map/pallas_call | solution.py:161
  44.9 1.6 %collective-permute-start.14 = (bf16[256,1152]{1,0:T(8,128)(2,1)}, bf16[256,1152]{1,0:T(8,128)(2,1)S(1)}, u32[]{:S(2)}, u32[]{:S(2)}) collective-permute-start(bf16[256,1152]{1,0:T(8,128)(2,1)} %constant_dynamic-slice_fusion.4), channel_id=1, source_target_pairs={{0,3},{1,2},{2,1},{3,0},{4,7},{5,6},{6,5},{7,4},{8,11},{9,10},{10,... | collective-permute-start | bytes 1769480 | tf_op jit(solution)/shard_map/ppermute | solution.py:23
  47.2 2.7 %collective-permute-start.12 = (bf16[64,2048]{1,0:T(8,128)(2,1)S(1)}, bf16[64,2048]{1,0:T(8,128)(2,1)S(1)}, u32[]{:S(2)}, u32[]{:S(2)}) collective-permute-start(bf16[64,2048]{1,0:T(8,128)(2,1)S(1)} %slice.86), channel_id=1, source_target_pairs={{0,16},{4,20},{8,0},{12,4},{16,24},{20,28},{24,8},{28,12},{1,17},{... | collective-permute-start | bytes 786440 | tf_op jit(solution)/shard_map/ppermute | solution.py:30
  50.0 4.8 %collective-permute-done.11.refs_2_.refs_6_.refs_7_.refs_16_ = bf16[64,2048]{1,0:T(8,128)(2,1)S(1)} collective-permute-done((bf16[64,2048]{1,0:T(8,128)(2,1)S(1)}, bf16[64,2048]{1,0:T(8,128)(2,1)S(1)}, u32[]{:S(2)}, u32[]{:S(2)}) %collective-permute-start.11) | collective-permute-done | bytes 262176 | tf_op jit(solution)/shard_map/ppermute | solution.py:23
  57.0 4.8 %shard_map.157.refs_2_ = bf16[256,1024]{1,0:T(8,128)(2,1)} custom-call(bf16[2,128,2048]{2,1,0:T(8,128)(2,1)} %bitcast.99, f32[2048,128]{1,0:T(8,128)} %get-tuple-element.63.numerator_ref, f32[2048,128]{1,0:T(8,128)} %get-tuple-element.64.total_ref, bf16[128,2048]{1,0:T(8,128)(2,1)} %copy-done.4, bf16[128,2048]{1,0:T(8,128)(2,1)} %copy-done.5, ...), custom_call_target="tpu_custom_call" | custom-call | flops 402653184 | bytes 4194304 | tf_op jit(solution)/shard_map/pallas_call | solution.py:161
  61.9 2.2 %collective-permute-done.14.refs_5_ = bf16[256,1152]{1,0:T(8,128)(2,1)S(1)} collective-permute-done((bf16[256,1152]{1,0:T(8,128)(2,1)}, bf16[256,1152]{1,0:T(8,128)(2,1)S(1)}, u32[]{:S(2)}, u32[]{:S(2)}) %collective-permute-start.14) | collective-permute-done | bytes 589856 | tf_op jit(solution)/shard_map/ppermute | solution.py:23
  64.0 1.5 %collective-permute-start.15 = (bf16[256,1024]{1,0:T(8,128)(2,1)}, bf16[256,1024]{1,0:T(8,128)(2,1)}, u32[]{:S(2)}, u32[]{:S(2)}) collective-permute-start(bf16[256,1024]{1,0:T(8,128)(2,1)} %shard_map.157.refs_2_), channel_id=1, source_target_pairs={{0,2},{1,3},{2,0},{3,1},{4,6},{5,7},{6,4},{7,5},{8,10},{9,11},{10,... | collective-permute-start | bytes 1572872 | tf_op jit(solution)/shard_map/ppermute | solution.py:23
  65.5 2.2 %constant_dynamic-slice_fusion.1 = (bf16[256,1152]{1,0:T(8,128)(2,1)}, bf16[256,1152]{1,0:T(8,128)(2,1)S(1)}) fusion(bf16[256,4608]{1,0:T(8,128)(2,1)} %bitcast.109, s32[]{:T(128)S(6)} %select_n.56, s32[]{:T(128)S(6)} %select_n.55), kind=kLoop, calls=%fused_computation.50 | loop fusion | bytes 2359304 | tf_op jit(solution)/shard_map/dynamic_slice | solution.py:261
  69.7 7.6 %shard_map.158.refs_3_ = bf16[256,1024]{1,0:T(8,128)(2,1)} custom-call(bf16[2,128,2048]{2,1,0:T(8,128)(2,1)} %bitcast.100, bf16[2,128,2048]{2,1,0:T(8,128)(2,1)} %bitcast.96, bf16[2,128,2048]{2,1,0:T(8,128)(2,1)} %bitcast.97, bf16[128,2048]{1,0:T(8,128)(2,1)} %bitcast.105, bf16[128,2048]{1,0:T(8,128)(2,1)} %copy-done.6, bf16[128,2048]{1,0:T(8,128)(2,1)} %copy-done.7, ...), custom_call_target="tpu_custom_call" | custom-call | flops 1207959552 | bytes 4194304 | tf_op jit(solution)/shard_map/pallas_call | solution.py:161
  78.3 1.5 %collective-permute-start.23 = (bf16[256,1024]{1,0:T(8,128)(2,1)}, bf16[256,1024]{1,0:T(8,128)(2,1)S(1)}, u32[]{:S(2)}, u32[]{:S(2)}) collective-permute-start(bf16[256,1024]{1,0:T(8,128)(2,1)} %shard_map.158.refs_3_), channel_id=1, source_target_pairs={{0,2},{1,3},{2,0},{3,1},{4,6},{5,7},{6,4},{7,5},{8,10},{9,11},{10,... | collective-permute-start | bytes 1572872 | tf_op jit(solution)/shard_map/ppermute | solution.py:23
  80.4 2.3 %copy-done = bf16[2048,1152]{1,0:T(8,128)(2,1)S(1)} copy-done((bf16[2048,1152]{1,0:T(8,128)(2,1)S(1)}, bf16[2048,1152]{1,0:T(8,128)(2,1)}, u32[]{:S(2)}) %copy-start) | copy-done | bytes 4718616
  83.8 4.9 %shard_map.159 = f32[2,8,256]{2,1,0:T(8,128)S(1)} custom-call(bf16[2048,1152]{1,0:T(8,128)(2,1)S(1)} %copy-done, f32[2,1152]{1,0:T(2,128)S(1)} %fusion.gain_ref, bf16[256,1152]{1,0:T(8,128)(2,1)S(1)} %get-tuple-element.99.refs_0_, bf16[256,1152]{1,0:T(8,128)(2,1)S(1)} %get-tuple-element.97.refs_1_, bf16[256,1024]{1,0:T(8,128)(2,1)S(1)} %copy-done.3, ...), custom_call_target="tpu_custom_call" | custom-call | flops 2415919104 | bytes 8388608 | tf_op jit(solution)/shard_map/pallas_call | solution.py:216
  88.8 4.1 %collective-permute-done.23.refs_3_ = bf16[256,1024]{1,0:T(8,128)(2,1)S(1)} collective-permute-done((bf16[256,1024]{1,0:T(8,128)(2,1)}, bf16[256,1024]{1,0:T(8,128)(2,1)S(1)}, u32[]{:S(2)}, u32[]{:S(2)}) %collective-permute-start.23) | collective-permute-done | bytes 524320 | tf_op jit(solution)/shard_map/ppermute | solution.py:23
  92.9 1.9 %collective-permute-done.25.refs_7_ = bf16[256,1024]{1,0:T(8,128)(2,1)S(1)} collective-permute-done((bf16[256,1024]{1,0:T(8,128)(2,1)S(1)}, bf16[256,1024]{1,0:T(8,128)(2,1)S(1)}, u32[]{:S(2)}, u32[]{:S(2)}) %collective-permute-start.25) | collective-permute-done | bytes 524320 | tf_op jit(solution)/shard_map/ppermute | solution.py:23
  94.8 2.3 %copy-done.1 = bf16[2048,1152]{1,0:T(8,128)(2,1)S(1)} copy-done((bf16[2048,1152]{1,0:T(8,128)(2,1)S(1)}, bf16[2048,1152]{1,0:T(8,128)(2,1)}, u32[]{:S(2)}) %copy-start.1) | copy-done | bytes 4718616
  97.1 4.8 %shard_map.160 = f32[2,8,256]{2,1,0:T(8,128)S(1)} custom-call(bf16[2048,1152]{1,0:T(8,128)(2,1)S(1)} %copy-done.1, f32[2,1152]{1,0:T(2,128)S(1)} %fusion.gain_ref, bf16[256,1152]{1,0:T(8,128)(2,1)S(1)} %collective-permute-done.5.refs_0_, bf16[256,1152]{1,0:T(8,128)(2,1)S(1)} %collective-permute-done.9.refs_1_, ...), custom_call_target="tpu_custom_call" | custom-call | flops 2415919104 | bytes 8388608 | tf_op jit(solution)/shard_map/pallas_call | solution.py:216
  103.2 1.6 %collective-permute-start.27 = (f32[4,8,256]{2,1,0:T(8,128)S(1)}, f32[4,8,256]{2,1,0:T(8,128)S(1)}, u32[]{:S(2)}, u32[]{:S(2)}) collective-permute-start(f32[4,8,256]{2,1,0:T(8,128)S(1)} %maximum_add_fusion), channel_id=1, source_target_pairs={{0,2},{1,3},{2,0},{3,1},{4,6},{5,7},{6,4},{7,5},{8,10},{9,11},{10,... | collective-permute-start | bytes 98312 | tf_op jit(solution)/shard_map/ppermute | solution.py:23
  104.9 2.2 %collective-permute-done.27 = f32[4,8,256]{2,1,0:T(8,128)S(1)} collective-permute-done((f32[4,8,256]{2,1,0:T(8,128)S(1)}, f32[4,8,256]{2,1,0:T(8,128)S(1)}, u32[]{:S(2)}, u32[]{:S(2)}) %collective-permute-start.27) | collective-permute-done | bytes 32800 | tf_op jit(solution)/shard_map/ppermute | solution.py:23
  109.8 2.3 %collective-permute-done.28 = f32[1,128]{1,0:T(1,128)S(1)} collective-permute-done((f32[1,128]{1,0:T(1,128)S(1)}, f32[1,128]{1,0:T(1,128)S(1)}, u32[]{:S(2)}, u32[]{:S(2)}) %collective-permute-start.28) | collective-permute-done | bytes 544 | tf_op jit(solution)/shard_map/ppermute | solution.py:23
  112.8 1.5 %collective-permute-start.29 = (f32[1,128]{1,0:T(1,128)S(1)}, f32[1,128]{1,0:T(1,128)S(1)}, u32[]{:S(2)}, u32[]{:S(2)}) collective-permute-start(f32[1,128]{1,0:T(1,128)S(1)} %broadcast_add_fusion), channel_id=1, source_target_pairs={{0,8},{4,12},{8,0},{12,4},{16,24},{20,28},{24,16},{28,20},{1,9},{5... | collective-permute-start | bytes 1544 | tf_op jit(solution)/shard_map/ppermute | solution.py:23
  114.3 2.0 %collective-permute-done.29 = f32[1,128]{1,0:T(1,128)S(1)} collective-permute-done((f32[1,128]{1,0:T(1,128)S(1)}, f32[1,128]{1,0:T(1,128)S(1)}, u32[]{:S(2)}, u32[]{:S(2)}) %collective-permute-start.29) | collective-permute-done | bytes 544 | tf_op jit(solution)/shard_map/ppermute | solution.py:23
  117.0 2.4 %collective-permute-start.30 = (f32[1,128]{1,0:T(1,128)S(1)}, f32[1,128]{1,0:T(1,128)S(1)}, u32[]{:S(2)}, u32[]{:S(2)}) collective-permute-start(f32[1,128]{1,0:T(1,128)S(1)} %fusion.20), channel_id=1, source_target_pairs={{0,16},{4,20},{8,24},{12,28},{16,0},{20,4},{24,8},{28,12},{1,17},{... | collective-permute-start | bytes 1544 | tf_op jit(solution)/shard_map/ppermute | solution.py:23
  (115 shorter events, 26.8 us)
Async XLA Ops:
  0.6 17.8 %collective-permute-start = (bf16[128,2048]{1,0:T(8,128)(2,1)}, bf16[128,2048]{1,0:T(8,128)(2,1)S(1)}, u32[]{:S(2)}, u32[]{:S(2)}) collective-permute-start(bf16[128,2048]{1,0:T(8,128)(2,1)} %bitcast.101), channel_id=1, source_target_pairs={{0,16},{4,20},{8,0},{12,4},{16,24},{20,28},{24,8},{28,12},{1,17},{... | collective-permute-start | bytes 1572872 | tf_op jit(solution)/shard_map/ppermute | solution.py:30
  4.7 13.7 %collective-permute-start.1 = (bf16[128,2048]{1,0:T(8,128)(2,1)}, bf16[128,2048]{1,0:T(8,128)(2,1)S(1)}, u32[]{:S(2)}, u32[]{:S(2)}) collective-permute-start(bf16[128,2048]{1,0:T(8,128)(2,1)} %bitcast.102), channel_id=1, source_target_pairs={{0,4},{4,0},{8,12},{12,8},{16,20},{20,16},{24,28},{28,24},{1,5},{5... | collective-permute-start | bytes 1572872 | tf_op jit(solution)/shard_map/ppermute | solution.py:23
  11.3 7.1 %collective-permute-start.2 = (f32[1,128]{1,0:T(1,128)S(1)}, f32[1,128]{1,0:T(1,128)S(1)}, u32[]{:S(2)}, u32[]{:S(2)}) collective-permute-start(f32[1,128]{1,0:T(1,128)S(1)} %compare_select_fusion.1), channel_id=1, source_target_pairs={{0,4},{4,0},{8,12},{12,8},{16,20},{20,16},{24,28},{28,24},{1,5},{5... | collective-permute-start | bytes 1544 | tf_op jit(solution)/shard_map/ppermute | solution.py:23
  11.9 19.1 %collective-permute-start.5 = (bf16[256,1152]{1,0:T(8,128)(2,1)S(1)}, bf16[256,1152]{1,0:T(8,128)(2,1)S(1)}, u32[]{:S(2)}, u32[]{:S(2)}) collective-permute-start(bf16[256,1152]{1,0:T(8,128)(2,1)S(1)} %constant_dynamic-slice_fusion.7), channel_id=1, source_target_pairs={{0,2},{1,3},{2,0},{3,1},{4,6},{5,7},{6,4},{7,5},{8,10},{9,11},{10,... | collective-permute-start | bytes 1769480 | tf_op jit(solution)/shard_map/ppermute | solution.py:23
  18.4 19.0 %copy-start.6 = (bf16[128,2048]{1,0:T(8,128)(2,1)}, bf16[128,2048]{1,0:T(8,128)(2,1)S(1)}, u32[]{:S(2)}) copy-start(bf16[128,2048]{1,0:T(8,128)(2,1)S(1)} %collective-permute-done.refs_1_.refs_6_.refs_10_) | copy-start | bytes 1572868
  18.4 12.6 %collective-permute-start.3 = (bf16[128,2048]{1,0:T(8,128)(2,1)S(1)}, bf16[128,2048]{1,0:T(8,128)(2,1)}, u32[]{:S(2)}, u32[]{:S(2)}) collective-permute-start(bf16[128,2048]{1,0:T(8,128)(2,1)S(1)} %collective-permute-done.refs_1_.refs_6_.refs_10_), channel_id=1, source_target_pairs={{0,16},{4,20},{8,0},{12,4},{16,24},{20,28},{24,8},{28,12},{1,17},{... | collective-permute-start | bytes 1572872 | tf_op jit(solution)/shard_map/ppermute | solution.py:30
  20.0 12.1 %collective-permute-start.4 = (bf16[128,2048]{1,0:T(8,128)(2,1)S(1)}, bf16[128,2048]{1,0:T(8,128)(2,1)S(1)}, u32[]{:S(2)}, u32[]{:S(2)}) collective-permute-start(bf16[128,2048]{1,0:T(8,128)(2,1)S(1)} %collective-permute-done.refs_1_.refs_6_.refs_10_), channel_id=1, source_target_pairs={{0,4},{4,0},{8,12},{12,8},{16,20},{20,16},{24,28},{28,24},{1,5},{5... | collective-permute-start | bytes 1572872 | tf_op jit(solution)/shard_map/ppermute | solution.py:23
  21.5 9.4 %collective-permute-start.6 = (f32[1,128]{1,0:T(1,128)S(1)}, f32[1,128]{1,0:T(1,128)S(1)}, u32[]{:S(2)}, u32[]{:S(2)}) collective-permute-start(f32[1,128]{1,0:T(1,128)S(1)} %add.65), channel_id=1, source_target_pairs={{0,8},{4,12},{8,0},{12,4},{16,24},{20,28},{24,16},{28,20},{1,9},{5... | collective-permute-start | bytes 1544 | tf_op jit(solution)/shard_map/ppermute | solution.py:23
  22.0 22.7 %collective-permute-start.9 = (bf16[256,1152]{1,0:T(8,128)(2,1)}, bf16[256,1152]{1,0:T(8,128)(2,1)S(1)}, u32[]{:S(2)}, u32[]{:S(2)}) collective-permute-start(bf16[256,1152]{1,0:T(8,128)(2,1)} %constant_dynamic-slice_fusion.6), channel_id=1, source_target_pairs={{0,2},{1,3},{2,0},{3,1},{4,6},{5,7},{6,4},{7,5},{8,10},{9,11},{10,... | collective-permute-start | bytes 1769480 | tf_op jit(solution)/shard_map/ppermute | solution.py:23
  32.2 12.5 %collective-permute-start.7 = (bf16[128,2048]{1,0:T(8,128)(2,1)}, bf16[128,2048]{1,0:T(8,128)(2,1)S(1)}, u32[]{:S(2)}, u32[]{:S(2)}) collective-permute-start(bf16[128,2048]{1,0:T(8,128)(2,1)} %collective-permute-done.3.refs_3_.refs_8_.refs_12_), channel_id=1, source_target_pairs={{0,16},{4,20},{8,0},{12,4},{16,24},{20,28},{24,8},{28,12},{1,17},{... | collective-permute-start | bytes 1572872 | tf_op jit(solution)/shard_map/ppermute | solution.py:30
  33.5 11.4 %collective-permute-start.8 = (bf16[128,2048]{1,0:T(8,128)(2,1)}, bf16[128,2048]{1,0:T(8,128)(2,1)S(1)}, u32[]{:S(2)}, u32[]{:S(2)}) collective-permute-start(bf16[128,2048]{1,0:T(8,128)(2,1)} %collective-permute-done.3.refs_3_.refs_8_.refs_12_), channel_id=1, source_target_pairs={{0,4},{4,0},{8,12},{12,8},{16,20},{20,16},{24,28},{28,24},{1,5},{5... | collective-permute-start | bytes 1572872 | tf_op jit(solution)/shard_map/ppermute | solution.py:23
  35.0 9.6 %collective-permute-start.10 = (f32[1,128]{1,0:T(1,128)S(1)}, f32[1,128]{1,0:T(1,128)S(1)}, u32[]{:S(2)}, u32[]{:S(2)}) collective-permute-start(f32[1,128]{1,0:T(1,128)S(1)} %add.67), channel_id=1, source_target_pairs={{0,16},{4,20},{8,24},{12,28},{16,0},{20,4},{24,8},{28,12},{1,17},{... | collective-permute-start | bytes 1544 | tf_op jit(solution)/shard_map/ppermute | solution.py:23
  35.5 26.4 %collective-permute-start.13 = (bf16[256,1152]{1,0:T(8,128)(2,1)}, bf16[256,1152]{1,0:T(8,128)(2,1)S(1)}, u32[]{:S(2)}, u32[]{:S(2)}) collective-permute-start(bf16[256,1152]{1,0:T(8,128)(2,1)} %constant_dynamic-slice_fusion.5), channel_id=1, source_target_pairs={{0,3},{1,2},{2,1},{3,0},{4,7},{5,6},{6,5},{7,4},{8,11},{9,10},{10,... | collective-permute-start | bytes 1769480 | tf_op jit(solution)/shard_map/ppermute | solution.py:23
  44.9 19.1 %collective-permute-start.14 = (bf16[256,1152]{1,0:T(8,128)(2,1)}, bf16[256,1152]{1,0:T(8,128)(2,1)S(1)}, u32[]{:S(2)}, u32[]{:S(2)}) collective-permute-start(bf16[256,1152]{1,0:T(8,128)(2,1)} %constant_dynamic-slice_fusion.4), channel_id=1, source_target_pairs={{0,3},{1,2},{2,1},{3,0},{4,7},{5,6},{6,5},{7,4},{8,11},{9,10},{10,... | collective-permute-start | bytes 1769480 | tf_op jit(solution)/shard_map/ppermute | solution.py:23
  46.5 8.3 %collective-permute-start.11 = (bf16[64,2048]{1,0:T(8,128)(2,1)S(1)}, bf16[64,2048]{1,0:T(8,128)(2,1)S(1)}, u32[]{:S(2)}, u32[]{:S(2)}) collective-permute-start(bf16[64,2048]{1,0:T(8,128)(2,1)S(1)} %slice.85), channel_id=1, source_target_pairs={{0,4},{4,0},{8,12},{12,8},{16,20},{20,16},{24,28},{28,24},{1,5},{5... | collective-permute-start | bytes 786440 | tf_op jit(solution)/shard_map/ppermute | solution.py:23
  47.2 9.2 %collective-permute-start.12 = (bf16[64,2048]{1,0:T(8,128)(2,1)S(1)}, bf16[64,2048]{1,0:T(8,128)(2,1)S(1)}, u32[]{:S(2)}, u32[]{:S(2)}) collective-permute-start(bf16[64,2048]{1,0:T(8,128)(2,1)S(1)} %slice.86), channel_id=1, source_target_pairs={{0,16},{4,20},{8,0},{12,4},{16,24},{20,28},{24,8},{28,12},{1,17},{... | collective-permute-start | bytes 786440 | tf_op jit(solution)/shard_map/ppermute | solution.py:30
  50.0 19.2 %collective-permute-start.16 = (f32[7,128]{1,0:T(8,128)S(1)}, f32[7,128]{1,0:T(8,128)S(1)}, u32[]{:S(2)}, u32[]{:S(2)}) collective-permute-start(f32[7,128]{1,0:T(8,128)S(1)} %select_maximum_fusion), channel_id=1, source_target_pairs={{0,1},{1,0},{2,3},{3,2},{4,5},{5,4},{6,7},{7,6},{8,9},{9,8},{10,11... | collective-permute-start | bytes 10760 | tf_op jit(solution)/shard_map/ppermute | solution.py:23
  54.9 22.4 %collective-permute-start.17 = (f32[7,128]{1,0:T(8,128)S(1)}, f32[7,128]{1,0:T(8,128)S(1)}, u32[]{:S(2)}, u32[]{:S(2)}) collective-permute-start(f32[7,128]{1,0:T(8,128)S(1)} %select_maximum_fusion), channel_id=1, source_target_pairs={{0,2},{1,3},{2,0},{3,1},{4,6},{5,7},{6,4},{7,5},{8,10},{9,11},{10,... | collective-permute-start | bytes 10760 | tf_op jit(solution)/shard_map/ppermute | solution.py:23
  64.0 14.3 %collective-permute-start.15 = (bf16[256,1024]{1,0:T(8,128)(2,1)}, bf16[256,1024]{1,0:T(8,128)(2,1)}, u32[]{:S(2)}, u32[]{:S(2)}) collective-permute-start(bf16[256,1024]{1,0:T(8,128)(2,1)} %shard_map.157.refs_2_), channel_id=1, source_target_pairs={{0,2},{1,3},{2,0},{3,1},{4,6},{5,7},{6,4},{7,5},{8,10},{9,11},{10,... | collective-permute-start | bytes 1572872 | tf_op jit(solution)/shard_map/ppermute | solution.py:23
  68.6 11.4 %collective-permute-start.19 = (bf16[256,1152]{1,0:T(8,128)(2,1)}, bf16[256,1152]{1,0:T(8,128)(2,1)}, u32[]{:S(2)}, u32[]{:S(2)}) collective-permute-start(bf16[256,1152]{1,0:T(8,128)(2,1)} %get-tuple-element.98), channel_id=1, source_target_pairs={{0,1},{1,0},{2,3},{3,2},{4,5},{5,4},{6,7},{7,6},{8,9},{9,8},{10,11... | collective-permute-start | bytes 1769480 | tf_op jit(solution)/shard_map/ppermute | solution.py:23
  68.7 11.6 %collective-permute-start.20 = (bf16[256,1152]{1,0:T(8,128)(2,1)}, bf16[256,1152]{1,0:T(8,128)(2,1)}, u32[]{:S(2)}, u32[]{:S(2)}) collective-permute-start(bf16[256,1152]{1,0:T(8,128)(2,1)} %get-tuple-element.96), channel_id=1, source_target_pairs={{0,1},{1,0},{2,3},{3,2},{4,5},{5,4},{6,7},{7,6},{8,9},{9,8},{10,11... | collective-permute-start | bytes 1769480 | tf_op jit(solution)/shard_map/ppermute | solution.py:23
  69.2 9.2 %collective-permute-start.18 = (f32[7,128]{1,0:T(8,128)S(1)}, f32[7,128]{1,0:T(8,128)S(1)}, u32[]{:S(2)}, u32[]{:S(2)}) collective-permute-start(f32[7,128]{1,0:T(8,128)S(1)} %collective-permute-done.16), channel_id=1, source_target_pairs={{0,2},{1,3},{2,0},{3,1},{4,6},{5,7},{6,4},{7,5},{8,10},{9,11},{10,... | collective-permute-start | bytes 10760 | tf_op jit(solution)/shard_map/ppermute | solution.py:23
  77.3 3.0 %collective-permute-start.21 = (bf16[256,1024]{1,0:T(8,128)(2,1)S(1)}, bf16[256,1024]{1,0:T(8,128)(2,1)S(1)}, u32[]{:S(2)}, u32[]{:S(2)}) collective-permute-start(bf16[256,1024]{1,0:T(8,128)(2,1)S(1)} %copy-done.3), channel_id=1, source_target_pairs={{0,1},{1,0},{2,3},{3,2},{4,5},{5,4},{6,7},{7,6},{8,9},{9,8},{10,11... | collective-permute-start | bytes 1572872 | tf_op jit(solution)/shard_map/ppermute | solution.py:23
  78.3 2.1 %collective-permute-start.22 = (bf16[256,1024]{1,0:T(8,128)(2,1)}, bf16[256,1024]{1,0:T(8,128)(2,1)S(1)}, u32[]{:S(2)}, u32[]{:S(2)}) collective-permute-start(bf16[256,1024]{1,0:T(8,128)(2,1)} %shard_map.158.refs_3_), channel_id=1, source_target_pairs={{0,1},{1,0},{2,3},{3,2},{4,5},{5,4},{6,7},{7,6},{8,9},{9,8},{10,11... | collective-permute-start | bytes 1572872 | tf_op jit(solution)/shard_map/ppermute | solution.py:23
  78.3 14.5 %collective-permute-start.23 = (bf16[256,1024]{1,0:T(8,128)(2,1)}, bf16[256,1024]{1,0:T(8,128)(2,1)S(1)}, u32[]{:S(2)}, u32[]{:S(2)}) collective-permute-start(bf16[256,1024]{1,0:T(8,128)(2,1)} %shard_map.158.refs_3_), channel_id=1, source_target_pairs={{0,2},{1,3},{2,0},{3,1},{4,6},{5,7},{6,4},{7,5},{8,10},{9,11},{10,... | collective-permute-start | bytes 1572872 | tf_op jit(solution)/shard_map/ppermute | solution.py:23
  80.0 12.9 %collective-permute-start.24 = (bf16[256,1024]{1,0:T(8,128)(2,1)}, bf16[256,1024]{1,0:T(8,128)(2,1)S(1)}, u32[]{:S(2)}, u32[]{:S(2)}) collective-permute-start(bf16[256,1024]{1,0:T(8,128)(2,1)} %collective-permute-done.15.refs_2_), channel_id=1, source_target_pairs={{0,1},{1,0},{2,3},{3,2},{4,5},{5,4},{6,7},{7,6},{8,9},{9,8},{10,11... | collective-permute-start | bytes 1572872 | tf_op jit(solution)/shard_map/ppermute | solution.py:23
  92.9 1.9 %collective-permute-start.25 = (bf16[256,1024]{1,0:T(8,128)(2,1)S(1)}, bf16[256,1024]{1,0:T(8,128)(2,1)S(1)}, u32[]{:S(2)}, u32[]{:S(2)}) collective-permute-start(bf16[256,1024]{1,0:T(8,128)(2,1)S(1)} %collective-permute-done.23.refs_3_), channel_id=1, source_target_pairs={{0,1},{1,0},{2,3},{3,2},{4,5},{5,4},{6,7},{7,6},{8,9},{9,8},{10,11... | collective-permute-start | bytes 1572872 | tf_op jit(solution)/shard_map/ppermute | solution.py:23
  101.9 1.3 %collective-permute-start.26 = (f32[4,8,256]{2,1,0:T(8,128)S(1)}, f32[4,8,256]{2,1,0:T(8,128)S(1)}, u32[]{:S(2)}, u32[]{:S(2)}) collective-permute-start(f32[4,8,256]{2,1,0:T(8,128)S(1)} %pad_maximum_fusion), channel_id=1, source_target_pairs={{0,1},{1,0},{2,3},{3,2},{4,5},{5,4},{6,7},{7,6},{8,9},{9,8},{10,11... | collective-permute-start | bytes 98312 | tf_op jit(solution)/shard_map/ppermute | solution.py:23
  103.2 4.0 %collective-permute-start.27 = (f32[4,8,256]{2,1,0:T(8,128)S(1)}, f32[4,8,256]{2,1,0:T(8,128)S(1)}, u32[]{:S(2)}, u32[]{:S(2)}) collective-permute-start(f32[4,8,256]{2,1,0:T(8,128)S(1)} %maximum_add_fusion), channel_id=1, source_target_pairs={{0,2},{1,3},{2,0},{3,1},{4,6},{5,7},{6,4},{7,5},{8,10},{9,11},{10,... | collective-permute-start | bytes 98312 | tf_op jit(solution)/shard_map/ppermute | solution.py:23
  108.5 3.6 %collective-permute-start.28 = (f32[1,128]{1,0:T(1,128)S(1)}, f32[1,128]{1,0:T(1,128)S(1)}, u32[]{:S(2)}, u32[]{:S(2)}) collective-permute-start(f32[1,128]{1,0:T(1,128)S(1)} %broadcast_in_dim.29), channel_id=1, source_target_pairs={{0,4},{4,0},{8,12},{12,8},{16,20},{20,16},{24,28},{28,24},{1,5},{5... | collective-permute-start | bytes 1544 | tf_op jit(solution)/shard_map/ppermute | solution.py:23
  112.8 3.6 %collective-permute-start.29 = (f32[1,128]{1,0:T(1,128)S(1)}, f32[1,128]{1,0:T(1,128)S(1)}, u32[]{:S(2)}, u32[]{:S(2)}) collective-permute-start(f32[1,128]{1,0:T(1,128)S(1)} %broadcast_add_fusion), channel_id=1, source_target_pairs={{0,8},{4,12},{8,0},{12,4},{16,24},{20,28},{24,16},{28,20},{1,9},{5... | collective-permute-start | bytes 1544 | tf_op jit(solution)/shard_map/ppermute | solution.py:23
  117.0 4.5 %collective-permute-start.30 = (f32[1,128]{1,0:T(1,128)S(1)}, f32[1,128]{1,0:T(1,128)S(1)}, u32[]{:S(2)}, u32[]{:S(2)}) collective-permute-start(f32[1,128]{1,0:T(1,128)S(1)} %fusion.20), channel_id=1, source_target_pairs={{0,16},{4,20},{8,24},{12,28},{16,0},{20,4},{24,8},{28,12},{1,17},{... | collective-permute-start | bytes 1544 | tf_op jit(solution)/shard_map/ppermute | solution.py:23
  (17 other events, 133.4 us)

commit v4 on v3

--- a/solution.py
+++ b/solution.py
@@ -176,20 +176,20 @@
     post = gain_ref[0:1, :]
     final = gain_ref[1:2, :]
     part = weight_ref.shape[0] // GROUPS
-    count = GROUPS + 2
-    tokens = refs[2].shape[0]
+    count = GROUPS + 1
+    tokens = refs[1].shape[0]
     everything = None
     for g in range(GROUPS):
-        rows = jnp.concatenate([refs[s * count + 2 + g][...] for s in range(sources)], axis=0)
+        rows = jnp.concatenate([refs[s * count + 1 + g][...] for s in range(sources)], axis=0)
         product = jnp.dot(
             rows, weight_ref[g * part : (g + 1) * part, :], preferred_element_type=jnp.float32
         )
         everything = product if g == 0 else everything + product
     for s in range(sources):
-        stream_ref, target_ref = refs[s * count : s * count + 2]
+        tail_ref = refs[s * count]
         projected = everything[s * tokens : (s + 1) * tokens]
-        residual = stream_ref[...].astype(jnp.float32)
-        target = target_ref[...].astype(jnp.float32) * final
+        residual = tail_ref[0:tokens, :].astype(jnp.float32)
+        target = tail_ref[tokens : 2 * tokens, :].astype(jnp.float32) * final
         scaled = projected * post
         lane = lax.broadcasted_iota(jnp.int32, (tokens, 128), 1)
         packed = jnp.zeros((tokens, 128), jnp.float32)
@@ -206,17 +206,17 @@
         out_ref[s] = jnp.transpose(packed)[0:SUMS, :]
 
 
-def project(weight, gains, tails, attended):
+def project(weight, gains, tails, attended, limit):
     sources = len(tails)
     tokens = attended[0][0].shape[0]
     width = weight.shape[1]
     operands = [weight, gains]
     for s in range(sources):
-        operands += list(tails[s]) + list(attended[s])
+        operands += [tails[s]] + list(attended[s])
     return pl.pallas_call(
         functools.partial(project_kernel, sources),
         out_shape=jax.ShapeDtypeStruct((sources, SUMS, tokens), jnp.float32),
-        compiler_params=pltpu.CompilerParams(vmem_limit_bytes=24 * 1024 * 1024),
+        compiler_params=pltpu.CompilerParams(vmem_limit_bytes=limit * 1024 * 1024),
         cost_estimate=pl.CostEstimate(
             flops=2 * sources * tokens * 2048 * width,
             bytes_accessed=8 * 1024 * 1024,
@@ -257,27 +257,28 @@
 
     streams = (residual[0].reshape(tokens, D), target_rows[0].reshape(tokens, D))
 
-    def cut(which, k):
-        return lax.dynamic_slice_in_dim(streams[which], (here ^ k) * columns, columns, 1)
+    def cut(k):
+        start = (here ^ k) * columns
+        return jnp.concatenate(
+            [lax.dynamic_slice_in_dim(value, start, columns, 1) for value in streams], axis=0
+        )
 
     tails = {}
-    far = [(k, which) for k in range(2, fsdp) for which in (0, 1)]
+    far = list(range(2, fsdp))
 
     block = prompt_kv[0]
     gathered = [block]
     rounds = dp // 2
-    share = -(-len(far) // rounds)
+    share = -(-len(far) // max(rounds - 2, 1))
     rows = block.shape[0]
-    pieces = {key: cut(key[1], key[0]) for key in far[:share]}
-    sums, streams, pieces = lax.optimization_barrier((sums, streams, pieces))
-    behind = []
+    pieces = {key: cut(key) for key in far[:share]}
     state = None
     for step in range(rounds):
         keys = far[step * share : (step + 1) * share]
         later = far[(step + 1) * share : (step + 2) * share]
         for key in keys:
-            tails[key] = swap(pieces[key], "fsdp", key[0])
-        if bit < dp:
+            tails[key] = swap(pieces[key], "fsdp", key)
+        if step and bit < dp:
             sums = sums + swap(sums, "dp", bit)
             bit *= 2
         if step == rounds - 1:
@@ -285,11 +286,12 @@
             final_blocks.append(swap(block[: rows // 2], "dp", 1))
             final_blocks.append(around(crossed[rows // 2 :], "dp"))
             break
-        pieces.update({key: cut(key[1], key[0]) for key in later})
+        pieces.update({key: cut(key) for key in later})
         if step == rounds - 2:
             known_blocks = list(gathered)
             state = attend(queries[0], response_key_value[0], None, gathered, 0, True)
         block, crossed = around(block, "dp"), swap(block, "dp", 1)
+        behind = far[max(step - 2, 0) * share : max(step - 1, 0) * share]
         held = [tails[key] for key in behind] + [pieces[key] for key in later] + [sums]
         held += state or []
         block, crossed, *held = lax.optimization_barrier((block, crossed, *held))
@@ -298,18 +300,16 @@
             held = held[:-2]
         tails.update(zip(behind, held))
         held = held[len(behind) :]
-        behind = keys
         pieces.update(zip(later, held))
         sums = held[len(later)]
         gathered += [block, crossed]
         streams, _ = lax.optimization_barrier((streams, sums))
-    waiting = far[(rounds - 2) * share :]
+    waiting = far[(rounds - 3) * share :]
     while bit < dp:
         sums = sums + swap(sums, "dp", bit)
         bit *= 2
-    for which in (0, 1):
-        tails[0, which] = cut(which, 0)
-        tails[1, which] = swap(cut(which, 1), "fsdp", 1)
+    tails[0] = cut(0)
+    tails[1] = swap(cut(1), "fsdp", 1)
 
     meta = jnp.concatenate([rewards[0], lengths[0].astype(jnp.float32), sums[0, :2]])
     meta = jnp.pad(meta[None], ((0, 0), (0, length - meta.shape[0])))
@@ -335,8 +335,8 @@
         asked, attended[0][g], *last = lax.optimization_barrier((asked, attended[0][g], *last))
         tails.update(zip(waiting, last))
         if g and fsdp > 2:
-            attended[0][g], attended[fsdp // 2][g - 1], facts = lax.optimization_barrier(
-                (attended[0][g], attended[fsdp // 2][g - 1], facts)
+            attended[0][g], attended[fsdp // 2][g - 1] = lax.optimization_barrier(
+                (attended[0][g], attended[fsdp // 2][g - 1])
             )
         bit = fsdp // 2
         known = [0]
@@ -347,24 +347,25 @@
             bit //= 2
 
 
-    def project_some(some):
+    def project_some(some, limit):
         for k in some:
             if k & 1:
                 attended[k] = [swap(value, "fsdp", 1) for value in attended[k ^ 1]]
         return project(
             out_weight,
             gains,
-            [(tails[k, 0], tails[k, 1]) for k in some],
+            [tails[k] for k in some],
             [attended[k] for k in some],
-        )
-
-    near = project_some(list(range(min(2, fsdp))))
+            limit,
+        )
+
+    near = project_some(list(range(min(2, fsdp))), 24)
     flat = [attended[k][-1] for k in range(2, fsdp, 2)]
-    near, *flat = lax.optimization_barrier((near, *flat))
+    near, facts, *flat = lax.optimization_barrier((near, facts, *flat))
     for k, value in zip(range(2, fsdp, 2), flat):
         attended[k][-1] = value
     facts = jnp.stack(facts)
-    parts = [near, project_some(list(range(2, fsdp)))]
+    parts = [near, project_some(list(range(2, fsdp)), min(6 * (fsdp - 2), 60))]
     totals = jnp.concatenate(parts, axis=0)
     bit = 1
     while bit < fsdp:

time: 124 us -> 120 us (0.968)
  local copies, waits for them, and re-layouts: 18.4 us -> 10.2 us
  other arithmetic: 6.89 us -> 10.2 us
  waiting for transfers between devices: 32.3 us -> 35.5 us
  starting transfers between devices: 33 us -> 31.3 us
    dynamic_slice x6 -> x3, local copies, waits for them, and re-layouts: 10 us -> 4.64 us  [cut(): lax.dynamic_slice_in_dim(value, start, columns, 1)]
    ppermute x27 -> x24, starting transfers between devices: 23.2 us -> 18.5 us  [swap(): return lax.ppermute(value, axis, [(i, i ^ bit) for i in range(count)])]
    concatenate x0 -> x4, other arithmetic: none -> 4.7 us  [cut(): jnp.concatenate([lax.dynamic_slice_in_dim(value, start, columns, 1) for v...]
    ppermute x4, starting transfers between devices: 9.77 us -> 12.8 us  [around(): lax.ppermute(value, axis, [(i, after[i // 2] * 2 + i % 2) for i in range(...]
    unnamed x36 -> x40, local copies, waits for them, and re-layouts: 6.46 us -> 3.65 us
    ppermute x4, waiting for transfers between devices: 0.96 us -> 2.92 us  [around(): lax.ppermute(value, axis, [(i, after[i // 2] * 2 + i % 2) for i in range(...]
    ppermute x27 -> x24, waiting for transfers between devices: 31.4 us -> 32.5 us  [swap(): return lax.ppermute(value, axis, [(i, i ^ bit) for i in range(count)])]
  transfers between devices with their start and end apart: 31 -> 28, of which waited for: 16 -> 16; matrix products, arithmetic and copies ran while one was open for 13% -> 12% of each run, Pallas kernels for 20% -> 20%
where the time goes in v4:
time: 120 us
  waiting for transfers between devices  35.5 us (30%)
  starting transfers between devices  31.3 us (26%)
  Pallas kernels  29.1 us (24%)
  local copies, waits for them, and re-layouts  10.2 us (8%)
  other arithmetic  10.2 us (8%)
  between operations  3.51 us (3%)
    ppermute x24, waiting for transfers between devices, swap(): return lax.ppermute(value, axis, [(i, i ^ bit) for i in range(count)])  32.5 us
    pallas_call x3, Pallas kernels, attend(): pl.pallas_call(functools.partial(kernel, len(blocks)), grid=(per_group,),...  19.6 us
    ppermute x24, starting transfers between devices, swap(): return lax.ppermute(value, axis, [(i, i ^ bit) for i in range(count)])  18.5 us
    ppermute x4, starting transfers between devices, around(): lax.ppermute(value, axis, [(i, after[i // 2] * 2 + i % 2) for i in range(...  12.8 us
    pallas_call x2, Pallas kernels, project(): pl.pallas_call(functools.partial(project_kernel, sources), out_shape=jax....  9.52 us
    concatenate x4, other arithmetic, cut(): jnp.concatenate([lax.dynamic_slice_in_dim(value, start, columns, 1) for v...  4.7 us
    dynamic_slice x3, local copies, waits for them, and re-layouts, cut(): lax.dynamic_slice_in_dim(value, start, columns, 1)  4.64 us
    unnamed x40, local copies, waits for them, and re-layouts  3.65 us
  transfers between devices with their start and end apart: 28, of which 16 were waited for; matrix products, arithmetic and copies ran while one was open for 12% of the time, Pallas kernels for 20%

profile of v4, /device:TPU:0, one launch (start us, length us, event | category | flops | bytes accessed | tf_op | source)
XLA Modules:
  0.0 119.7 jit_solution(13998284193535877736)
XLA Ops:
  0.6 3.0 %collective-permute-start.1 = (bf16[128,2048]{1,0:T(8,128)(2,1)}, bf16[128,2048]{1,0:T(8,128)(2,1)S(1)}, u32[]{:S(2)}, u32[]{:S(2)}) collective-permute-start(bf16[128,2048]{1,0:T(8,128)(2,1)} %bitcast.101), channel_id=1, source_target_pairs={{0,4},{4,0},{8,12},{12,8},{16,20},{20,16},{24,28},{28,24},{1,5},{5... | collective-permute-start | bytes 1572872 | tf_op jit(solution)/shard_map/ppermute | solution.py:23
  3.6 2.6 %collective-permute-start = (bf16[128,2048]{1,0:T(8,128)(2,1)}, bf16[128,2048]{1,0:T(8,128)(2,1)S(1)}, u32[]{:S(2)}, u32[]{:S(2)}) collective-permute-start(bf16[128,2048]{1,0:T(8,128)(2,1)} %bitcast.102), channel_id=1, source_target_pairs={{0,16},{4,20},{8,0},{12,4},{16,24},{20,28},{24,8},{28,12},{1,17},{... | collective-permute-start | bytes 1572872 | tf_op jit(solution)/shard_map/ppermute | solution.py:30
  6.2 1.5 %constant_dynamic-slice_fusion.5 = (bf16[256,1152]{1,0:T(8,128)(2,1)S(1)}, bf16[256,1152]{1,0:T(8,128)(2,1)S(1)}) fusion(bf16[256,4608]{1,0:T(8,128)(2,1)} %bitcast.109, s32[]{:T(128)S(6)} %select_n.55, s32[]{:T(128)S(6)} %select_n.52), kind=kLoop, calls=%fused_computation.58 | loop fusion | bytes 2359304 | tf_op jit(solution)/shard_map/dynamic_slice | solution.py:263
  9.5 1.5 %collective-permute-start.7 = (bf16[512,1152]{1,0:T(8,128)(2,1)}, bf16[512,1152]{1,0:T(8,128)(2,1)S(1)}, u32[]{:S(2)}, u32[]{:S(2)}) collective-permute-start(bf16[512,1152]{1,0:T(8,128)(2,1)} %pad_maximum_fusion.1), channel_id=1, source_target_pairs={{0,2},{1,3},{2,0},{3,1},{4,6},{5,7},{6,4},{7,5},{8,10},{9,11},{10,... | collective-permute-start | bytes 3538952 | tf_op jit(solution)/shard_map/ppermute | solution.py:23
  15.8 1.7 %collective-permute-done.refs_1_.refs_6_.refs_10_ = bf16[128,2048]{1,0:T(8,128)(2,1)S(1)} collective-permute-done((bf16[128,2048]{1,0:T(8,128)(2,1)}, bf16[128,2048]{1,0:T(8,128)(2,1)S(1)}, u32[]{:S(2)}, u32[]{:S(2)}) %collective-permute-start) | collective-permute-done | bytes 524320 | tf_op jit(solution)/shard_map/ppermute | solution.py:30
  18.0 3.3 %collective-permute-start.2 = (bf16[128,2048]{1,0:T(8,128)(2,1)S(1)}, bf16[128,2048]{1,0:T(8,128)(2,1)}, u32[]{:S(2)}, u32[]{:S(2)}) collective-permute-start(bf16[128,2048]{1,0:T(8,128)(2,1)S(1)} %collective-permute-done.refs_1_.refs_6_.refs_10_), channel_id=1, source_target_pairs={{0,16},{4,20},{8,0},{12,4},{16,24},{20,28},{24,8},{28,12},{1,17},{... | collective-permute-start | bytes 1572872 | tf_op jit(solution)/shard_map/ppermute | solution.py:30
  21.3 1.5 %collective-permute-start.4 = (f32[1,128]{1,0:T(1,128)S(1)}, f32[1,128]{1,0:T(1,128)S(1)}, u32[]{:S(2)}, u32[]{:S(2)}) collective-permute-start(f32[1,128]{1,0:T(1,128)S(1)} %compare_select_fusion.1), channel_id=1, source_target_pairs={{0,4},{4,0},{8,12},{12,8},{16,20},{20,16},{24,28},{28,24},{1,5},{5... | collective-permute-start | bytes 1544 | tf_op jit(solution)/shard_map/ppermute | solution.py:23
  22.8 7.2 %collective-permute-done.4 = f32[1,128]{1,0:T(1,128)S(1)} collective-permute-done((f32[1,128]{1,0:T(1,128)S(1)}, f32[1,128]{1,0:T(1,128)S(1)}, u32[]{:S(2)}, u32[]{:S(2)}) %collective-permute-start.4) | collective-permute-done | bytes 544 | tf_op jit(solution)/shard_map/ppermute | solution.py:23
  31.0 1.5 %collective-permute-start.6 = (bf16[128,2048]{1,0:T(8,128)(2,1)}, bf16[128,2048]{1,0:T(8,128)(2,1)S(1)}, u32[]{:S(2)}, u32[]{:S(2)}) collective-permute-start(bf16[128,2048]{1,0:T(8,128)(2,1)} %collective-permute-done.2.refs_3_.refs_8_.refs_12_), channel_id=1, source_target_pairs={{0,4},{4,0},{8,12},{12,8},{16,20},{20,16},{24,28},{28,24},{1,5},{5... | collective-permute-start | bytes 1572872 | tf_op jit(solution)/shard_map/ppermute | solution.py:23
  32.5 3.5 %collective-permute-start.5 = (bf16[128,2048]{1,0:T(8,128)(2,1)}, bf16[128,2048]{1,0:T(8,128)(2,1)S(1)}, u32[]{:S(2)}, u32[]{:S(2)}) collective-permute-start(bf16[128,2048]{1,0:T(8,128)(2,1)} %collective-permute-done.2.refs_3_.refs_8_.refs_12_), channel_id=1, source_target_pairs={{0,16},{4,20},{8,0},{12,4},{16,24},{20,28},{24,8},{28,12},{1,17},{... | collective-permute-start | bytes 1572872 | tf_op jit(solution)/shard_map/ppermute | solution.py:30
  36.0 7.2 %shard_map.156 = (f32[2048,128]{1,0:T(8,128)}, f32[2048,128]{1,0:T(8,128)}) custom-call(bf16[2,128,2048]{2,1,0:T(8,128)(2,1)} %bitcast.98, bf16[2,128,2048]{2,1,0:T(8,128)(2,1)} %bitcast.94, bf16[2,128,2048]{2,1,0:T(8,128)(2,1)} %bitcast.95, bf16[128,2048]{1,0:T(8,128)(2,1)} %bitcast.103, bf16[128,2048]{1,0:T(8,128)(2,1)} %copy-done.6, ...), custom_call_target="tpu_custom_call" | custom-call | flops 805306368 | bytes 4194304 | tf_op jit(solution)/shard_map/pallas_call | solution.py:161
  43.1 1.6 %collective-permute-done.8 = f32[1,128]{1,0:T(1,128)S(1)} collective-permute-done((f32[1,128]{1,0:T(1,128)S(1)}, f32[1,128]{1,0:T(1,128)S(1)}, u32[]{:S(2)}, u32[]{:S(2)}) %collective-permute-start.8) | collective-permute-done | bytes 544 | tf_op jit(solution)/shard_map/ppermute | solution.py:23
  44.9 3.5 %collective-permute-start.10 = (bf16[64,2048]{1,0:T(8,128)(2,1)S(1)}, bf16[64,2048]{1,0:T(8,128)(2,1)S(1)}, u32[]{:S(2)}, u32[]{:S(2)}) collective-permute-start(bf16[64,2048]{1,0:T(8,128)(2,1)S(1)} %slice.86), channel_id=1, source_target_pairs={{0,16},{4,20},{8,0},{12,4},{16,24},{20,28},{24,8},{28,12},{1,17},{... | collective-permute-start | bytes 786440 | tf_op jit(solution)/shard_map/ppermute | solution.py:30
  48.9 3.1 %constant_dynamic-slice_fusion = (bf16[256,1152]{1,0:T(8,128)(2,1)}, bf16[256,1152]{1,0:T(8,128)(2,1)}, bf16[256,1152]{1,0:T(8,128)(2,1)}, bf16[256,1152]{1,0:T(8,128)(2,1)}) fusion(bf16[256,4608]{1,0:T(8,128)(2,1)} %bitcast.107, s32[]{:T(128)S(6)} %select_n.56, s32[]{:T(128)S(6)} %select_n.51, bf16[256,4608]{1,0:T(8,128)(2,1)} %bitcast.110), kind=kLoop, calls=%fused_computation.53 | loop fusion | bytes 4718600 | tf_op jit(solution)/shard_map/dynamic_slice | solution.py:263
  52.2 2.5 %collective-permute-done.9.refs_2_.refs_6_.refs_7_.refs_16_ = bf16[64,2048]{1,0:T(8,128)(2,1)S(1)} collective-permute-done((bf16[64,2048]{1,0:T(8,128)(2,1)S(1)}, bf16[64,2048]{1,0:T(8,128)(2,1)S(1)}, u32[]{:S(2)}, u32[]{:S(2)}) %collective-permute-start.9) | collective-permute-done | bytes 262176 | tf_op jit(solution)/shard_map/ppermute | solution.py:23
  55.4 4.7 %shard_map.157.refs_1_ = bf16[256,1024]{1,0:T(8,128)(2,1)} custom-call(bf16[2,128,2048]{2,1,0:T(8,128)(2,1)} %bitcast.99, f32[2048,128]{1,0:T(8,128)} %get-tuple-element.53.numerator_ref, f32[2048,128]{1,0:T(8,128)} %get-tuple-element.54.total_ref, bf16[128,2048]{1,0:T(8,128)(2,1)} %copy-done.4, bf16[128,2048]{1,0:T(8,128)(2,1)} %copy-done.3, ...), custom_call_target="tpu_custom_call" | custom-call | flops 402653184 | bytes 4194304 | tf_op jit(solution)/shard_map/pallas_call | solution.py:161
  63.0 1.3 %collective-permute-start.13 = (bf16[512,1152]{1,0:T(8,128)(2,1)}, bf16[512,1152]{1,0:T(8,128)(2,1)S(1)}, u32[]{:S(2)}, u32[]{:S(2)}) collective-permute-start(bf16[512,1152]{1,0:T(8,128)(2,1)} %pad_maximum_fusion.3), channel_id=1, source_target_pairs={{0,1},{1,0},{2,3},{3,2},{4,5},{5,4},{6,7},{7,6},{8,9},{9,8},{10,11... | collective-permute-start | bytes 3538952 | tf_op jit(solution)/shard_map/ppermute | solution.py:23
  64.4 1.6 %collective-permute-start.16 = (f32[1,128]{1,0:T(1,128)S(1)}, f32[1,128]{1,0:T(1,128)S(1)}, u32[]{:S(2)}, u32[]{:S(2)}) collective-permute-start(f32[1,128]{1,0:T(1,128)S(1)} %add.68), channel_id=1, source_target_pairs={{0,16},{4,20},{8,24},{12,28},{16,0},{20,4},{24,8},{28,12},{1,17},{... | collective-permute-start | bytes 1544 | tf_op jit(solution)/shard_map/ppermute | solution.py:23
  66.1 2.8 %collective-permute-done.16 = f32[1,128]{1,0:T(1,128)S(1)} collective-permute-done((f32[1,128]{1,0:T(1,128)S(1)}, f32[1,128]{1,0:T(1,128)S(1)}, u32[]{:S(2)}, u32[]{:S(2)}) %collective-permute-start.16) | collective-permute-done | bytes 544 | tf_op jit(solution)/shard_map/ppermute | solution.py:23
  69.0 7.6 %shard_map.158.refs_2_ = bf16[256,1024]{1,0:T(8,128)(2,1)} custom-call(bf16[2,128,2048]{2,1,0:T(8,128)(2,1)} %bitcast.100, bf16[2,128,2048]{2,1,0:T(8,128)(2,1)} %bitcast.96, bf16[2,128,2048]{2,1,0:T(8,128)(2,1)} %bitcast.97, bf16[128,2048]{1,0:T(8,128)(2,1)} %bitcast.105, bf16[128,2048]{1,0:T(8,128)(2,1)} %copy-done.6, bf16[128,2048]{1,0:T(8,128)(2,1)} %copy-done.5, ...), custom_call_target="tpu_custom_call" | custom-call | flops 1207959552 | bytes 4194304 | tf_op jit(solution)/shard_map/pallas_call | solution.py:161
  77.9 1.3 %pad_maximum_fusion.2.refs_0_ = bf16[512,1152]{1,0:T(8,128)(2,1)S(1)} fusion(bf16[256,1152]{1,0:T(8,128)(2,1)} %get-tuple-element.81, bf16[256,1152]{1,0:T(8,128)(2,1)} %get-tuple-element.100), kind=kLoop, calls=%fused_computation.2 | loop fusion | flops 2359296 | bytes 2359296 | tf_op jit(solution)/shard_map/concatenate | solution.py:262
  79.2 1.6 %collective-permute-start.18 = (f32[7,128]{1,0:T(8,128)S(1)}, f32[7,128]{1,0:T(8,128)S(1)}, u32[]{:S(2)}, u32[]{:S(2)}) collective-permute-start(f32[7,128]{1,0:T(8,128)S(1)} %select_maximum_fusion), channel_id=1, source_target_pairs={{0,2},{1,3},{2,0},{3,1},{4,6},{5,7},{6,4},{7,5},{8,10},{9,11},{10,... | collective-permute-start | bytes 10760 | tf_op jit(solution)/shard_map/ppermute | solution.py:23
  81.3 2.3 %copy-done = bf16[2048,1152]{1,0:T(8,128)(2,1)S(1)} copy-done((bf16[2048,1152]{1,0:T(8,128)(2,1)S(1)}, bf16[2048,1152]{1,0:T(8,128)(2,1)}, u32[]{:S(2)}) %copy-start) | copy-done | bytes 4718616
  83.7 4.8 %shard_map.159 = f32[2,8,256]{2,1,0:T(8,128)S(1)} custom-call(bf16[2048,1152]{1,0:T(8,128)(2,1)S(1)} %copy-done, f32[2,1152]{1,0:T(2,128)S(1)} %fusion.gain_ref, bf16[512,1152]{1,0:T(8,128)(2,1)S(1)} %pad_maximum_fusion.2.refs_0_, bf16[256,1024]{1,0:T(8,128)(2,1)S(1)} %copy-done.2, bf16[256,1024]{1,0:T(8,128)(2,1)S(1)} %copy-done.1, ...), custom_call_target="tpu_custom_call" | custom-call | flops 2415919104 | bytes 8388608 | tf_op jit(solution)/shard_map/pallas_call | solution.py:216
  88.4 3.0 %collective-permute-done.18 = f32[7,128]{1,0:T(8,128)S(1)} collective-permute-done((f32[7,128]{1,0:T(8,128)S(1)}, f32[7,128]{1,0:T(8,128)S(1)}, u32[]{:S(2)}, u32[]{:S(2)}) %collective-permute-start.18) | collective-permute-done | bytes 3616 | tf_op jit(solution)/shard_map/ppermute | solution.py:23
  91.5 1.9 %collective-permute-done.22.refs_5_ = bf16[256,1024]{1,0:T(8,128)(2,1)S(1)} collective-permute-done((bf16[256,1024]{1,0:T(8,128)(2,1)S(1)}, bf16[256,1024]{1,0:T(8,128)(2,1)S(1)}, u32[]{:S(2)}, u32[]{:S(2)}) %collective-permute-start.22) | collective-permute-done | bytes 524320 | tf_op jit(solution)/shard_map/ppermute | solution.py:23
  93.4 4.8 %shard_map.160 = f32[2,8,256]{2,1,0:T(8,128)S(1)} custom-call(bf16[2048,1152]{1,0:T(8,128)(2,1)S(1)} %copy-done, f32[2,1152]{1,0:T(2,128)S(1)} %fusion.gain_ref, bf16[512,1152]{1,0:T(8,128)(2,1)S(1)} %collective-permute-done.7.refs_0_, bf16[256,1024]{1,0:T(8,128)(2,1)} %collective-permute-done.12.refs_1_, ...), custom_call_target="tpu_custom_call" | custom-call | flops 2415919104 | bytes 8388608 | tf_op jit(solution)/shard_map/pallas_call | solution.py:216
  100.2 3.3 %collective-permute-done.24 = f32[4,8,256]{2,1,0:T(8,128)S(1)} collective-permute-done((f32[4,8,256]{2,1,0:T(8,128)S(1)}, f32[4,8,256]{2,1,0:T(8,128)S(1)}, u32[]{:S(2)}, u32[]{:S(2)}) %collective-permute-start.24) | collective-permute-done | bytes 32800 | tf_op jit(solution)/shard_map/ppermute | solution.py:23
  105.4 3.0 %collective-permute-done.25 = f32[1,128]{1,0:T(1,128)S(1)} collective-permute-done((f32[1,128]{1,0:T(1,128)S(1)}, f32[1,128]{1,0:T(1,128)S(1)}, u32[]{:S(2)}, u32[]{:S(2)}) %collective-permute-start.25) | collective-permute-done | bytes 544 | tf_op jit(solution)/shard_map/ppermute | solution.py:23
  109.2 3.5 %collective-permute-done.26 = f32[1,128]{1,0:T(1,128)S(1)} collective-permute-done((f32[1,128]{1,0:T(1,128)S(1)}, f32[1,128]{1,0:T(1,128)S(1)}, u32[]{:S(2)}, u32[]{:S(2)}) %collective-permute-start.26) | collective-permute-done | bytes 544 | tf_op jit(solution)/shard_map/ppermute | solution.py:23
  113.3 1.6 %collective-permute-start.27 = (f32[1,128]{1,0:T(1,128)S(1)}, f32[1,128]{1,0:T(1,128)S(1)}, u32[]{:S(2)}, u32[]{:S(2)}) collective-permute-start(f32[1,128]{1,0:T(1,128)S(1)} %fusion.20), channel_id=1, source_target_pairs={{0,16},{4,20},{8,24},{12,28},{16,0},{20,4},{24,8},{28,12},{1,17},{... | collective-permute-start | bytes 1544 | tf_op jit(solution)/shard_map/ppermute | solution.py:23
  116.7 1.2 collective-permute-done.27
  (114 shorter events, 20.8 us)
Async XLA Ops:
  0.6 15.1 %collective-permute-start.1 = (bf16[128,2048]{1,0:T(8,128)(2,1)}, bf16[128,2048]{1,0:T(8,128)(2,1)S(1)}, u32[]{:S(2)}, u32[]{:S(2)}) collective-permute-start(bf16[128,2048]{1,0:T(8,128)(2,1)} %bitcast.101), channel_id=1, source_target_pairs={{0,4},{4,0},{8,12},{12,8},{16,20},{20,16},{24,28},{28,24},{1,5},{5... | collective-permute-start | bytes 1572872 | tf_op jit(solution)/shard_map/ppermute | solution.py:23
  3.6 13.8 %collective-permute-start = (bf16[128,2048]{1,0:T(8,128)(2,1)}, bf16[128,2048]{1,0:T(8,128)(2,1)S(1)}, u32[]{:S(2)}, u32[]{:S(2)}) collective-permute-start(bf16[128,2048]{1,0:T(8,128)(2,1)} %bitcast.102), channel_id=1, source_target_pairs={{0,16},{4,20},{8,0},{12,4},{16,24},{20,28},{24,8},{28,12},{1,17},{... | collective-permute-start | bytes 1572872 | tf_op jit(solution)/shard_map/ppermute | solution.py:30
  9.5 35.3 %collective-permute-start.7 = (bf16[512,1152]{1,0:T(8,128)(2,1)}, bf16[512,1152]{1,0:T(8,128)(2,1)S(1)}, u32[]{:S(2)}, u32[]{:S(2)}) collective-permute-start(bf16[512,1152]{1,0:T(8,128)(2,1)} %pad_maximum_fusion.1), channel_id=1, source_target_pairs={{0,2},{1,3},{2,0},{3,1},{4,6},{5,7},{6,4},{7,5},{8,10},{9,11},{10,... | collective-permute-start | bytes 3538952 | tf_op jit(solution)/shard_map/ppermute | solution.py:23
  17.4 12.6 %copy-start.6 = (bf16[128,2048]{1,0:T(8,128)(2,1)}, bf16[128,2048]{1,0:T(8,128)(2,1)S(1)}, u32[]{:S(2)}) copy-start(bf16[128,2048]{1,0:T(8,128)(2,1)S(1)} %collective-permute-done.refs_1_.refs_6_.refs_10_) | copy-start | bytes 1572868
  17.4 12.5 %collective-permute-start.3 = (bf16[128,2048]{1,0:T(8,128)(2,1)S(1)}, bf16[128,2048]{1,0:T(8,128)(2,1)S(1)}, u32[]{:S(2)}, u32[]{:S(2)}) collective-permute-start(bf16[128,2048]{1,0:T(8,128)(2,1)S(1)} %collective-permute-done.refs_1_.refs_6_.refs_10_), channel_id=1, source_target_pairs={{0,4},{4,0},{8,12},{12,8},{16,20},{20,16},{24,28},{28,24},{1,5},{5... | collective-permute-start | bytes 1572872 | tf_op jit(solution)/shard_map/ppermute | solution.py:23
  18.0 13.0 %collective-permute-start.2 = (bf16[128,2048]{1,0:T(8,128)(2,1)S(1)}, bf16[128,2048]{1,0:T(8,128)(2,1)}, u32[]{:S(2)}, u32[]{:S(2)}) collective-permute-start(bf16[128,2048]{1,0:T(8,128)(2,1)S(1)} %collective-permute-done.refs_1_.refs_6_.refs_10_), channel_id=1, source_target_pairs={{0,16},{4,20},{8,0},{12,4},{16,24},{20,28},{24,8},{28,12},{1,17},{... | collective-permute-start | bytes 1572872 | tf_op jit(solution)/shard_map/ppermute | solution.py:30
  21.3 40.0 %collective-permute-start.11 = (bf16[512,1152]{1,0:T(8,128)(2,1)}, bf16[512,1152]{1,0:T(8,128)(2,1)S(1)}, u32[]{:S(2)}, u32[]{:S(2)}) collective-permute-start(bf16[512,1152]{1,0:T(8,128)(2,1)} %pad_maximum_fusion), channel_id=1, source_target_pairs={{0,3},{1,2},{2,1},{3,0},{4,7},{5,6},{6,5},{7,4},{8,11},{9,10},{10,... | collective-permute-start | bytes 3538952 | tf_op jit(solution)/shard_map/ppermute | solution.py:23
  21.3 8.7 %collective-permute-start.4 = (f32[1,128]{1,0:T(1,128)S(1)}, f32[1,128]{1,0:T(1,128)S(1)}, u32[]{:S(2)}, u32[]{:S(2)}) collective-permute-start(f32[1,128]{1,0:T(1,128)S(1)} %compare_select_fusion.1), channel_id=1, source_target_pairs={{0,4},{4,0},{8,12},{12,8},{16,20},{20,16},{24,28},{28,24},{1,5},{5... | collective-permute-start | bytes 1544 | tf_op jit(solution)/shard_map/ppermute | solution.py:23
  31.0 13.8 %collective-permute-start.6 = (bf16[128,2048]{1,0:T(8,128)(2,1)}, bf16[128,2048]{1,0:T(8,128)(2,1)S(1)}, u32[]{:S(2)}, u32[]{:S(2)}) collective-permute-start(bf16[128,2048]{1,0:T(8,128)(2,1)} %collective-permute-done.2.refs_3_.refs_8_.refs_12_), channel_id=1, source_target_pairs={{0,4},{4,0},{8,12},{12,8},{16,20},{20,16},{24,28},{28,24},{1,5},{5... | collective-permute-start | bytes 1572872 | tf_op jit(solution)/shard_map/ppermute | solution.py:23
  32.5 12.3 %collective-permute-start.5 = (bf16[128,2048]{1,0:T(8,128)(2,1)}, bf16[128,2048]{1,0:T(8,128)(2,1)S(1)}, u32[]{:S(2)}, u32[]{:S(2)}) collective-permute-start(bf16[128,2048]{1,0:T(8,128)(2,1)} %collective-permute-done.2.refs_3_.refs_8_.refs_12_), channel_id=1, source_target_pairs={{0,16},{4,20},{8,0},{12,4},{16,24},{20,28},{24,8},{28,12},{1,17},{... | collective-permute-start | bytes 1572872 | tf_op jit(solution)/shard_map/ppermute | solution.py:30
  36.0 8.8 %collective-permute-start.8 = (f32[1,128]{1,0:T(1,128)S(1)}, f32[1,128]{1,0:T(1,128)S(1)}, u32[]{:S(2)}, u32[]{:S(2)}) collective-permute-start(f32[1,128]{1,0:T(1,128)S(1)} %add.66), channel_id=1, source_target_pairs={{0,8},{4,12},{8,0},{12,4},{16,24},{20,28},{24,16},{28,20},{1,9},{5... | collective-permute-start | bytes 1544 | tf_op jit(solution)/shard_map/ppermute | solution.py:23
  44.9 7.4 %collective-permute-start.10 = (bf16[64,2048]{1,0:T(8,128)(2,1)S(1)}, bf16[64,2048]{1,0:T(8,128)(2,1)S(1)}, u32[]{:S(2)}, u32[]{:S(2)}) collective-permute-start(bf16[64,2048]{1,0:T(8,128)(2,1)S(1)} %slice.86), channel_id=1, source_target_pairs={{0,16},{4,20},{8,0},{12,4},{16,24},{20,28},{24,8},{28,12},{1,17},{... | collective-permute-start | bytes 786440 | tf_op jit(solution)/shard_map/ppermute | solution.py:30
  48.3 6.4 %collective-permute-start.9 = (bf16[64,2048]{1,0:T(8,128)(2,1)S(1)}, bf16[64,2048]{1,0:T(8,128)(2,1)S(1)}, u32[]{:S(2)}, u32[]{:S(2)}) collective-permute-start(bf16[64,2048]{1,0:T(8,128)(2,1)S(1)} %slice.85), channel_id=1, source_target_pairs={{0,4},{4,0},{8,12},{12,8},{16,20},{20,16},{24,28},{28,24},{1,5},{5... | collective-permute-start | bytes 786440 | tf_op jit(solution)/shard_map/ppermute | solution.py:23
  52.2 9.6 %copy-start.10 = (bf16[256,1152]{1,0:T(8,128)(2,1)S(1)}, bf16[256,1152]{1,0:T(8,128)(2,1)}, u32[]{:S(2)}) copy-start(bf16[256,1152]{1,0:T(8,128)(2,1)} %get-tuple-element.80) | copy-start | bytes 1769476
  52.2 9.6 %copy-start.11 = (bf16[256,1152]{1,0:T(8,128)(2,1)S(1)}, bf16[256,1152]{1,0:T(8,128)(2,1)}, u32[]{:S(2)}) copy-start(bf16[256,1152]{1,0:T(8,128)(2,1)} %get-tuple-element.101) | copy-start | bytes 1769476
  61.3 15.4 %collective-permute-start.12 = (bf16[256,1024]{1,0:T(8,128)(2,1)}, bf16[256,1024]{1,0:T(8,128)(2,1)}, u32[]{:S(2)}, u32[]{:S(2)}) collective-permute-start(bf16[256,1024]{1,0:T(8,128)(2,1)} %shard_map.157.refs_1_), channel_id=1, source_target_pairs={{0,2},{1,3},{2,0},{3,1},{4,6},{5,7},{6,4},{7,5},{8,10},{9,11},{10,... | collective-permute-start | bytes 1572872 | tf_op jit(solution)/shard_map/ppermute | solution.py:23
  63.0 18.3 %collective-permute-start.13 = (bf16[512,1152]{1,0:T(8,128)(2,1)}, bf16[512,1152]{1,0:T(8,128)(2,1)S(1)}, u32[]{:S(2)}, u32[]{:S(2)}) collective-permute-start(bf16[512,1152]{1,0:T(8,128)(2,1)} %pad_maximum_fusion.3), channel_id=1, source_target_pairs={{0,1},{1,0},{2,3},{3,2},{4,5},{5,4},{6,7},{7,6},{8,9},{9,8},{10,11... | collective-permute-start | bytes 3538952 | tf_op jit(solution)/shard_map/ppermute | solution.py:23
  64.4 4.5 %collective-permute-start.16 = (f32[1,128]{1,0:T(1,128)S(1)}, f32[1,128]{1,0:T(1,128)S(1)}, u32[]{:S(2)}, u32[]{:S(2)}) collective-permute-start(f32[1,128]{1,0:T(1,128)S(1)} %add.68), channel_id=1, source_target_pairs={{0,16},{4,20},{8,24},{12,28},{16,0},{20,4},{24,8},{28,12},{1,17},{... | collective-permute-start | bytes 1544 | tf_op jit(solution)/shard_map/ppermute | solution.py:23
  68.9 8.9 %copy-start.15 = (f32[1,2,128]{2,1,0:T(2,128)S(1)}, f32[1,2,128]{2,1,0:T(2,128)}, u32[]{:S(2)}) copy-start(f32[1,2,128]{2,1,0:T(2,128)} %param.23) | copy-start | bytes 3076
  68.9 11.9 %collective-permute-start.14 = (bf16[256,1024]{1,0:T(8,128)(2,1)S(1)}, bf16[256,1024]{1,0:T(8,128)(2,1)}, u32[]{:S(2)}, u32[]{:S(2)}) collective-permute-start(bf16[256,1024]{1,0:T(8,128)(2,1)S(1)} %copy-done.2), channel_id=1, source_target_pairs={{0,1},{1,0},{2,3},{3,2},{4,5},{5,4},{6,7},{7,6},{8,9},{9,8},{10,11... | collective-permute-start | bytes 1572872 | tf_op jit(solution)/shard_map/ppermute | solution.py:23
  76.6 4.7 %collective-permute-start.15 = (bf16[256,1024]{1,0:T(8,128)(2,1)}, bf16[256,1024]{1,0:T(8,128)(2,1)S(1)}, u32[]{:S(2)}, u32[]{:S(2)}) collective-permute-start(bf16[256,1024]{1,0:T(8,128)(2,1)} %shard_map.158.refs_2_), channel_id=1, source_target_pairs={{0,1},{1,0},{2,3},{3,2},{4,5},{5,4},{6,7},{7,6},{8,9},{9,8},{10,11... | collective-permute-start | bytes 1572872 | tf_op jit(solution)/shard_map/ppermute | solution.py:23
  77.3 14.3 %collective-permute-start.20 = (bf16[256,1024]{1,0:T(8,128)(2,1)}, bf16[256,1024]{1,0:T(8,128)(2,1)S(1)}, u32[]{:S(2)}, u32[]{:S(2)}) collective-permute-start(bf16[256,1024]{1,0:T(8,128)(2,1)} %shard_map.158.refs_2_), channel_id=1, source_target_pairs={{0,2},{1,3},{2,0},{3,1},{4,6},{5,7},{6,4},{7,5},{8,10},{9,11},{10,... | collective-permute-start | bytes 1572872 | tf_op jit(solution)/shard_map/ppermute | solution.py:23
  77.8 1.4 %collective-permute-start.17 = (f32[7,128]{1,0:T(8,128)S(1)}, f32[7,128]{1,0:T(8,128)S(1)}, u32[]{:S(2)}, u32[]{:S(2)}) collective-permute-start(f32[7,128]{1,0:T(8,128)S(1)} %select_maximum_fusion), channel_id=1, source_target_pairs={{0,1},{1,0},{2,3},{3,2},{4,5},{5,4},{6,7},{7,6},{8,9},{9,8},{10,11... | collective-permute-start | bytes 10760 | tf_op jit(solution)/shard_map/ppermute | solution.py:23
  79.2 12.3 %collective-permute-start.18 = (f32[7,128]{1,0:T(8,128)S(1)}, f32[7,128]{1,0:T(8,128)S(1)}, u32[]{:S(2)}, u32[]{:S(2)}) collective-permute-start(f32[7,128]{1,0:T(8,128)S(1)} %select_maximum_fusion), channel_id=1, source_target_pairs={{0,2},{1,3},{2,0},{3,1},{4,6},{5,7},{6,4},{7,5},{8,10},{9,11},{10,... | collective-permute-start | bytes 10760 | tf_op jit(solution)/shard_map/ppermute | solution.py:23
  80.8 10.7 %collective-permute-start.19 = (f32[7,128]{1,0:T(8,128)S(1)}, f32[7,128]{1,0:T(8,128)S(1)}, u32[]{:S(2)}, u32[]{:S(2)}) collective-permute-start(f32[7,128]{1,0:T(8,128)S(1)} %collective-permute-done.17), channel_id=1, source_target_pairs={{0,2},{1,3},{2,0},{3,1},{4,6},{5,7},{6,4},{7,5},{8,10},{9,11},{10,... | collective-permute-start | bytes 10760 | tf_op jit(solution)/shard_map/ppermute | solution.py:23
  81.3 10.2 %collective-permute-start.21 = (bf16[256,1024]{1,0:T(8,128)(2,1)}, bf16[256,1024]{1,0:T(8,128)(2,1)S(1)}, u32[]{:S(2)}, u32[]{:S(2)}) collective-permute-start(bf16[256,1024]{1,0:T(8,128)(2,1)} %collective-permute-done.12.refs_1_), channel_id=1, source_target_pairs={{0,1},{1,0},{2,3},{3,2},{4,5},{5,4},{6,7},{7,6},{8,9},{9,8},{10,11... | collective-permute-start | bytes 1572872 | tf_op jit(solution)/shard_map/ppermute | solution.py:23
  91.5 1.9 %collective-permute-start.22 = (bf16[256,1024]{1,0:T(8,128)(2,1)S(1)}, bf16[256,1024]{1,0:T(8,128)(2,1)S(1)}, u32[]{:S(2)}, u32[]{:S(2)}) collective-permute-start(bf16[256,1024]{1,0:T(8,128)(2,1)S(1)} %collective-permute-done.20.refs_2_), channel_id=1, source_target_pairs={{0,1},{1,0},{2,3},{3,2},{4,5},{5,4},{6,7},{7,6},{8,9},{9,8},{10,11... | collective-permute-start | bytes 1572872 | tf_op jit(solution)/shard_map/ppermute | solution.py:23
  98.2 1.3 %collective-permute-start.23 = (f32[4,8,256]{2,1,0:T(8,128)S(1)}, f32[4,8,256]{2,1,0:T(8,128)S(1)}, u32[]{:S(2)}, u32[]{:S(2)}) collective-permute-start(f32[4,8,256]{2,1,0:T(8,128)S(1)} %pad_maximum_fusion.4), channel_id=1, source_target_pairs={{0,1},{1,0},{2,3},{3,2},{4,5},{5,4},{6,7},{7,6},{8,9},{9,8},{10,11... | collective-permute-start | bytes 98312 | tf_op jit(solution)/shard_map/ppermute | solution.py:23
  99.5 4.0 %collective-permute-start.24 = (f32[4,8,256]{2,1,0:T(8,128)S(1)}, f32[4,8,256]{2,1,0:T(8,128)S(1)}, u32[]{:S(2)}, u32[]{:S(2)}) collective-permute-start(f32[4,8,256]{2,1,0:T(8,128)S(1)} %maximum_add_fusion), channel_id=1, source_target_pairs={{0,2},{1,3},{2,0},{3,1},{4,6},{5,7},{6,4},{7,5},{8,10},{9,11},{10,... | collective-permute-start | bytes 98312 | tf_op jit(solution)/shard_map/ppermute | solution.py:23
  104.8 3.6 %collective-permute-start.25 = (f32[1,128]{1,0:T(1,128)S(1)}, f32[1,128]{1,0:T(1,128)S(1)}, u32[]{:S(2)}, u32[]{:S(2)}) collective-permute-start(f32[1,128]{1,0:T(1,128)S(1)} %broadcast_in_dim.29), channel_id=1, source_target_pairs={{0,4},{4,0},{8,12},{12,8},{16,20},{20,16},{24,28},{28,24},{1,5},{5... | collective-permute-start | bytes 1544 | tf_op jit(solution)/shard_map/ppermute | solution.py:23
  109.1 3.6 %collective-permute-start.26 = (f32[1,128]{1,0:T(1,128)S(1)}, f32[1,128]{1,0:T(1,128)S(1)}, u32[]{:S(2)}, u32[]{:S(2)}) collective-permute-start(f32[1,128]{1,0:T(1,128)S(1)} %broadcast_add_fusion), channel_id=1, source_target_pairs={{0,8},{4,12},{8,0},{12,4},{16,24},{20,28},{24,16},{28,20},{1,9},{5... | collective-permute-start | bytes 1544 | tf_op jit(solution)/shard_map/ppermute | solution.py:23
  113.3 4.5 %collective-permute-start.27 = (f32[1,128]{1,0:T(1,128)S(1)}, f32[1,128]{1,0:T(1,128)S(1)}, u32[]{:S(2)}, u32[]{:S(2)}) collective-permute-start(f32[1,128]{1,0:T(1,128)S(1)} %fusion.20), channel_id=1, source_target_pairs={{0,16},{4,20},{8,24},{12,28},{16,0},{20,4},{24,8},{28,12},{1,17},{... | collective-permute-start | bytes 1544 | tf_op jit(solution)/shard_map/ppermute | solution.py:23
  (16 other events, 73.4 us)

commit v5 on v4

--- a/solution.py
+++ b/solution.py
@@ -285,6 +285,7 @@
             final_blocks = [block, crossed]
             final_blocks.append(swap(block[: rows // 2], "dp", 1))
             final_blocks.append(around(crossed[rows // 2 :], "dp"))
+            sums, state = lax.optimization_barrier((sums, state))
             break
         pieces.update({key: cut(key) for key in later})
         if step == rounds - 2:
@@ -396,12 +397,12 @@
     ratio = jnp.exp(logp - old)
     surrogate = jnp.minimum(ratio * advantage, jnp.clip(ratio, 0.8, 1.2) * advantage)
     objective = jnp.where(live, 0.04 * kl_terms - surrogate, 0.0)
-    loss = jnp.full((1, 128), jnp.sum(objective))
+    loss = jnp.sum(objective, axis=(0, 1))[None]
     bit = 1
     while bit < dp:
         loss = loss + swap(loss, "dp", bit)
         bit *= 2
-    batch_loss = loss[0, 0] / jnp.sum(group_count)
+    batch_loss = jnp.sum(loss) / jnp.sum(group_count)
     return (log_ratio[:1], kl_terms[:1], objective[:1], batch_loss)
 
 

time: 120 us -> 118 us (0.983)
  waiting for transfers between devices: 35.5 us -> 33.9 us
  other arithmetic: 10.2 us -> 8.98 us
    ppermute x24, waiting for transfers between devices: 32.5 us -> 28.7 us  [swap(): return lax.ppermute(value, axis, [(i, i ^ bit) for i in range(count)])]
    ppermute x24, starting transfers between devices: 18.5 us -> 21.8 us  [swap(): return lax.ppermute(value, axis, [(i, i ^ bit) for i in range(count)])]
    ppermute x4, starting transfers between devices: 12.8 us -> 9.59 us  [around(): lax.ppermute(value, axis, [(i, after[i // 2] * 2 + i % 2) for i in range(...]
    ppermute x4, waiting for transfers between devices: 2.92 us -> 5.29 us  [around(): lax.ppermute(value, axis, [(i, after[i // 2] * 2 + i % 2) for i in range(...]
    add x3 -> x2, other arithmetic: 1.3 us -> 0.01 us  [body(): loss = loss + swap(loss, 'dp', bit)]
  transfers between devices with their start and end apart: 28 -> 28, of which waited for: 16 -> 16; matrix products, arithmetic and copies ran while one was open for 12% -> 12% of each run, Pallas kernels for 20% -> 21%
where the time goes in v5:
time: 118 us
  waiting for transfers between devices  33.9 us (29%)
  starting transfers between devices  31.4 us (27%)
  Pallas kernels  29.1 us (25%)
  local copies, waits for them, and re-layouts  10.2 us (9%)
  other arithmetic  8.98 us (8%)
  between operations  4.09 us (3%)
    ppermute x24, waiting for transfers between devices, swap(): return lax.ppermute(value, axis, [(i, i ^ bit) for i in range(count)])  28.7 us
    ppermute x24, starting transfers between devices, swap(): return lax.ppermute(value, axis, [(i, i ^ bit) for i in range(count)])  21.8 us
    pallas_call x3, Pallas kernels, attend(): pl.pallas_call(functools.partial(kernel, len(blocks)), grid=(per_group,),...  19.5 us
    ppermute x4, starting transfers between devices, around(): lax.ppermute(value, axis, [(i, after[i // 2] * 2 + i % 2) for i in range(...  9.59 us
    pallas_call x2, Pallas kernels, project(): pl.pallas_call(functools.partial(project_kernel, sources), out_shape=jax....  9.51 us
    ppermute x4, waiting for transfers between devices, around(): lax.ppermute(value, axis, [(i, after[i // 2] * 2 + i % 2) for i in range(...  5.29 us
    concatenate x4, other arithmetic, cut(): jnp.concatenate([lax.dynamic_slice_in_dim(value, start, columns, 1) for v...  4.71 us
    dynamic_slice x3, local copies, waits for them, and re-layouts, cut(): lax.dynamic_slice_in_dim(value, start, columns, 1)  4.64 us
  transfers between devices with their start and end apart: 28, of which 16 were waited for; matrix products, arithmetic and copies ran while one was open for 12% of the time, Pallas kernels for 21%

profile of v5, /device:TPU:0, one launch (start us, length us, event | category | flops | bytes accessed | tf_op | source)
XLA Modules:
  0.0 117.6 jit_solution(5943435699408077180)
XLA Ops:
  0.6 3.0 %collective-permute-start.1 = (bf16[128,2048]{1,0:T(8,128)(2,1)}, bf16[128,2048]{1,0:T(8,128)(2,1)S(1)}, u32[]{:S(2)}, u32[]{:S(2)}) collective-permute-start(bf16[128,2048]{1,0:T(8,128)(2,1)} %bitcast.101), channel_id=1, source_target_pairs={{0,4},{4,0},{8,12},{12,8},{16,20},{20,16},{24,28},{28,24},{1,5},{5... | collective-permute-start | bytes 1572872 | tf_op jit(solution)/shard_map/ppermute | solution.py:23
  3.6 2.6 %collective-permute-start = (bf16[128,2048]{1,0:T(8,128)(2,1)}, bf16[128,2048]{1,0:T(8,128)(2,1)S(1)}, u32[]{:S(2)}, u32[]{:S(2)}) collective-permute-start(bf16[128,2048]{1,0:T(8,128)(2,1)} %bitcast.102), channel_id=1, source_target_pairs={{0,16},{4,20},{8,0},{12,4},{16,24},{20,28},{24,8},{28,12},{1,17},{... | collective-permute-start | bytes 1572872 | tf_op jit(solution)/shard_map/ppermute | solution.py:30
  6.2 1.5 %constant_dynamic-slice_fusion.5 = (bf16[256,1152]{1,0:T(8,128)(2,1)S(1)}, bf16[256,1152]{1,0:T(8,128)(2,1)S(1)}) fusion(bf16[256,4608]{1,0:T(8,128)(2,1)} %bitcast.109, s32[]{:T(128)S(6)} %select_n.55, s32[]{:T(128)S(6)} %select_n.52), kind=kLoop, calls=%fused_computation.58 | loop fusion | bytes 2359304 | tf_op jit(solution)/shard_map/dynamic_slice | solution.py:263
  9.5 1.5 %collective-permute-start.7 = (bf16[512,1152]{1,0:T(8,128)(2,1)}, bf16[512,1152]{1,0:T(8,128)(2,1)S(1)}, u32[]{:S(2)}, u32[]{:S(2)}) collective-permute-start(bf16[512,1152]{1,0:T(8,128)(2,1)} %pad_maximum_fusion.1), channel_id=1, source_target_pairs={{0,2},{1,3},{2,0},{3,1},{4,6},{5,7},{6,4},{7,5},{8,10},{9,11},{10,... | collective-permute-start | bytes 3538952 | tf_op jit(solution)/shard_map/ppermute | solution.py:23
  15.8 1.7 %collective-permute-done.refs_1_.refs_6_.refs_10_ = bf16[128,2048]{1,0:T(8,128)(2,1)S(1)} collective-permute-done((bf16[128,2048]{1,0:T(8,128)(2,1)}, bf16[128,2048]{1,0:T(8,128)(2,1)S(1)}, u32[]{:S(2)}, u32[]{:S(2)}) %collective-permute-start) | collective-permute-done | bytes 524320 | tf_op jit(solution)/shard_map/ppermute | solution.py:30
  18.0 3.3 %collective-permute-start.2 = (bf16[128,2048]{1,0:T(8,128)(2,1)S(1)}, bf16[128,2048]{1,0:T(8,128)(2,1)}, u32[]{:S(2)}, u32[]{:S(2)}) collective-permute-start(bf16[128,2048]{1,0:T(8,128)(2,1)S(1)} %collective-permute-done.refs_1_.refs_6_.refs_10_), channel_id=1, source_target_pairs={{0,16},{4,20},{8,0},{12,4},{16,24},{20,28},{24,8},{28,12},{1,17},{... | collective-permute-start | bytes 1572872 | tf_op jit(solution)/shard_map/ppermute | solution.py:30
  21.3 1.5 %collective-permute-start.4 = (f32[1,128]{1,0:T(1,128)S(1)}, f32[1,128]{1,0:T(1,128)S(1)}, u32[]{:S(2)}, u32[]{:S(2)}) collective-permute-start(f32[1,128]{1,0:T(1,128)S(1)} %compare_select_fusion.1), channel_id=1, source_target_pairs={{0,4},{4,0},{8,12},{12,8},{16,20},{20,16},{24,28},{28,24},{1,5},{5... | collective-permute-start | bytes 1544 | tf_op jit(solution)/shard_map/ppermute | solution.py:23
  22.8 7.2 %collective-permute-done.4 = f32[1,128]{1,0:T(1,128)S(1)} collective-permute-done((f32[1,128]{1,0:T(1,128)S(1)}, f32[1,128]{1,0:T(1,128)S(1)}, u32[]{:S(2)}, u32[]{:S(2)}) %collective-permute-start.4) | collective-permute-done | bytes 544 | tf_op jit(solution)/shard_map/ppermute | solution.py:23
  31.0 1.5 %collective-permute-start.6 = (bf16[128,2048]{1,0:T(8,128)(2,1)}, bf16[128,2048]{1,0:T(8,128)(2,1)S(1)}, u32[]{:S(2)}, u32[]{:S(2)}) collective-permute-start(bf16[128,2048]{1,0:T(8,128)(2,1)} %collective-permute-done.2.refs_3_.refs_8_.refs_12_), channel_id=1, source_target_pairs={{0,4},{4,0},{8,12},{12,8},{16,20},{20,16},{24,28},{28,24},{1,5},{5... | collective-permute-start | bytes 1572872 | tf_op jit(solution)/shard_map/ppermute | solution.py:23
  32.5 3.5 %collective-permute-start.5 = (bf16[128,2048]{1,0:T(8,128)(2,1)}, bf16[128,2048]{1,0:T(8,128)(2,1)S(1)}, u32[]{:S(2)}, u32[]{:S(2)}) collective-permute-start(bf16[128,2048]{1,0:T(8,128)(2,1)} %collective-permute-done.2.refs_3_.refs_8_.refs_12_), channel_id=1, source_target_pairs={{0,16},{4,20},{8,0},{12,4},{16,24},{20,28},{24,8},{28,12},{1,17},{... | collective-permute-start | bytes 1572872 | tf_op jit(solution)/shard_map/ppermute | solution.py:30
  36.0 7.2 %shard_map.156 = (f32[2048,128]{1,0:T(8,128)}, f32[2048,128]{1,0:T(8,128)}) custom-call(bf16[2,128,2048]{2,1,0:T(8,128)(2,1)} %bitcast.98, bf16[2,128,2048]{2,1,0:T(8,128)(2,1)} %bitcast.94, bf16[2,128,2048]{2,1,0:T(8,128)(2,1)} %bitcast.95, bf16[128,2048]{1,0:T(8,128)(2,1)} %bitcast.103, bf16[128,2048]{1,0:T(8,128)(2,1)} %copy-done.6, ...), custom_call_target="tpu_custom_call" | custom-call | flops 805306368 | bytes 4194304 | tf_op jit(solution)/shard_map/pallas_call | solution.py:161
  43.1 1.7 %collective-permute-done.8 = f32[1,128]{1,0:T(1,128)S(1)} collective-permute-done((f32[1,128]{1,0:T(1,128)S(1)}, f32[1,128]{1,0:T(1,128)S(1)}, u32[]{:S(2)}, u32[]{:S(2)}) %collective-permute-start.8) | collective-permute-done | bytes 544 | tf_op jit(solution)/shard_map/ppermute | solution.py:23
  44.8 3.2 %collective-permute-start.9 = (f32[1,128]{1,0:T(1,128)S(1)}, f32[1,128]{1,0:T(1,128)S(1)}, u32[]{:S(2)}, u32[]{:S(2)}) collective-permute-start(f32[1,128]{1,0:T(1,128)S(1)} %add.68), channel_id=1, source_target_pairs={{0,16},{4,20},{8,24},{12,28},{16,0},{20,4},{24,8},{28,12},{1,17},{... | collective-permute-start | bytes 1544 | tf_op jit(solution)/shard_map/ppermute | solution.py:23
  49.0 3.1 %constant_dynamic-slice_fusion = (bf16[256,1152]{1,0:T(8,128)(2,1)}, bf16[256,1152]{1,0:T(8,128)(2,1)}, bf16[256,1152]{1,0:T(8,128)(2,1)}, bf16[256,1152]{1,0:T(8,128)(2,1)}) fusion(bf16[256,4608]{1,0:T(8,128)(2,1)} %bitcast.107, s32[]{:T(128)S(6)} %select_n.56, s32[]{:T(128)S(6)} %select_n.51, bf16[256,4608]{1,0:T(8,128)(2,1)} %bitcast.110), kind=kLoop, calls=%fused_computation.53 | loop fusion | bytes 4718600 | tf_op jit(solution)/shard_map/dynamic_slice | solution.py:263
  52.1 2.7 %collective-permute-done.11.refs_3_.refs_7_.refs_8_.refs_17_ = bf16[64,2048]{1,0:T(8,128)(2,1)S(1)} collective-permute-done((bf16[64,2048]{1,0:T(8,128)(2,1)S(1)}, bf16[64,2048]{1,0:T(8,128)(2,1)S(1)}, u32[]{:S(2)}, u32[]{:S(2)}) %collective-permute-start.11) | collective-permute-done | bytes 262176 | tf_op jit(solution)/shard_map/ppermute | solution.py:30
  56.1 4.7 %shard_map.157.refs_1_ = bf16[256,1024]{1,0:T(8,128)(2,1)} custom-call(bf16[2,128,2048]{2,1,0:T(8,128)(2,1)} %bitcast.99, f32[2048,128]{1,0:T(8,128)} %get-tuple-element.58.numerator_ref, f32[2048,128]{1,0:T(8,128)} %get-tuple-element.59.total_ref, bf16[128,2048]{1,0:T(8,128)(2,1)} %copy-done.4, bf16[128,2048]{1,0:T(8,128)(2,1)} %copy-done.3, ...), custom_call_target="tpu_custom_call" | custom-call | flops 402653184 | bytes 4194304 | tf_op jit(solution)/shard_map/pallas_call | solution.py:161
  61.3 1.2 %collective-permute-start.13 = (bf16[256,1024]{1,0:T(8,128)(2,1)}, bf16[256,1024]{1,0:T(8,128)(2,1)}, u32[]{:S(2)}, u32[]{:S(2)}) collective-permute-start(bf16[256,1024]{1,0:T(8,128)(2,1)} %shard_map.157.refs_1_), channel_id=1, source_target_pairs={{0,2},{1,3},{2,0},{3,1},{4,6},{5,7},{6,4},{7,5},{8,10},{9,11},{10,... | collective-permute-start | bytes 1572872 | tf_op jit(solution)/shard_map/ppermute | solution.py:23
  64.6 7.6 %shard_map.158.refs_2_ = bf16[256,1024]{1,0:T(8,128)(2,1)} custom-call(bf16[2,128,2048]{2,1,0:T(8,128)(2,1)} %bitcast.100, bf16[2,128,2048]{2,1,0:T(8,128)(2,1)} %bitcast.96, bf16[2,128,2048]{2,1,0:T(8,128)(2,1)} %bitcast.97, bf16[128,2048]{1,0:T(8,128)(2,1)} %bitcast.105, bf16[128,2048]{1,0:T(8,128)(2,1)} %copy-done.6, bf16[128,2048]{1,0:T(8,128)(2,1)} %copy-done.5, ...), custom_call_target="tpu_custom_call" | custom-call | flops 1207959552 | bytes 4194304 | tf_op jit(solution)/shard_map/pallas_call | solution.py:161
  72.3 3.8 %collective-permute-done.13.refs_1_ = bf16[256,1024]{1,0:T(8,128)(2,1)} collective-permute-done((bf16[256,1024]{1,0:T(8,128)(2,1)}, bf16[256,1024]{1,0:T(8,128)(2,1)}, u32[]{:S(2)}, u32[]{:S(2)}) %collective-permute-start.13) | collective-permute-done | bytes 524320 | tf_op jit(solution)/shard_map/ppermute | solution.py:23
  76.2 1.6 %collective-permute-start.20 = (bf16[256,1024]{1,0:T(8,128)(2,1)}, bf16[256,1024]{1,0:T(8,128)(2,1)S(1)}, u32[]{:S(2)}, u32[]{:S(2)}) collective-permute-start(bf16[256,1024]{1,0:T(8,128)(2,1)} %shard_map.158.refs_2_), channel_id=1, source_target_pairs={{0,2},{1,3},{2,0},{3,1},{4,6},{5,7},{6,4},{7,5},{8,10},{9,11},{10,... | collective-permute-start | bytes 1572872 | tf_op jit(solution)/shard_map/ppermute | solution.py:23
  78.0 1.3 %pad_maximum_fusion.2.refs_0_ = bf16[512,1152]{1,0:T(8,128)(2,1)S(1)} fusion(bf16[256,1152]{1,0:T(8,128)(2,1)} %get-tuple-element.87, bf16[256,1152]{1,0:T(8,128)(2,1)} %get-tuple-element.106), kind=kLoop, calls=%fused_computation.2 | loop fusion | flops 2359296 | bytes 2359296 | tf_op jit(solution)/shard_map/concatenate | solution.py:262
  79.9 1.5 %collective-permute-start.19 = (f32[7,128]{1,0:T(8,128)S(1)}, f32[7,128]{1,0:T(8,128)S(1)}, u32[]{:S(2)}, u32[]{:S(2)}) collective-permute-start(f32[7,128]{1,0:T(8,128)S(1)} %collective-permute-done.17), channel_id=1, source_target_pairs={{0,2},{1,3},{2,0},{3,1},{4,6},{5,7},{6,4},{7,5},{8,10},{9,11},{10,... | collective-permute-start | bytes 10760 | tf_op jit(solution)/shard_map/ppermute | solution.py:23
  81.5 2.3 %copy-done = bf16[2048,1152]{1,0:T(8,128)(2,1)S(1)} copy-done((bf16[2048,1152]{1,0:T(8,128)(2,1)S(1)}, bf16[2048,1152]{1,0:T(8,128)(2,1)}, u32[]{:S(2)}) %copy-start) | copy-done | bytes 4718616
  83.8 4.8 %shard_map.159 = f32[2,8,256]{2,1,0:T(8,128)S(1)} custom-call(bf16[2048,1152]{1,0:T(8,128)(2,1)S(1)} %copy-done, f32[2,1152]{1,0:T(2,128)S(1)} %fusion.gain_ref, bf16[512,1152]{1,0:T(8,128)(2,1)S(1)} %pad_maximum_fusion.2.refs_0_, bf16[256,1024]{1,0:T(8,128)(2,1)S(1)} %copy-done.2, bf16[256,1024]{1,0:T(8,128)(2,1)S(1)} %copy-done.1, ...), custom_call_target="tpu_custom_call" | custom-call | flops 2415919104 | bytes 8388608 | tf_op jit(solution)/shard_map/pallas_call | solution.py:216
  88.6 2.2 %collective-permute-done.18 = f32[7,128]{1,0:T(8,128)S(1)} collective-permute-done((f32[7,128]{1,0:T(8,128)S(1)}, f32[7,128]{1,0:T(8,128)S(1)}, u32[]{:S(2)}, u32[]{:S(2)}) %collective-permute-start.18) | collective-permute-done | bytes 3616 | tf_op jit(solution)/shard_map/ppermute | solution.py:23
  90.9 1.9 %collective-permute-done.22.refs_5_ = bf16[256,1024]{1,0:T(8,128)(2,1)S(1)} collective-permute-done((bf16[256,1024]{1,0:T(8,128)(2,1)S(1)}, bf16[256,1024]{1,0:T(8,128)(2,1)S(1)}, u32[]{:S(2)}, u32[]{:S(2)}) %collective-permute-start.22) | collective-permute-done | bytes 524320 | tf_op jit(solution)/shard_map/ppermute | solution.py:23
  92.8 4.8 %shard_map.160 = f32[2,8,256]{2,1,0:T(8,128)S(1)} custom-call(bf16[2048,1152]{1,0:T(8,128)(2,1)S(1)} %copy-done, f32[2,1152]{1,0:T(2,128)S(1)} %fusion.gain_ref, bf16[512,1152]{1,0:T(8,128)(2,1)S(1)} %collective-permute-done.7.refs_0_, bf16[256,1024]{1,0:T(8,128)(2,1)} %collective-permute-done.13.refs_1_, ...), custom_call_target="tpu_custom_call" | custom-call | flops 2415919104 | bytes 8388608 | tf_op jit(solution)/shard_map/pallas_call | solution.py:216
  98.8 1.6 %collective-permute-start.24 = (f32[4,8,256]{2,1,0:T(8,128)S(1)}, f32[4,8,256]{2,1,0:T(8,128)S(1)}, u32[]{:S(2)}, u32[]{:S(2)}) collective-permute-start(f32[4,8,256]{2,1,0:T(8,128)S(1)} %maximum_add_fusion), channel_id=1, source_target_pairs={{0,2},{1,3},{2,0},{3,1},{4,6},{5,7},{6,4},{7,5},{8,10},{9,11},{10,... | collective-permute-start | bytes 98312 | tf_op jit(solution)/shard_map/ppermute | solution.py:23
  100.6 2.2 %collective-permute-done.24 = f32[4,8,256]{2,1,0:T(8,128)S(1)} collective-permute-done((f32[4,8,256]{2,1,0:T(8,128)S(1)}, f32[4,8,256]{2,1,0:T(8,128)S(1)}, u32[]{:S(2)}, u32[]{:S(2)}) %collective-permute-start.24) | collective-permute-done | bytes 32800 | tf_op jit(solution)/shard_map/ppermute | solution.py:23
  103.5 3.0 %collective-permute-done.25 = f32[1,128]{1,0:T(1,128)S(1)} collective-permute-done((f32[1,128]{1,0:T(1,128)S(1)}, f32[1,128]{1,0:T(1,128)S(1)}, u32[]{:S(2)}, u32[]{:S(2)}) %collective-permute-start.25) | collective-permute-done | bytes 544 | tf_op jit(solution)/shard_map/ppermute | solution.py:23
  106.6 3.5 %collective-permute-done.26 = f32[1,128]{1,0:T(1,128)S(1)} collective-permute-done((f32[1,128]{1,0:T(1,128)S(1)}, f32[1,128]{1,0:T(1,128)S(1)}, u32[]{:S(2)}, u32[]{:S(2)}) %collective-permute-start.26) | collective-permute-done | bytes 544 | tf_op jit(solution)/shard_map/ppermute | solution.py:23
  110.1 1.6 %collective-permute-start.27 = (f32[1,128]{1,0:T(1,128)S(1)}, f32[1,128]{1,0:T(1,128)S(1)}, u32[]{:S(2)}, u32[]{:S(2)}) collective-permute-start(f32[1,128]{1,0:T(1,128)S(1)} %add.80), channel_id=1, source_target_pairs={{0,16},{4,20},{8,24},{12,28},{16,0},{20,4},{24,8},{28,12},{1,17},{... | collective-permute-start | bytes 1544 | tf_op jit(solution)/shard_map/ppermute | solution.py:23
  (113 shorter events, 18.7 us)
Async XLA Ops:
  0.6 15.1 %collective-permute-start.1 = (bf16[128,2048]{1,0:T(8,128)(2,1)}, bf16[128,2048]{1,0:T(8,128)(2,1)S(1)}, u32[]{:S(2)}, u32[]{:S(2)}) collective-permute-start(bf16[128,2048]{1,0:T(8,128)(2,1)} %bitcast.101), channel_id=1, source_target_pairs={{0,4},{4,0},{8,12},{12,8},{16,20},{20,16},{24,28},{28,24},{1,5},{5... | collective-permute-start | bytes 1572872 | tf_op jit(solution)/shard_map/ppermute | solution.py:23
  3.6 13.8 %collective-permute-start = (bf16[128,2048]{1,0:T(8,128)(2,1)}, bf16[128,2048]{1,0:T(8,128)(2,1)S(1)}, u32[]{:S(2)}, u32[]{:S(2)}) collective-permute-start(bf16[128,2048]{1,0:T(8,128)(2,1)} %bitcast.102), channel_id=1, source_target_pairs={{0,16},{4,20},{8,0},{12,4},{16,24},{20,28},{24,8},{28,12},{1,17},{... | collective-permute-start | bytes 1572872 | tf_op jit(solution)/shard_map/ppermute | solution.py:30
  9.5 35.3 %collective-permute-start.7 = (bf16[512,1152]{1,0:T(8,128)(2,1)}, bf16[512,1152]{1,0:T(8,128)(2,1)S(1)}, u32[]{:S(2)}, u32[]{:S(2)}) collective-permute-start(bf16[512,1152]{1,0:T(8,128)(2,1)} %pad_maximum_fusion.1), channel_id=1, source_target_pairs={{0,2},{1,3},{2,0},{3,1},{4,6},{5,7},{6,4},{7,5},{8,10},{9,11},{10,... | collective-permute-start | bytes 3538952 | tf_op jit(solution)/shard_map/ppermute | solution.py:23
  17.4 12.6 %copy-start.6 = (bf16[128,2048]{1,0:T(8,128)(2,1)}, bf16[128,2048]{1,0:T(8,128)(2,1)S(1)}, u32[]{:S(2)}) copy-start(bf16[128,2048]{1,0:T(8,128)(2,1)S(1)} %collective-permute-done.refs_1_.refs_6_.refs_10_) | copy-start | bytes 1572868
  17.4 12.5 %collective-permute-start.3 = (bf16[128,2048]{1,0:T(8,128)(2,1)S(1)}, bf16[128,2048]{1,0:T(8,128)(2,1)S(1)}, u32[]{:S(2)}, u32[]{:S(2)}) collective-permute-start(bf16[128,2048]{1,0:T(8,128)(2,1)S(1)} %collective-permute-done.refs_1_.refs_6_.refs_10_), channel_id=1, source_target_pairs={{0,4},{4,0},{8,12},{12,8},{16,20},{20,16},{24,28},{28,24},{1,5},{5... | collective-permute-start | bytes 1572872 | tf_op jit(solution)/shard_map/ppermute | solution.py:23
  18.0 13.0 %collective-permute-start.2 = (bf16[128,2048]{1,0:T(8,128)(2,1)S(1)}, bf16[128,2048]{1,0:T(8,128)(2,1)}, u32[]{:S(2)}, u32[]{:S(2)}) collective-permute-start(bf16[128,2048]{1,0:T(8,128)(2,1)S(1)} %collective-permute-done.refs_1_.refs_6_.refs_10_), channel_id=1, source_target_pairs={{0,16},{4,20},{8,0},{12,4},{16,24},{20,28},{24,8},{28,12},{1,17},{... | collective-permute-start | bytes 1572872 | tf_op jit(solution)/shard_map/ppermute | solution.py:30
  21.3 40.0 %collective-permute-start.12 = (bf16[512,1152]{1,0:T(8,128)(2,1)}, bf16[512,1152]{1,0:T(8,128)(2,1)S(1)}, u32[]{:S(2)}, u32[]{:S(2)}) collective-permute-start(bf16[512,1152]{1,0:T(8,128)(2,1)} %pad_maximum_fusion), channel_id=1, source_target_pairs={{0,3},{1,2},{2,1},{3,0},{4,7},{5,6},{6,5},{7,4},{8,11},{9,10},{10,... | collective-permute-start | bytes 3538952 | tf_op jit(solution)/shard_map/ppermute | solution.py:23
  21.3 8.7 %collective-permute-start.4 = (f32[1,128]{1,0:T(1,128)S(1)}, f32[1,128]{1,0:T(1,128)S(1)}, u32[]{:S(2)}, u32[]{:S(2)}) collective-permute-start(f32[1,128]{1,0:T(1,128)S(1)} %compare_select_fusion.1), channel_id=1, source_target_pairs={{0,4},{4,0},{8,12},{12,8},{16,20},{20,16},{24,28},{28,24},{1,5},{5... | collective-permute-start | bytes 1544 | tf_op jit(solution)/shard_map/ppermute | solution.py:23
  31.0 13.8 %collective-permute-start.6 = (bf16[128,2048]{1,0:T(8,128)(2,1)}, bf16[128,2048]{1,0:T(8,128)(2,1)S(1)}, u32[]{:S(2)}, u32[]{:S(2)}) collective-permute-start(bf16[128,2048]{1,0:T(8,128)(2,1)} %collective-permute-done.2.refs_3_.refs_8_.refs_12_), channel_id=1, source_target_pairs={{0,4},{4,0},{8,12},{12,8},{16,20},{20,16},{24,28},{28,24},{1,5},{5... | collective-permute-start | bytes 1572872 | tf_op jit(solution)/shard_map/ppermute | solution.py:23
  32.5 12.3 %collective-permute-start.5 = (bf16[128,2048]{1,0:T(8,128)(2,1)}, bf16[128,2048]{1,0:T(8,128)(2,1)S(1)}, u32[]{:S(2)}, u32[]{:S(2)}) collective-permute-start(bf16[128,2048]{1,0:T(8,128)(2,1)} %collective-permute-done.2.refs_3_.refs_8_.refs_12_), channel_id=1, source_target_pairs={{0,16},{4,20},{8,0},{12,4},{16,24},{20,28},{24,8},{28,12},{1,17},{... | collective-permute-start | bytes 1572872 | tf_op jit(solution)/shard_map/ppermute | solution.py:30
  36.0 8.8 %collective-permute-start.8 = (f32[1,128]{1,0:T(1,128)S(1)}, f32[1,128]{1,0:T(1,128)S(1)}, u32[]{:S(2)}, u32[]{:S(2)}) collective-permute-start(f32[1,128]{1,0:T(1,128)S(1)} %add.66), channel_id=1, source_target_pairs={{0,8},{4,12},{8,0},{12,4},{16,24},{20,28},{24,16},{28,20},{1,9},{5... | collective-permute-start | bytes 1544 | tf_op jit(solution)/shard_map/ppermute | solution.py:23
  44.8 7.2 %collective-permute-start.9 = (f32[1,128]{1,0:T(1,128)S(1)}, f32[1,128]{1,0:T(1,128)S(1)}, u32[]{:S(2)}, u32[]{:S(2)}) collective-permute-start(f32[1,128]{1,0:T(1,128)S(1)} %add.68), channel_id=1, source_target_pairs={{0,16},{4,20},{8,24},{12,28},{16,0},{20,4},{24,8},{28,12},{1,17},{... | collective-permute-start | bytes 1544 | tf_op jit(solution)/shard_map/ppermute | solution.py:23
  48.1 6.6 %collective-permute-start.11 = (bf16[64,2048]{1,0:T(8,128)(2,1)S(1)}, bf16[64,2048]{1,0:T(8,128)(2,1)S(1)}, u32[]{:S(2)}, u32[]{:S(2)}) collective-permute-start(bf16[64,2048]{1,0:T(8,128)(2,1)S(1)} %slice.83), channel_id=1, source_target_pairs={{0,16},{4,20},{8,0},{12,4},{16,24},{20,28},{24,8},{28,12},{1,17},{... | collective-permute-start | bytes 786440 | tf_op jit(solution)/shard_map/ppermute | solution.py:30
  48.4 6.4 %collective-permute-start.10 = (bf16[64,2048]{1,0:T(8,128)(2,1)S(1)}, bf16[64,2048]{1,0:T(8,128)(2,1)S(1)}, u32[]{:S(2)}, u32[]{:S(2)}) collective-permute-start(bf16[64,2048]{1,0:T(8,128)(2,1)S(1)} %slice.82), channel_id=1, source_target_pairs={{0,4},{4,0},{8,12},{12,8},{16,20},{20,16},{24,28},{28,24},{1,5},{5... | collective-permute-start | bytes 786440 | tf_op jit(solution)/shard_map/ppermute | solution.py:23
  61.3 14.8 %collective-permute-start.13 = (bf16[256,1024]{1,0:T(8,128)(2,1)}, bf16[256,1024]{1,0:T(8,128)(2,1)}, u32[]{:S(2)}, u32[]{:S(2)}) collective-permute-start(bf16[256,1024]{1,0:T(8,128)(2,1)} %shard_map.157.refs_1_), channel_id=1, source_target_pairs={{0,2},{1,3},{2,0},{3,1},{4,6},{5,7},{6,4},{7,5},{8,10},{9,11},{10,... | collective-permute-start | bytes 1572872 | tf_op jit(solution)/shard_map/ppermute | solution.py:23
  63.6 17.8 %collective-permute-start.14 = (bf16[512,1152]{1,0:T(8,128)(2,1)}, bf16[512,1152]{1,0:T(8,128)(2,1)S(1)}, u32[]{:S(2)}, u32[]{:S(2)}) collective-permute-start(bf16[512,1152]{1,0:T(8,128)(2,1)} %pad_maximum_fusion.3), channel_id=1, source_target_pairs={{0,1},{1,0},{2,3},{3,2},{4,5},{5,4},{6,7},{7,6},{8,9},{9,8},{10,11... | collective-permute-start | bytes 3538952 | tf_op jit(solution)/shard_map/ppermute | solution.py:23
  64.5 13.3 %copy-start.15 = (f32[1,2,128]{2,1,0:T(2,128)S(1)}, f32[1,2,128]{2,1,0:T(2,128)}, u32[]{:S(2)}) copy-start(f32[1,2,128]{2,1,0:T(2,128)} %param.23) | copy-start | bytes 3076
  64.5 13.3 %copy-start.16 = (f32[1,2,128]{2,1,0:T(2,128)S(1)}, f32[1,2,128]{2,1,0:T(2,128)}, u32[]{:S(2)}) copy-start(f32[1,2,128]{2,1,0:T(2,128)} %param.22) | copy-start | bytes 3076
  64.5 13.3 %copy-start.17 = (f32[1,2,128]{2,1,0:T(2,128)S(1)}, f32[1,2,128]{2,1,0:T(2,128)}, u32[]{:S(2)}) copy-start(f32[1,2,128]{2,1,0:T(2,128)} %param.21) | copy-start | bytes 3076
  64.5 15.4 %collective-permute-start.15 = (bf16[256,1024]{1,0:T(8,128)(2,1)S(1)}, bf16[256,1024]{1,0:T(8,128)(2,1)}, u32[]{:S(2)}, u32[]{:S(2)}) collective-permute-start(bf16[256,1024]{1,0:T(8,128)(2,1)S(1)} %copy-done.2), channel_id=1, source_target_pairs={{0,1},{1,0},{2,3},{3,2},{4,5},{5,4},{6,7},{7,6},{8,9},{9,8},{10,11... | collective-permute-start | bytes 1572872 | tf_op jit(solution)/shard_map/ppermute | solution.py:23
  76.1 5.4 %collective-permute-start.16 = (bf16[256,1024]{1,0:T(8,128)(2,1)}, bf16[256,1024]{1,0:T(8,128)(2,1)S(1)}, u32[]{:S(2)}, u32[]{:S(2)}) collective-permute-start(bf16[256,1024]{1,0:T(8,128)(2,1)} %shard_map.158.refs_2_), channel_id=1, source_target_pairs={{0,1},{1,0},{2,3},{3,2},{4,5},{5,4},{6,7},{7,6},{8,9},{9,8},{10,11... | collective-permute-start | bytes 1572872 | tf_op jit(solution)/shard_map/ppermute | solution.py:23
  76.2 14.7 %collective-permute-start.20 = (bf16[256,1024]{1,0:T(8,128)(2,1)}, bf16[256,1024]{1,0:T(8,128)(2,1)S(1)}, u32[]{:S(2)}, u32[]{:S(2)}) collective-permute-start(bf16[256,1024]{1,0:T(8,128)(2,1)} %shard_map.158.refs_2_), channel_id=1, source_target_pairs={{0,2},{1,3},{2,0},{3,1},{4,6},{5,7},{6,4},{7,5},{8,10},{9,11},{10,... | collective-permute-start | bytes 1572872 | tf_op jit(solution)/shard_map/ppermute | solution.py:23
  77.8 1.6 %collective-permute-start.17 = (f32[7,128]{1,0:T(8,128)S(1)}, f32[7,128]{1,0:T(8,128)S(1)}, u32[]{:S(2)}, u32[]{:S(2)}) collective-permute-start(f32[7,128]{1,0:T(8,128)S(1)} %select_maximum_fusion), channel_id=1, source_target_pairs={{0,1},{1,0},{2,3},{3,2},{4,5},{5,4},{6,7},{7,6},{8,9},{9,8},{10,11... | collective-permute-start | bytes 10760 | tf_op jit(solution)/shard_map/ppermute | solution.py:23
  79.4 11.5 %collective-permute-start.18 = (f32[7,128]{1,0:T(8,128)S(1)}, f32[7,128]{1,0:T(8,128)S(1)}, u32[]{:S(2)}, u32[]{:S(2)}) collective-permute-start(f32[7,128]{1,0:T(8,128)S(1)} %select_maximum_fusion), channel_id=1, source_target_pairs={{0,2},{1,3},{2,0},{3,1},{4,6},{5,7},{6,4},{7,5},{8,10},{9,11},{10,... | collective-permute-start | bytes 10760 | tf_op jit(solution)/shard_map/ppermute | solution.py:23
  79.9 11.0 %collective-permute-start.19 = (f32[7,128]{1,0:T(8,128)S(1)}, f32[7,128]{1,0:T(8,128)S(1)}, u32[]{:S(2)}, u32[]{:S(2)}) collective-permute-start(f32[7,128]{1,0:T(8,128)S(1)} %collective-permute-done.17), channel_id=1, source_target_pairs={{0,2},{1,3},{2,0},{3,1},{4,6},{5,7},{6,4},{7,5},{8,10},{9,11},{10,... | collective-permute-start | bytes 10760 | tf_op jit(solution)/shard_map/ppermute | solution.py:23
  81.5 9.4 %collective-permute-start.21 = (bf16[256,1024]{1,0:T(8,128)(2,1)}, bf16[256,1024]{1,0:T(8,128)(2,1)S(1)}, u32[]{:S(2)}, u32[]{:S(2)}) collective-permute-start(bf16[256,1024]{1,0:T(8,128)(2,1)} %collective-permute-done.13.refs_1_), channel_id=1, source_target_pairs={{0,1},{1,0},{2,3},{3,2},{4,5},{5,4},{6,7},{7,6},{8,9},{9,8},{10,11... | collective-permute-start | bytes 1572872 | tf_op jit(solution)/shard_map/ppermute | solution.py:23
  90.9 1.9 %collective-permute-start.22 = (bf16[256,1024]{1,0:T(8,128)(2,1)S(1)}, bf16[256,1024]{1,0:T(8,128)(2,1)S(1)}, u32[]{:S(2)}, u32[]{:S(2)}) collective-permute-start(bf16[256,1024]{1,0:T(8,128)(2,1)S(1)} %collective-permute-done.20.refs_2_), channel_id=1, source_target_pairs={{0,1},{1,0},{2,3},{3,2},{4,5},{5,4},{6,7},{7,6},{8,9},{9,8},{10,11... | collective-permute-start | bytes 1572872 | tf_op jit(solution)/shard_map/ppermute | solution.py:23
  97.6 1.3 %collective-permute-start.23 = (f32[4,8,256]{2,1,0:T(8,128)S(1)}, f32[4,8,256]{2,1,0:T(8,128)S(1)}, u32[]{:S(2)}, u32[]{:S(2)}) collective-permute-start(f32[4,8,256]{2,1,0:T(8,128)S(1)} %pad_maximum_fusion.4), channel_id=1, source_target_pairs={{0,1},{1,0},{2,3},{3,2},{4,5},{5,4},{6,7},{7,6},{8,9},{9,8},{10,11... | collective-permute-start | bytes 98312 | tf_op jit(solution)/shard_map/ppermute | solution.py:23
  98.8 4.0 %collective-permute-start.24 = (f32[4,8,256]{2,1,0:T(8,128)S(1)}, f32[4,8,256]{2,1,0:T(8,128)S(1)}, u32[]{:S(2)}, u32[]{:S(2)}) collective-permute-start(f32[4,8,256]{2,1,0:T(8,128)S(1)} %maximum_add_fusion), channel_id=1, source_target_pairs={{0,2},{1,3},{2,0},{3,1},{4,6},{5,7},{6,4},{7,5},{8,10},{9,11},{10,... | collective-permute-start | bytes 98312 | tf_op jit(solution)/shard_map/ppermute | solution.py:23
  102.9 3.6 %collective-permute-start.25 = (f32[1,128]{1,0:T(1,128)S(1)}, f32[1,128]{1,0:T(1,128)S(1)}, u32[]{:S(2)}, u32[]{:S(2)}) collective-permute-start(f32[1,128]{1,0:T(1,128)S(1)} %bitcast.124), channel_id=1, source_target_pairs={{0,4},{4,0},{8,12},{12,8},{16,20},{20,16},{24,28},{28,24},{1,5},{5... | collective-permute-start | bytes 1544 | tf_op jit(solution)/shard_map/ppermute | solution.py:23
  106.6 3.5 %collective-permute-start.26 = (f32[1,128]{1,0:T(1,128)S(1)}, f32[1,128]{1,0:T(1,128)S(1)}, u32[]{:S(2)}, u32[]{:S(2)}) collective-permute-start(f32[1,128]{1,0:T(1,128)S(1)} %bitcast_add_fusion), channel_id=1, source_target_pairs={{0,8},{4,12},{8,0},{12,4},{16,24},{20,28},{24,16},{28,20},{1,9},{5... | collective-permute-start | bytes 1544 | tf_op jit(solution)/shard_map/ppermute | solution.py:23
  110.1 4.4 %collective-permute-start.27 = (f32[1,128]{1,0:T(1,128)S(1)}, f32[1,128]{1,0:T(1,128)S(1)}, u32[]{:S(2)}, u32[]{:S(2)}) collective-permute-start(f32[1,128]{1,0:T(1,128)S(1)} %add.80), channel_id=1, source_target_pairs={{0,16},{4,20},{8,24},{12,28},{16,0},{20,4},{24,8},{28,12},{1,17},{... | collective-permute-start | bytes 1544 | tf_op jit(solution)/shard_map/ppermute | solution.py:23
  (16 other events, 72.9 us)

commit v6 on v5

--- a/solution.py
+++ b/solution.py
@@ -164,7 +164,7 @@
         in_specs=in_specs + block_specs(blocks, first),
         out_specs=out_specs,
         out_shape=out_shape,
-        compiler_params=pltpu.CompilerParams(vmem_limit_bytes=60 * 1024 * 1024),
+        compiler_params=pltpu.CompilerParams(vmem_limit_bytes=(24 if state else 60) * 1024 * 1024),
         cost_estimate=attention_cost(
             tokens, per_group, sum(block.shape[0] for block in blocks) + (0 if state else length)
         ),
@@ -283,8 +283,7 @@
             bit *= 2
         if step == rounds - 1:
             final_blocks = [block, crossed]
-            final_blocks.append(swap(block[: rows // 2], "dp", 1))
-            final_blocks.append(around(crossed[rows // 2 :], "dp"))
+            final_blocks.append(swap(block, "dp", 1))
             sums, state = lax.optimization_barrier((sums, state))
             break
         pieces.update({key: cut(key) for key in later})
@@ -370,9 +369,11 @@
     totals = jnp.concatenate(parts, axis=0)
     bit = 1
     while bit < fsdp:
-        other = swap(totals, "fsdp", bit)
-        totals = totals + jnp.stack([other[k ^ bit] for k in range(fsdp)])
-        bit *= 2
+        steps = [bit, 2 * bit, 3 * bit] if 2 * bit < fsdp else [bit]
+        others = [(step, swap(totals, "fsdp", step)) for step in steps]
+        for step, other in others:
+            totals = totals + jnp.stack([other[k ^ step] for k in range(fsdp)])
+        bit *= 4
 
     totals = totals.reshape(fsdp, SUMS, responses, length)
     inverse = lax.rsqrt(totals[:, 0] / D + 1e-06)
@@ -400,8 +401,9 @@
     loss = jnp.sum(objective, axis=(0, 1))[None]
     bit = 1
     while bit < dp:
-        loss = loss + swap(loss, "dp", bit)
-        bit *= 2
+        steps = [bit, 2 * bit, 3 * bit] if 1 < bit and 2 * bit < dp else [bit]
+        loss = sum([swap(loss, "dp", step) for step in steps], loss)
+        bit *= 4 if len(steps) > 1 else 2
     batch_loss = jnp.sum(loss) / jnp.sum(group_count)
     return (log_ratio[:1], kl_terms[:1], objective[:1], batch_loss)
 

time: 118 us -> 115 us (0.975)
  Pallas kernels: 29.1 us -> 26.1 us
  local copies, waits for them, and re-layouts: 10.2 us -> 8.75 us
  other arithmetic: 8.98 us -> 7.66 us
  waiting for transfers between devices: 33.9 us -> 35.1 us
    ppermute x24 -> x26, waiting for transfers between devices: 28.7 us -> 32.4 us  [swap(): return lax.ppermute(value, axis, [(i, i ^ bit) for i in range(count)])]
    ppermute x4 -> x3, waiting for transfers between devices: 5.29 us -> 2.63 us  [around(): lax.ppermute(value, axis, [(i, after[i // 2] * 2 + i % 2) for i in range(...]
    pallas_call x3, Pallas kernels: 19.5 us -> 17.4 us  [attend(): pl.pallas_call(functools.partial(kernel, len(blocks)), grid=(per_group,),...]
    ppermute x24 -> x26, starting transfers between devices: 21.8 us -> 23.1 us  [swap(): return lax.ppermute(value, axis, [(i, i ^ bit) for i in range(count)])]
    concatenate x4, other arithmetic: 4.71 us -> 3.44 us  [cut(): jnp.concatenate([lax.dynamic_slice_in_dim(value, start, columns, 1) for v...]
    unnamed x40 -> x44, local copies, waits for them, and re-layouts: 4.29 us -> 3.45 us
    ppermute x4 -> x3, starting transfers between devices: 9.59 us -> 9.35 us  [around(): lax.ppermute(value, axis, [(i, after[i // 2] * 2 + i % 2) for i in range(...]
  transfers between devices with their start and end apart: 28 -> 29, of which waited for: 16 -> 13; matrix products, arithmetic and copies ran while one was open for 12% -> 11% of each run, Pallas kernels for 21% -> 19%
where the time goes in v6:
time: 115 us; the launch traced here: 114 us
  waiting for transfers between devices  35.1 us (31%)
  starting transfers between devices  32.4 us (28%)
  Pallas kernels  26.1 us (23%)
  local copies, waits for them, and re-layouts  8.75 us (8%)
  other arithmetic  7.66 us (7%)
  between operations  4.15 us (4%)
    ppermute x26, waiting for transfers between devices, swap(): return lax.ppermute(value, axis, [(i, i ^ bit) for i in range(count)])  32.4 us
    ppermute x26, starting transfers between devices, swap(): return lax.ppermute(value, axis, [(i, i ^ bit) for i in range(count)])  23.1 us
    pallas_call x3, Pallas kernels, attend(): pl.pallas_call(functools.partial(kernel, len(blocks)), grid=(per_group,),...  17.4 us
    ppermute x3, starting transfers between devices, around(): lax.ppermute(value, axis, [(i, after[i // 2] * 2 + i % 2) for i in range(...  9.35 us
    pallas_call x2, Pallas kernels, project(): pl.pallas_call(functools.partial(project_kernel, sources), out_shape=jax....  8.73 us
    dynamic_slice x3, local copies, waits for them, and re-layouts, cut(): lax.dynamic_slice_in_dim(value, start, columns, 1)  4.05 us
    unnamed x44, local copies, waits for them, and re-layouts  3.45 us
    concatenate x4, other arithmetic, cut(): jnp.concatenate([lax.dynamic_slice_in_dim(value, start, columns, 1) for v...  3.44 us
  transfers between devices with their start and end apart: 29, of which 13 were waited for; matrix products, arithmetic and copies ran while one was open for 11% of the time, Pallas kernels for 19%

profile of v6, /device:TPU:0, one launch (start us, length us, event | category | flops | bytes accessed | tf_op | source)
XLA Modules:
  0.0 114.2 jit_solution(16995293054333697419)
XLA Ops:
  0.6 3.0 %collective-permute-start.1 = (bf16[128,2048]{1,0:T(8,128)(2,1)}, bf16[128,2048]{1,0:T(8,128)(2,1)S(1)}, u32[]{:S(2)}, u32[]{:S(2)}) collective-permute-start(bf16[128,2048]{1,0:T(8,128)(2,1)} %bitcast.109), channel_id=1, source_target_pairs={{0,4},{4,0},{8,12},{12,8},{16,20},{20,16},{24,28},{28,24},{1,5},{5... | collective-permute-start | bytes 1572872 | tf_op jit(solution)/shard_map/ppermute | solution.py:23
  3.6 2.6 %collective-permute-start = (bf16[128,2048]{1,0:T(8,128)(2,1)}, bf16[128,2048]{1,0:T(8,128)(2,1)S(1)}, u32[]{:S(2)}, u32[]{:S(2)}) collective-permute-start(bf16[128,2048]{1,0:T(8,128)(2,1)} %bitcast.110), channel_id=1, source_target_pairs={{0,16},{4,20},{8,0},{12,4},{16,24},{20,28},{24,8},{28,12},{1,17},{... | collective-permute-start | bytes 1572872 | tf_op jit(solution)/shard_map/ppermute | solution.py:30
  6.2 1.3 %constant_dynamic-slice_fusion.5 = (bf16[256,1152]{1,0:T(8,128)(2,1)S(1)}, bf16[256,1152]{1,0:T(8,128)(2,1)S(1)}) fusion(bf16[256,4608]{1,0:T(8,128)(2,1)} %bitcast.117, s32[]{:T(128)S(6)} %select_n.55, s32[]{:T(128)S(6)} %select_n.52), kind=kLoop, calls=%fused_computation.71 | loop fusion | bytes 2359304 | tf_op jit(solution)/shard_map/dynamic_slice | solution.py:263
  8.8 1.5 %collective-permute-start.7 = (bf16[512,1152]{1,0:T(8,128)(2,1)}, bf16[512,1152]{1,0:T(8,128)(2,1)S(1)}, u32[]{:S(2)}, u32[]{:S(2)}) collective-permute-start(bf16[512,1152]{1,0:T(8,128)(2,1)} %pad_maximum_fusion.1), channel_id=1, source_target_pairs={{0,2},{1,3},{2,0},{3,1},{4,6},{5,7},{6,4},{7,5},{8,10},{9,11},{10,... | collective-permute-start | bytes 3538952 | tf_op jit(solution)/shard_map/ppermute | solution.py:23
  14.0 1.8 %collective-permute-done.1.refs_2_.refs_7_.refs_10_ = bf16[128,2048]{1,0:T(8,128)(2,1)S(1)} collective-permute-done((bf16[128,2048]{1,0:T(8,128)(2,1)}, bf16[128,2048]{1,0:T(8,128)(2,1)S(1)}, u32[]{:S(2)}, u32[]{:S(2)}) %collective-permute-start.1) | collective-permute-done | bytes 524320 | tf_op jit(solution)/shard_map/ppermute | solution.py:23
  15.8 1.7 %collective-permute-done.refs_1_.refs_6_.refs_9_ = bf16[128,2048]{1,0:T(8,128)(2,1)S(1)} collective-permute-done((bf16[128,2048]{1,0:T(8,128)(2,1)}, bf16[128,2048]{1,0:T(8,128)(2,1)S(1)}, u32[]{:S(2)}, u32[]{:S(2)}) %collective-permute-start) | collective-permute-done | bytes 524320 | tf_op jit(solution)/shard_map/ppermute | solution.py:30
  18.0 3.3 %collective-permute-start.2 = (bf16[128,2048]{1,0:T(8,128)(2,1)S(1)}, bf16[128,2048]{1,0:T(8,128)(2,1)}, u32[]{:S(2)}, u32[]{:S(2)}) collective-permute-start(bf16[128,2048]{1,0:T(8,128)(2,1)S(1)} %collective-permute-done.refs_1_.refs_6_.refs_9_), channel_id=1, source_target_pairs={{0,16},{4,20},{8,0},{12,4},{16,24},{20,28},{24,8},{28,12},{1,17},{... | collective-permute-start | bytes 1572872 | tf_op jit(solution)/shard_map/ppermute | solution.py:30
  21.3 1.5 %collective-permute-start.4 = (f32[1,128]{1,0:T(1,128)S(1)}, f32[1,128]{1,0:T(1,128)S(1)}, u32[]{:S(2)}, u32[]{:S(2)}) collective-permute-start(f32[1,128]{1,0:T(1,128)S(1)} %compare_select_fusion.1), channel_id=1, source_target_pairs={{0,4},{4,0},{8,12},{12,8},{16,20},{20,16},{24,28},{28,24},{1,5},{5... | collective-permute-start | bytes 1544 | tf_op jit(solution)/shard_map/ppermute | solution.py:23
  22.8 7.2 %collective-permute-done.4 = f32[1,128]{1,0:T(1,128)S(1)} collective-permute-done((f32[1,128]{1,0:T(1,128)S(1)}, f32[1,128]{1,0:T(1,128)S(1)}, u32[]{:S(2)}, u32[]{:S(2)}) %collective-permute-start.4) | collective-permute-done | bytes 544 | tf_op jit(solution)/shard_map/ppermute | solution.py:23
  31.0 1.5 %collective-permute-start.6 = (bf16[128,2048]{1,0:T(8,128)(2,1)}, bf16[128,2048]{1,0:T(8,128)(2,1)S(1)}, u32[]{:S(2)}, u32[]{:S(2)}) collective-permute-start(bf16[128,2048]{1,0:T(8,128)(2,1)} %collective-permute-done.2.refs_3_.refs_8_.refs_11_), channel_id=1, source_target_pairs={{0,4},{4,0},{8,12},{12,8},{16,20},{20,16},{24,28},{28,24},{1,5},{5... | collective-permute-start | bytes 1572872 | tf_op jit(solution)/shard_map/ppermute | solution.py:23
  32.5 3.5 %collective-permute-start.5 = (bf16[128,2048]{1,0:T(8,128)(2,1)}, bf16[128,2048]{1,0:T(8,128)(2,1)S(1)}, u32[]{:S(2)}, u32[]{:S(2)}) collective-permute-start(bf16[128,2048]{1,0:T(8,128)(2,1)} %collective-permute-done.2.refs_3_.refs_8_.refs_11_), channel_id=1, source_target_pairs={{0,16},{4,20},{8,0},{12,4},{16,24},{20,28},{24,8},{28,12},{1,17},{... | collective-permute-start | bytes 1572872 | tf_op jit(solution)/shard_map/ppermute | solution.py:30
  36.0 7.2 %shard_map.156 = (f32[2048,128]{1,0:T(8,128)}, f32[2048,128]{1,0:T(8,128)}) custom-call(bf16[2,128,2048]{2,1,0:T(8,128)(2,1)} %bitcast.100, bf16[2,128,2048]{2,1,0:T(8,128)(2,1)} %bitcast.105, bf16[2,128,2048]{2,1,0:T(8,128)(2,1)} %bitcast.106, bf16[128,2048]{1,0:T(8,128)(2,1)} %bitcast.111, bf16[128,2048]{1,0:T(8,128)(2,1)} %copy-done.11, ...), custom_call_target="tpu_custom_call" | custom-call | flops 805306368 | bytes 4194304 | tf_op jit(solution)/shard_map/pallas_call | solution.py:161
  43.2 1.6 %collective-permute-done.8 = f32[1,128]{1,0:T(1,128)S(1)} collective-permute-done((f32[1,128]{1,0:T(1,128)S(1)}, f32[1,128]{1,0:T(1,128)S(1)}, u32[]{:S(2)}, u32[]{:S(2)}) %collective-permute-start.8) | collective-permute-done | bytes 544 | tf_op jit(solution)/shard_map/ppermute | solution.py:23
  46.4 2.3 %collective-permute-start.9 = (f32[1,128]{1,0:T(1,128)S(1)}, f32[1,128]{1,0:T(1,128)S(1)}, u32[]{:S(2)}, u32[]{:S(2)}) collective-permute-start(f32[1,128]{1,0:T(1,128)S(1)} %add.73), channel_id=1, source_target_pairs={{0,16},{4,20},{8,24},{12,28},{16,0},{20,4},{24,8},{28,12},{1,17},{... | collective-permute-start | bytes 1544 | tf_op jit(solution)/shard_map/ppermute | solution.py:23
  48.7 2.6 %constant_dynamic-slice_fusion = (bf16[256,1152]{1,0:T(8,128)(2,1)S(1)}, bf16[256,1152]{1,0:T(8,128)(2,1)S(1)}, bf16[256,1152]{1,0:T(8,128)(2,1)}, bf16[256,1152]{1,0:T(8,128)(2,1)S(1)}) fusion(bf16[256,4608]{1,0:T(8,128)(2,1)} %bitcast.115, s32[]{:T(128)S(6)} %select_n.56, s32[]{:T(128)S(6)} %select_n.51, bf16[256,4608]{1,0:T(8,128)(2,1)} %bitcast.118), kind=kLoop, calls=%fused_computation.66 | loop fusion | bytes 4718600 | tf_op jit(solution)/shard_map/dynamic_slice | solution.py:263
  51.4 4.7 %collective-permute-done.10.refs_2_.refs_5_.refs_7_.refs_15_ = bf16[128,2048]{1,0:T(8,128)(2,1)S(1)} collective-permute-done((bf16[128,2048]{1,0:T(8,128)(2,1)S(1)}, bf16[128,2048]{1,0:T(8,128)(2,1)S(1)}, u32[]{:S(2)}, u32[]{:S(2)}) %collective-permute-start.10) | collective-permute-done | bytes 524320 | tf_op jit(solution)/shard_map/ppermute | solution.py:23
  56.1 2.5 %shard_map.157.refs_1_ = bf16[256,1024]{1,0:T(8,128)(2,1)S(1)} custom-call(bf16[2,128,2048]{2,1,0:T(8,128)(2,1)S(1)} %bitcast.102, f32[2048,128]{1,0:T(8,128)S(1)} %copy-done.8, f32[2048,128]{1,0:T(8,128)S(1)} %copy-done.9, bf16[128,2048]{1,0:T(8,128)(2,1)S(1)} %collective-permute-done.5.refs_0_.refs_3_.refs_5_.refs_13_, ...), custom_call_target="tpu_custom_call" | custom-call | flops 402653184 | bytes 4194304 | tf_op jit(solution)/shard_map/pallas_call | solution.py:161
  58.7 1.9 %collective-permute-done.11.refs_3_ = bf16[512,1152]{1,0:T(8,128)(2,1)} collective-permute-done((bf16[512,1152]{1,0:T(8,128)(2,1)}, bf16[512,1152]{1,0:T(8,128)(2,1)}, u32[]{:S(2)}, u32[]{:S(2)}) %collective-permute-start.11) | collective-permute-done | bytes 1179680 | tf_op jit(solution)/shard_map/ppermute | solution.py:23
  62.4 1.3 %collective-permute-start.13 = (bf16[512,1152]{1,0:T(8,128)(2,1)}, bf16[512,1152]{1,0:T(8,128)(2,1)S(1)}, u32[]{:S(2)}, u32[]{:S(2)}) collective-permute-start(bf16[512,1152]{1,0:T(8,128)(2,1)} %pad_maximum_fusion.3), channel_id=1, source_target_pairs={{0,1},{1,0},{2,3},{3,2},{4,5},{5,4},{6,7},{7,6},{8,9},{9,8},{10,11... | collective-permute-start | bytes 3538952 | tf_op jit(solution)/shard_map/ppermute | solution.py:23
  64.0 7.6 %shard_map.158.refs_2_ = bf16[256,1024]{1,0:T(8,128)(2,1)} custom-call(bf16[2,128,2048]{2,1,0:T(8,128)(2,1)} %bitcast.101, bf16[2,128,2048]{2,1,0:T(8,128)(2,1)} %bitcast.107, bf16[2,128,2048]{2,1,0:T(8,128)(2,1)} %bitcast.108, bf16[128,2048]{1,0:T(8,128)(2,1)} %bitcast.113, bf16[128,2048]{1,0:T(8,128)(2,1)} %copy-done.11, bf16[128,2048]{1,0:T(8,128)(2,1)} %copy-done.10, ...), custom_call_target="tpu_custom_call" | custom-call | flops 1207959552 | bytes 4194304 | tf_op jit(solution)/shard_map/pallas_call | solution.py:161
  71.7 3.5 %collective-permute-done.12.refs_1_ = bf16[256,1024]{1,0:T(8,128)(2,1)S(1)} collective-permute-done((bf16[256,1024]{1,0:T(8,128)(2,1)S(1)}, bf16[256,1024]{1,0:T(8,128)(2,1)S(1)}, u32[]{:S(2)}, u32[]{:S(2)}) %collective-permute-start.12) | collective-permute-done | bytes 524320 | tf_op jit(solution)/shard_map/ppermute | solution.py:23
  77.3 1.3 %collective-permute-start.17 = (f32[7,128]{1,0:T(8,128)S(1)}, f32[7,128]{1,0:T(8,128)S(1)}, u32[]{:S(2)}, u32[]{:S(2)}) collective-permute-start(f32[7,128]{1,0:T(8,128)S(1)} %select_maximum_fusion), channel_id=1, source_target_pairs={{0,2},{1,3},{2,0},{3,1},{4,6},{5,7},{6,4},{7,5},{8,10},{9,11},{10,... | collective-permute-start | bytes 10760 | tf_op jit(solution)/shard_map/ppermute | solution.py:23
  79.3 2.3 %copy-done = bf16[2048,1152]{1,0:T(8,128)(2,1)S(1)} copy-done((bf16[2048,1152]{1,0:T(8,128)(2,1)S(1)}, bf16[2048,1152]{1,0:T(8,128)(2,1)}, u32[]{:S(2)}) %copy-start) | copy-done | bytes 4718616
  81.7 3.8 %shard_map.159 = f32[2,8,256]{2,1,0:T(8,128)S(1)} custom-call(bf16[2048,1152]{1,0:T(8,128)(2,1)S(1)} %copy-done, f32[2,1152]{1,0:T(2,128)S(1)} %fusion.gain_ref, bf16[512,1152]{1,0:T(8,128)(2,1)S(1)} %pad_maximum_fusion.2.refs_0_, bf16[256,1024]{1,0:T(8,128)(2,1)S(1)} %shard_map.157.refs_1_, bf16[256,1024]{1,0:T(8,128)(2,1)S(1)} %copy-done.5, ...), custom_call_target="tpu_custom_call" | custom-call | flops 2415919104 | bytes 8388608 | tf_op jit(solution)/shard_map/pallas_call | solution.py:216
  85.4 4.6 %collective-permute-done.17 = f32[7,128]{1,0:T(8,128)S(1)} collective-permute-done((f32[7,128]{1,0:T(8,128)S(1)}, f32[7,128]{1,0:T(8,128)S(1)}, u32[]{:S(2)}, u32[]{:S(2)}) %collective-permute-start.17) | collective-permute-done | bytes 3616 | tf_op jit(solution)/shard_map/ppermute | solution.py:23
  90.8 1.2 %collective-permute-done.21.refs_5_ = bf16[256,1024]{1,0:T(8,128)(2,1)S(1)} collective-permute-done((bf16[256,1024]{1,0:T(8,128)(2,1)S(1)}, bf16[256,1024]{1,0:T(8,128)(2,1)S(1)}, u32[]{:S(2)}, u32[]{:S(2)}) %collective-permute-start.21) | collective-permute-done | bytes 524320 | tf_op jit(solution)/shard_map/ppermute | solution.py:23
  91.9 5.0 %shard_map.160 = f32[2,8,256]{2,1,0:T(8,128)S(1)} custom-call(bf16[2048,1152]{1,0:T(8,128)(2,1)S(1)} %copy-done, f32[2,1152]{1,0:T(2,128)S(1)} %fusion.gain_ref, bf16[512,1152]{1,0:T(8,128)(2,1)S(1)} %copy-done.7, bf16[256,1024]{1,0:T(8,128)(2,1)S(1)} %collective-permute-done.12.refs_1_, bf16[256,1024]{1,0:T(8,128)(2,1)S(1)} %collective-permute-done.19.refs_2_, ...), custom_call_target="tpu_custom_call" | custom-call | flops 2415919104 | bytes 8388608 | tf_op jit(solution)/shard_map/pallas_call | solution.py:216
  97.4 1.2 %collective-permute-start.24 = (f32[4,8,256]{2,1,0:T(8,128)S(1)}, f32[4,8,256]{2,1,0:T(8,128)S(1)}, u32[]{:S(2)}, u32[]{:S(2)}) collective-permute-start(f32[4,8,256]{2,1,0:T(8,128)S(1)} %pad_maximum_fusion.4), channel_id=1, source_target_pairs={{0,3},{1,2},{2,1},{3,0},{4,7},{5,6},{6,5},{7,4},{8,11},{9,10},{10,... | collective-permute-start | bytes 98312 | tf_op jit(solution)/shard_map/ppermute | solution.py:23
  99.3 1.9 %collective-permute-done.23 = f32[4,8,256]{2,1,0:T(8,128)S(1)} collective-permute-done((f32[4,8,256]{2,1,0:T(8,128)S(1)}, f32[4,8,256]{2,1,0:T(8,128)S(1)}, u32[]{:S(2)}, u32[]{:S(2)}) %collective-permute-start.23) | collective-permute-done | bytes 32800 | tf_op jit(solution)/shard_map/ppermute | solution.py:23
  102.1 2.9 %collective-permute-done.25 = f32[1,128]{1,0:T(1,128)S(1)} collective-permute-done((f32[1,128]{1,0:T(1,128)S(1)}, f32[1,128]{1,0:T(1,128)S(1)}, u32[]{:S(2)}, u32[]{:S(2)}) %collective-permute-start.25) | collective-permute-done | bytes 544 | tf_op jit(solution)/shard_map/ppermute | solution.py:23
  105.1 1.3 %collective-permute-start.28 = (f32[1,128]{1,0:T(1,128)S(1)}, f32[1,128]{1,0:T(1,128)S(1)}, u32[]{:S(2)}, u32[]{:S(2)}) collective-permute-start(f32[1,128]{1,0:T(1,128)S(1)} %bitcast_add_fusion), channel_id=1, source_target_pairs={{0,24},{4,28},{8,16},{12,20},{16,8},{20,12},{24,0},{28,4},{1,25},{... | collective-permute-start | bytes 1544 | tf_op jit(solution)/shard_map/ppermute | solution.py:23
  107.1 2.4 %collective-permute-start.26 = (f32[1,128]{1,0:T(1,128)S(1)}, f32[1,128]{1,0:T(1,128)S(1)}, u32[]{:S(2)}, u32[]{:S(2)}) collective-permute-start(f32[1,128]{1,0:T(1,128)S(1)} %bitcast_add_fusion), channel_id=1, source_target_pairs={{0,8},{4,12},{8,0},{12,4},{16,24},{20,28},{24,16},{28,20},{1,9},{5... | collective-permute-start | bytes 1544 | tf_op jit(solution)/shard_map/ppermute | solution.py:23
  (120 shorter events, 18.0 us)
Async XLA Ops:
  0.6 15.1 %collective-permute-start.1 = (bf16[128,2048]{1,0:T(8,128)(2,1)}, bf16[128,2048]{1,0:T(8,128)(2,1)S(1)}, u32[]{:S(2)}, u32[]{:S(2)}) collective-permute-start(bf16[128,2048]{1,0:T(8,128)(2,1)} %bitcast.109), channel_id=1, source_target_pairs={{0,4},{4,0},{8,12},{12,8},{16,20},{20,16},{24,28},{28,24},{1,5},{5... | collective-permute-start | bytes 1572872 | tf_op jit(solution)/shard_map/ppermute | solution.py:23
  3.6 13.8 %collective-permute-start = (bf16[128,2048]{1,0:T(8,128)(2,1)}, bf16[128,2048]{1,0:T(8,128)(2,1)S(1)}, u32[]{:S(2)}, u32[]{:S(2)}) collective-permute-start(bf16[128,2048]{1,0:T(8,128)(2,1)} %bitcast.110), channel_id=1, source_target_pairs={{0,16},{4,20},{8,0},{12,4},{16,24},{20,28},{24,8},{28,12},{1,17},{... | collective-permute-start | bytes 1572872 | tf_op jit(solution)/shard_map/ppermute | solution.py:30
  8.8 36.0 %collective-permute-start.7 = (bf16[512,1152]{1,0:T(8,128)(2,1)}, bf16[512,1152]{1,0:T(8,128)(2,1)S(1)}, u32[]{:S(2)}, u32[]{:S(2)}) collective-permute-start(bf16[512,1152]{1,0:T(8,128)(2,1)} %pad_maximum_fusion.1), channel_id=1, source_target_pairs={{0,2},{1,3},{2,0},{3,1},{4,6},{5,7},{6,4},{7,5},{8,10},{9,11},{10,... | collective-permute-start | bytes 3538952 | tf_op jit(solution)/shard_map/ppermute | solution.py:23
  15.8 20.2 %copy-start.10 = (bf16[128,2048]{1,0:T(8,128)(2,1)}, bf16[128,2048]{1,0:T(8,128)(2,1)S(1)}, u32[]{:S(2)}) copy-start(bf16[128,2048]{1,0:T(8,128)(2,1)S(1)} %collective-permute-done.1.refs_2_.refs_7_.refs_10_) | copy-start | bytes 1572868
  17.5 12.6 %copy-start.11 = (bf16[128,2048]{1,0:T(8,128)(2,1)}, bf16[128,2048]{1,0:T(8,128)(2,1)S(1)}, u32[]{:S(2)}) copy-start(bf16[128,2048]{1,0:T(8,128)(2,1)S(1)} %collective-permute-done.refs_1_.refs_6_.refs_9_) | copy-start | bytes 1572868
  17.5 12.5 %collective-permute-start.3 = (bf16[128,2048]{1,0:T(8,128)(2,1)S(1)}, bf16[128,2048]{1,0:T(8,128)(2,1)S(1)}, u32[]{:S(2)}, u32[]{:S(2)}) collective-permute-start(bf16[128,2048]{1,0:T(8,128)(2,1)S(1)} %collective-permute-done.refs_1_.refs_6_.refs_9_), channel_id=1, source_target_pairs={{0,4},{4,0},{8,12},{12,8},{16,20},{20,16},{24,28},{28,24},{1,5},{5... | collective-permute-start | bytes 1572872 | tf_op jit(solution)/shard_map/ppermute | solution.py:23
  18.0 13.0 %collective-permute-start.2 = (bf16[128,2048]{1,0:T(8,128)(2,1)S(1)}, bf16[128,2048]{1,0:T(8,128)(2,1)}, u32[]{:S(2)}, u32[]{:S(2)}) collective-permute-start(bf16[128,2048]{1,0:T(8,128)(2,1)S(1)} %collective-permute-done.refs_1_.refs_6_.refs_9_), channel_id=1, source_target_pairs={{0,16},{4,20},{8,0},{12,4},{16,24},{20,28},{24,8},{28,12},{1,17},{... | collective-permute-start | bytes 1572872 | tf_op jit(solution)/shard_map/ppermute | solution.py:30
  21.3 39.3 %collective-permute-start.11 = (bf16[512,1152]{1,0:T(8,128)(2,1)}, bf16[512,1152]{1,0:T(8,128)(2,1)}, u32[]{:S(2)}, u32[]{:S(2)}) collective-permute-start(bf16[512,1152]{1,0:T(8,128)(2,1)} %pad_maximum_fusion), channel_id=1, source_target_pairs={{0,3},{1,2},{2,1},{3,0},{4,7},{5,6},{6,5},{7,4},{8,11},{9,10},{10,... | collective-permute-start | bytes 3538952 | tf_op jit(solution)/shard_map/ppermute | solution.py:23
  21.3 8.7 %collective-permute-start.4 = (f32[1,128]{1,0:T(1,128)S(1)}, f32[1,128]{1,0:T(1,128)S(1)}, u32[]{:S(2)}, u32[]{:S(2)}) collective-permute-start(f32[1,128]{1,0:T(1,128)S(1)} %compare_select_fusion.1), channel_id=1, source_target_pairs={{0,4},{4,0},{8,12},{12,8},{16,20},{20,16},{24,28},{28,24},{1,5},{5... | collective-permute-start | bytes 1544 | tf_op jit(solution)/shard_map/ppermute | solution.py:23
  31.0 14.8 %collective-permute-start.6 = (bf16[128,2048]{1,0:T(8,128)(2,1)}, bf16[128,2048]{1,0:T(8,128)(2,1)S(1)}, u32[]{:S(2)}, u32[]{:S(2)}) collective-permute-start(bf16[128,2048]{1,0:T(8,128)(2,1)} %collective-permute-done.2.refs_3_.refs_8_.refs_11_), channel_id=1, source_target_pairs={{0,4},{4,0},{8,12},{12,8},{16,20},{20,16},{24,28},{28,24},{1,5},{5... | collective-permute-start | bytes 1572872 | tf_op jit(solution)/shard_map/ppermute | solution.py:23
  32.5 13.4 %collective-permute-start.5 = (bf16[128,2048]{1,0:T(8,128)(2,1)}, bf16[128,2048]{1,0:T(8,128)(2,1)S(1)}, u32[]{:S(2)}, u32[]{:S(2)}) collective-permute-start(bf16[128,2048]{1,0:T(8,128)(2,1)} %collective-permute-done.2.refs_3_.refs_8_.refs_11_), channel_id=1, source_target_pairs={{0,16},{4,20},{8,0},{12,4},{16,24},{20,28},{24,8},{28,12},{1,17},{... | collective-permute-start | bytes 1572872 | tf_op jit(solution)/shard_map/ppermute | solution.py:30
  36.0 8.8 %collective-permute-start.8 = (f32[1,128]{1,0:T(1,128)S(1)}, f32[1,128]{1,0:T(1,128)S(1)}, u32[]{:S(2)}, u32[]{:S(2)}) collective-permute-start(f32[1,128]{1,0:T(1,128)S(1)} %add.71), channel_id=1, source_target_pairs={{0,8},{4,12},{8,0},{12,4},{16,24},{20,28},{24,16},{28,20},{1,9},{5... | collective-permute-start | bytes 1544 | tf_op jit(solution)/shard_map/ppermute | solution.py:23
  45.8 10.2 %collective-permute-start.10 = (bf16[128,2048]{1,0:T(8,128)(2,1)S(1)}, bf16[128,2048]{1,0:T(8,128)(2,1)S(1)}, u32[]{:S(2)}, u32[]{:S(2)}) collective-permute-start(bf16[128,2048]{1,0:T(8,128)(2,1)S(1)} %collective-permute-done.5.refs_0_.refs_3_.refs_5_.refs_13_), channel_id=1, source_target_pairs={{0,4},{4,0},{8,12},{12,8},{16,20},{20,16},{24,28},{28,24},{1,5},{5... | collective-permute-start | bytes 1572872 | tf_op jit(solution)/shard_map/ppermute | solution.py:23
  46.4 4.9 %collective-permute-start.9 = (f32[1,128]{1,0:T(1,128)S(1)}, f32[1,128]{1,0:T(1,128)S(1)}, u32[]{:S(2)}, u32[]{:S(2)}) collective-permute-start(f32[1,128]{1,0:T(1,128)S(1)} %add.73), channel_id=1, source_target_pairs={{0,16},{4,20},{8,24},{12,28},{16,0},{20,4},{24,8},{28,12},{1,17},{... | collective-permute-start | bytes 1544 | tf_op jit(solution)/shard_map/ppermute | solution.py:23
  60.6 14.6 %collective-permute-start.12 = (bf16[256,1024]{1,0:T(8,128)(2,1)S(1)}, bf16[256,1024]{1,0:T(8,128)(2,1)S(1)}, u32[]{:S(2)}, u32[]{:S(2)}) collective-permute-start(bf16[256,1024]{1,0:T(8,128)(2,1)S(1)} %shard_map.157.refs_1_), channel_id=1, source_target_pairs={{0,2},{1,3},{2,0},{3,1},{4,6},{5,7},{6,4},{7,5},{8,10},{9,11},{10,... | collective-permute-start | bytes 1572872 | tf_op jit(solution)/shard_map/ppermute | solution.py:23
  62.4 16.9 %collective-permute-start.13 = (bf16[512,1152]{1,0:T(8,128)(2,1)}, bf16[512,1152]{1,0:T(8,128)(2,1)S(1)}, u32[]{:S(2)}, u32[]{:S(2)}) collective-permute-start(bf16[512,1152]{1,0:T(8,128)(2,1)} %pad_maximum_fusion.3), channel_id=1, source_target_pairs={{0,1},{1,0},{2,3},{3,2},{4,5},{5,4},{6,7},{7,6},{8,9},{9,8},{10,11... | collective-permute-start | bytes 3538952 | tf_op jit(solution)/shard_map/ppermute | solution.py:23
  63.9 14.6 %collective-permute-start.14 = (bf16[256,1024]{1,0:T(8,128)(2,1)S(1)}, bf16[256,1024]{1,0:T(8,128)(2,1)S(1)}, u32[]{:S(2)}, u32[]{:S(2)}) collective-permute-start(bf16[256,1024]{1,0:T(8,128)(2,1)S(1)} %shard_map.157.refs_1_), channel_id=1, source_target_pairs={{0,1},{1,0},{2,3},{3,2},{4,5},{5,4},{6,7},{7,6},{8,9},{9,8},{10,11... | collective-permute-start | bytes 1572872 | tf_op jit(solution)/shard_map/ppermute | solution.py:23
  75.2 4.1 %collective-permute-start.15 = (bf16[256,1024]{1,0:T(8,128)(2,1)}, bf16[256,1024]{1,0:T(8,128)(2,1)S(1)}, u32[]{:S(2)}, u32[]{:S(2)}) collective-permute-start(bf16[256,1024]{1,0:T(8,128)(2,1)} %shard_map.158.refs_2_), channel_id=1, source_target_pairs={{0,1},{1,0},{2,3},{3,2},{4,5},{5,4},{6,7},{7,6},{8,9},{9,8},{10,11... | collective-permute-start | bytes 1572872 | tf_op jit(solution)/shard_map/ppermute | solution.py:23
  75.3 14.7 %collective-permute-start.19 = (bf16[256,1024]{1,0:T(8,128)(2,1)}, bf16[256,1024]{1,0:T(8,128)(2,1)S(1)}, u32[]{:S(2)}, u32[]{:S(2)}) collective-permute-start(bf16[256,1024]{1,0:T(8,128)(2,1)} %shard_map.158.refs_2_), channel_id=1, source_target_pairs={{0,2},{1,3},{2,0},{3,1},{4,6},{5,7},{6,4},{7,5},{8,10},{9,11},{10,... | collective-permute-start | bytes 1572872 | tf_op jit(solution)/shard_map/ppermute | solution.py:23
  76.0 1.2 %collective-permute-start.16 = (f32[7,128]{1,0:T(8,128)S(1)}, f32[7,128]{1,0:T(8,128)S(1)}, u32[]{:S(2)}, u32[]{:S(2)}) collective-permute-start(f32[7,128]{1,0:T(8,128)S(1)} %select_maximum_fusion), channel_id=1, source_target_pairs={{0,1},{1,0},{2,3},{3,2},{4,5},{5,4},{6,7},{7,6},{8,9},{9,8},{10,11... | collective-permute-start | bytes 10760 | tf_op jit(solution)/shard_map/ppermute | solution.py:23
  76.1 15.8 %copy-start.7 = (bf16[512,1152]{1,0:T(8,128)(2,1)S(1)}, bf16[512,1152]{1,0:T(8,128)(2,1)}, u32[]{:S(2)}) copy-start(bf16[512,1152]{1,0:T(8,128)(2,1)} %copy-done.6) | copy-start | bytes 3538948
  77.3 12.7 %collective-permute-start.17 = (f32[7,128]{1,0:T(8,128)S(1)}, f32[7,128]{1,0:T(8,128)S(1)}, u32[]{:S(2)}, u32[]{:S(2)}) collective-permute-start(f32[7,128]{1,0:T(8,128)S(1)} %select_maximum_fusion), channel_id=1, source_target_pairs={{0,2},{1,3},{2,0},{3,1},{4,6},{5,7},{6,4},{7,5},{8,10},{9,11},{10,... | collective-permute-start | bytes 10760 | tf_op jit(solution)/shard_map/ppermute | solution.py:23
  78.6 11.4 %collective-permute-start.18 = (f32[7,128]{1,0:T(8,128)S(1)}, f32[7,128]{1,0:T(8,128)S(1)}, u32[]{:S(2)}, u32[]{:S(2)}) collective-permute-start(f32[7,128]{1,0:T(8,128)S(1)} %collective-permute-done.16), channel_id=1, source_target_pairs={{0,2},{1,3},{2,0},{3,1},{4,6},{5,7},{6,4},{7,5},{8,10},{9,11},{10,... | collective-permute-start | bytes 10760 | tf_op jit(solution)/shard_map/ppermute | solution.py:23
  79.3 11.5 %collective-permute-start.20 = (bf16[256,1024]{1,0:T(8,128)(2,1)S(1)}, bf16[256,1024]{1,0:T(8,128)(2,1)S(1)}, u32[]{:S(2)}, u32[]{:S(2)}) collective-permute-start(bf16[256,1024]{1,0:T(8,128)(2,1)S(1)} %collective-permute-done.12.refs_1_), channel_id=1, source_target_pairs={{0,1},{1,0},{2,3},{3,2},{4,5},{5,4},{6,7},{7,6},{8,9},{9,8},{10,11... | collective-permute-start | bytes 1572872 | tf_op jit(solution)/shard_map/ppermute | solution.py:23
  90.0 1.9 %collective-permute-start.21 = (bf16[256,1024]{1,0:T(8,128)(2,1)S(1)}, bf16[256,1024]{1,0:T(8,128)(2,1)S(1)}, u32[]{:S(2)}, u32[]{:S(2)}) collective-permute-start(bf16[256,1024]{1,0:T(8,128)(2,1)S(1)} %collective-permute-done.19.refs_2_), channel_id=1, source_target_pairs={{0,1},{1,0},{2,3},{3,2},{4,5},{5,4},{6,7},{7,6},{8,9},{9,8},{10,11... | collective-permute-start | bytes 1572872 | tf_op jit(solution)/shard_map/ppermute | solution.py:23
  96.9 4.2 %collective-permute-start.23 = (f32[4,8,256]{2,1,0:T(8,128)S(1)}, f32[4,8,256]{2,1,0:T(8,128)S(1)}, u32[]{:S(2)}, u32[]{:S(2)}) collective-permute-start(f32[4,8,256]{2,1,0:T(8,128)S(1)} %pad_maximum_fusion.4), channel_id=1, source_target_pairs={{0,2},{1,3},{2,0},{3,1},{4,6},{5,7},{6,4},{7,5},{8,10},{9,11},{10,... | collective-permute-start | bytes 98312 | tf_op jit(solution)/shard_map/ppermute | solution.py:23
  97.4 3.8 %collective-permute-start.24 = (f32[4,8,256]{2,1,0:T(8,128)S(1)}, f32[4,8,256]{2,1,0:T(8,128)S(1)}, u32[]{:S(2)}, u32[]{:S(2)}) collective-permute-start(f32[4,8,256]{2,1,0:T(8,128)S(1)} %pad_maximum_fusion.4), channel_id=1, source_target_pairs={{0,3},{1,2},{2,1},{3,0},{4,7},{5,6},{6,5},{7,4},{8,11},{9,10},{10,... | collective-permute-start | bytes 98312 | tf_op jit(solution)/shard_map/ppermute | solution.py:23
  98.6 2.6 %collective-permute-start.22 = (f32[4,8,256]{2,1,0:T(8,128)S(1)}, f32[4,8,256]{2,1,0:T(8,128)S(1)}, u32[]{:S(2)}, u32[]{:S(2)}) collective-permute-start(f32[4,8,256]{2,1,0:T(8,128)S(1)} %pad_maximum_fusion.4), channel_id=1, source_target_pairs={{0,1},{1,0},{2,3},{3,2},{4,5},{5,4},{6,7},{7,6},{8,9},{9,8},{10,11... | collective-permute-start | bytes 98312 | tf_op jit(solution)/shard_map/ppermute | solution.py:23
  101.4 3.6 %collective-permute-start.25 = (f32[1,128]{1,0:T(1,128)S(1)}, f32[1,128]{1,0:T(1,128)S(1)}, u32[]{:S(2)}, u32[]{:S(2)}) collective-permute-start(f32[1,128]{1,0:T(1,128)S(1)} %bitcast.132), channel_id=1, source_target_pairs={{0,4},{4,0},{8,12},{12,8},{16,20},{20,16},{24,28},{28,24},{1,5},{5... | collective-permute-start | bytes 1544 | tf_op jit(solution)/shard_map/ppermute | solution.py:23
  105.1 6.1 %collective-permute-start.28 = (f32[1,128]{1,0:T(1,128)S(1)}, f32[1,128]{1,0:T(1,128)S(1)}, u32[]{:S(2)}, u32[]{:S(2)}) collective-permute-start(f32[1,128]{1,0:T(1,128)S(1)} %bitcast_add_fusion), channel_id=1, source_target_pairs={{0,24},{4,28},{8,16},{12,20},{16,8},{20,12},{24,0},{28,4},{1,25},{... | collective-permute-start | bytes 1544 | tf_op jit(solution)/shard_map/ppermute | solution.py:23
  106.4 4.7 %collective-permute-start.27 = (f32[1,128]{1,0:T(1,128)S(1)}, f32[1,128]{1,0:T(1,128)S(1)}, u32[]{:S(2)}, u32[]{:S(2)}) collective-permute-start(f32[1,128]{1,0:T(1,128)S(1)} %bitcast_add_fusion), channel_id=1, source_target_pairs={{0,16},{4,20},{8,24},{12,28},{16,0},{20,4},{24,8},{28,12},{1,17},{... | collective-permute-start | bytes 1544 | tf_op jit(solution)/shard_map/ppermute | solution.py:23
  107.1 4.1 %collective-permute-start.26 = (f32[1,128]{1,0:T(1,128)S(1)}, f32[1,128]{1,0:T(1,128)S(1)}, u32[]{:S(2)}, u32[]{:S(2)}) collective-permute-start(f32[1,128]{1,0:T(1,128)S(1)} %bitcast_add_fusion), channel_id=1, source_target_pairs={{0,8},{4,12},{8,0},{12,4},{16,24},{20,28},{24,16},{28,20},{1,9},{5... | collective-permute-start | bytes 1544 | tf_op jit(solution)/shard_map/ppermute | solution.py:23
  (19 other events, 143.5 us)

commit v7 on v6

--- a/solution.py
+++ b/solution.py
@@ -334,10 +334,6 @@
         last = [tails[key] for key in waiting]
         asked, attended[0][g], *last = lax.optimization_barrier((asked, attended[0][g], *last))
         tails.update(zip(waiting, last))
-        if g and fsdp > 2:
-            attended[0][g], attended[fsdp // 2][g - 1] = lax.optimization_barrier(
-                (attended[0][g], attended[fsdp // 2][g - 1])
-            )
         bit = fsdp // 2
         known = [0]
         while bit > 1:

time: 115 us -> 114 us (level)
  waiting for transfers between devices: 35.1 us -> 33.3 us
  other arithmetic: 7.66 us -> 8.91 us
    ppermute x26, waiting for transfers between devices: 32.4 us -> 30.7 us  [swap(): return lax.ppermute(value, axis, [(i, i ^ bit) for i in range(count)])]
    concatenate x4, other arithmetic: 3.44 us -> 4.68 us  [cut(): jnp.concatenate([lax.dynamic_slice_in_dim(value, start, columns, 1) for v...]
    unnamed x44 -> x38, local copies, waits for them, and re-layouts: 3.45 us -> 2.42 us
  transfers between devices with their start and end apart: 29 -> 29, of which waited for: 13 -> 15; matrix products, arithmetic and copies ran while one was open for 11% -> 12% of each run, Pallas kernels for 19% -> 20%
where the time goes in v7:
time: 114 us; the launch traced here: 113 us
  waiting for transfers between devices  33.3 us (29%)
  starting transfers between devices  32.9 us (29%)
  Pallas kernels  26 us (23%)
  other arithmetic  8.91 us (8%)
  local copies, waits for them, and re-layouts  8.02 us (7%)
  between operations  4.13 us (4%)
    ppermute x26, waiting for transfers between devices, swap(): return lax.ppermute(value, axis, [(i, i ^ bit) for i in range(count)])  30.7 us
    ppermute x26, starting transfers between devices, swap(): return lax.ppermute(value, axis, [(i, i ^ bit) for i in range(count)])  23.5 us
    pallas_call x3, Pallas kernels, attend(): pl.pallas_call(functools.partial(kernel, len(blocks)), grid=(per_group,),...  17.3 us
    ppermute x3, starting transfers between devices, around(): lax.ppermute(value, axis, [(i, after[i // 2] * 2 + i % 2) for i in range(...  9.35 us
    pallas_call x2, Pallas kernels, project(): pl.pallas_call(functools.partial(project_kernel, sources), out_shape=jax....  8.68 us
    concatenate x4, other arithmetic, cut(): jnp.concatenate([lax.dynamic_slice_in_dim(value, start, columns, 1) for v...  4.68 us
    dynamic_slice x3, local copies, waits for them, and re-layouts, cut(): lax.dynamic_slice_in_dim(value, start, columns, 1)  4.34 us
    ppermute x3, waiting for transfers between devices, around(): lax.ppermute(value, axis, [(i, after[i // 2] * 2 + i % 2) for i in range(...  2.63 us
  transfers between devices with their start and end apart: 29, of which 15 were waited for; matrix products, arithmetic and copies ran while one was open for 12% of the time, Pallas kernels for 20%

profile of v7, /device:TPU:0, one launch (start us, length us, event | category | flops | bytes accessed | tf_op | source)
XLA Modules:
  0.0 113.2 jit_solution(4300770388538857944)
XLA Ops:
  0.6 3.0 %collective-permute-start.1 = (bf16[128,2048]{1,0:T(8,128)(2,1)}, bf16[128,2048]{1,0:T(8,128)(2,1)S(1)}, u32[]{:S(2)}, u32[]{:S(2)}) collective-permute-start(bf16[128,2048]{1,0:T(8,128)(2,1)} %bitcast.109), channel_id=1, source_target_pairs={{0,4},{4,0},{8,12},{12,8},{16,20},{20,16},{24,28},{28,24},{1,5},{5... | collective-permute-start | bytes 1572872 | tf_op jit(solution)/shard_map/ppermute | solution.py:23
  3.6 2.6 %collective-permute-start = (bf16[128,2048]{1,0:T(8,128)(2,1)}, bf16[128,2048]{1,0:T(8,128)(2,1)S(1)}, u32[]{:S(2)}, u32[]{:S(2)}) collective-permute-start(bf16[128,2048]{1,0:T(8,128)(2,1)} %bitcast.110), channel_id=1, source_target_pairs={{0,16},{4,20},{8,0},{12,4},{16,24},{20,28},{24,8},{28,12},{1,17},{... | collective-permute-start | bytes 1572872 | tf_op jit(solution)/shard_map/ppermute | solution.py:30
  6.2 1.3 %constant_dynamic-slice_fusion.5 = (bf16[256,1152]{1,0:T(8,128)(2,1)S(1)}, bf16[256,1152]{1,0:T(8,128)(2,1)S(1)}) fusion(bf16[256,4608]{1,0:T(8,128)(2,1)} %bitcast.117, s32[]{:T(128)S(6)} %select_n.55, s32[]{:T(128)S(6)} %select_n.52), kind=kLoop, calls=%fused_computation.71 | loop fusion | bytes 2359304 | tf_op jit(solution)/shard_map/dynamic_slice | solution.py:263
  8.8 1.5 %collective-permute-start.7 = (bf16[512,1152]{1,0:T(8,128)(2,1)}, bf16[512,1152]{1,0:T(8,128)(2,1)S(1)}, u32[]{:S(2)}, u32[]{:S(2)}) collective-permute-start(bf16[512,1152]{1,0:T(8,128)(2,1)} %pad_maximum_fusion.1), channel_id=1, source_target_pairs={{0,2},{1,3},{2,0},{3,1},{4,6},{5,7},{6,4},{7,5},{8,10},{9,11},{10,... | collective-permute-start | bytes 3538952 | tf_op jit(solution)/shard_map/ppermute | solution.py:23
  14.0 1.8 %collective-permute-done.1.refs_2_.refs_7_.refs_10_ = bf16[128,2048]{1,0:T(8,128)(2,1)S(1)} collective-permute-done((bf16[128,2048]{1,0:T(8,128)(2,1)}, bf16[128,2048]{1,0:T(8,128)(2,1)S(1)}, u32[]{:S(2)}, u32[]{:S(2)}) %collective-permute-start.1) | collective-permute-done | bytes 524320 | tf_op jit(solution)/shard_map/ppermute | solution.py:23
  15.8 1.7 %collective-permute-done.refs_1_.refs_6_.refs_9_ = bf16[128,2048]{1,0:T(8,128)(2,1)S(1)} collective-permute-done((bf16[128,2048]{1,0:T(8,128)(2,1)}, bf16[128,2048]{1,0:T(8,128)(2,1)S(1)}, u32[]{:S(2)}, u32[]{:S(2)}) %collective-permute-start) | collective-permute-done | bytes 524320 | tf_op jit(solution)/shard_map/ppermute | solution.py:30
  18.0 3.3 %collective-permute-start.2 = (bf16[128,2048]{1,0:T(8,128)(2,1)S(1)}, bf16[128,2048]{1,0:T(8,128)(2,1)}, u32[]{:S(2)}, u32[]{:S(2)}) collective-permute-start(bf16[128,2048]{1,0:T(8,128)(2,1)S(1)} %collective-permute-done.refs_1_.refs_6_.refs_9_), channel_id=1, source_target_pairs={{0,16},{4,20},{8,0},{12,4},{16,24},{20,28},{24,8},{28,12},{1,17},{... | collective-permute-start | bytes 1572872 | tf_op jit(solution)/shard_map/ppermute | solution.py:30
  21.3 1.5 %collective-permute-start.4 = (f32[1,128]{1,0:T(1,128)S(1)}, f32[1,128]{1,0:T(1,128)S(1)}, u32[]{:S(2)}, u32[]{:S(2)}) collective-permute-start(f32[1,128]{1,0:T(1,128)S(1)} %compare_select_fusion.1), channel_id=1, source_target_pairs={{0,4},{4,0},{8,12},{12,8},{16,20},{20,16},{24,28},{28,24},{1,5},{5... | collective-permute-start | bytes 1544 | tf_op jit(solution)/shard_map/ppermute | solution.py:23
  22.8 7.2 %collective-permute-done.4 = f32[1,128]{1,0:T(1,128)S(1)} collective-permute-done((f32[1,128]{1,0:T(1,128)S(1)}, f32[1,128]{1,0:T(1,128)S(1)}, u32[]{:S(2)}, u32[]{:S(2)}) %collective-permute-start.4) | collective-permute-done | bytes 544 | tf_op jit(solution)/shard_map/ppermute | solution.py:23
  31.0 1.5 %collective-permute-start.6 = (bf16[128,2048]{1,0:T(8,128)(2,1)}, bf16[128,2048]{1,0:T(8,128)(2,1)S(1)}, u32[]{:S(2)}, u32[]{:S(2)}) collective-permute-start(bf16[128,2048]{1,0:T(8,128)(2,1)} %collective-permute-done.2.refs_3_.refs_8_.refs_11_), channel_id=1, source_target_pairs={{0,4},{4,0},{8,12},{12,8},{16,20},{20,16},{24,28},{28,24},{1,5},{5... | collective-permute-start | bytes 1572872 | tf_op jit(solution)/shard_map/ppermute | solution.py:23
  32.5 3.5 %collective-permute-start.5 = (bf16[128,2048]{1,0:T(8,128)(2,1)}, bf16[128,2048]{1,0:T(8,128)(2,1)S(1)}, u32[]{:S(2)}, u32[]{:S(2)}) collective-permute-start(bf16[128,2048]{1,0:T(8,128)(2,1)} %collective-permute-done.2.refs_3_.refs_8_.refs_11_), channel_id=1, source_target_pairs={{0,16},{4,20},{8,0},{12,4},{16,24},{20,28},{24,8},{28,12},{1,17},{... | collective-permute-start | bytes 1572872 | tf_op jit(solution)/shard_map/ppermute | solution.py:30
  36.0 7.2 %shard_map.156 = (f32[2048,128]{1,0:T(8,128)}, f32[2048,128]{1,0:T(8,128)}) custom-call(bf16[2,128,2048]{2,1,0:T(8,128)(2,1)} %bitcast.100, bf16[2,128,2048]{2,1,0:T(8,128)(2,1)} %bitcast.105, bf16[2,128,2048]{2,1,0:T(8,128)(2,1)} %bitcast.106, bf16[128,2048]{1,0:T(8,128)(2,1)} %bitcast.111, bf16[128,2048]{1,0:T(8,128)(2,1)} %copy-done.9, ...), custom_call_target="tpu_custom_call" | custom-call | flops 805306368 | bytes 4194304 | tf_op jit(solution)/shard_map/pallas_call | solution.py:161
  43.2 1.6 %collective-permute-done.8 = f32[1,128]{1,0:T(1,128)S(1)} collective-permute-done((f32[1,128]{1,0:T(1,128)S(1)}, f32[1,128]{1,0:T(1,128)S(1)}, u32[]{:S(2)}, u32[]{:S(2)}) %collective-permute-start.8) | collective-permute-done | bytes 544 | tf_op jit(solution)/shard_map/ppermute | solution.py:23
  45.4 2.9 %constant_dynamic-slice_fusion = (bf16[256,1152]{1,0:T(8,128)(2,1)S(1)}, bf16[256,1152]{1,0:T(8,128)(2,1)}, bf16[256,1152]{1,0:T(8,128)(2,1)}, bf16[256,1152]{1,0:T(8,128)(2,1)S(1)}) fusion(bf16[256,4608]{1,0:T(8,128)(2,1)} %bitcast.115, s32[]{:T(128)S(6)} %select_n.56, s32[]{:T(128)S(6)} %select_n.51, bf16[256,4608]{1,0:T(8,128)(2,1)} %bitcast.118), kind=kLoop, calls=%fused_computation.66 | loop fusion | bytes 4718600 | tf_op jit(solution)/shard_map/dynamic_slice | solution.py:263
  49.5 3.2 %collective-permute-start.9 = (f32[1,128]{1,0:T(1,128)S(1)}, f32[1,128]{1,0:T(1,128)S(1)}, u32[]{:S(2)}, u32[]{:S(2)}) collective-permute-start(f32[1,128]{1,0:T(1,128)S(1)} %add.73), channel_id=1, source_target_pairs={{0,16},{4,20},{8,24},{12,28},{16,0},{20,4},{24,8},{28,12},{1,17},{... | collective-permute-start | bytes 1544 | tf_op jit(solution)/shard_map/ppermute | solution.py:23
  52.6 1.5 %collective-permute-done.9 = f32[1,128]{1,0:T(1,128)S(1)} collective-permute-done((f32[1,128]{1,0:T(1,128)S(1)}, f32[1,128]{1,0:T(1,128)S(1)}, u32[]{:S(2)}, u32[]{:S(2)}) %collective-permute-start.9) | collective-permute-done | bytes 544 | tf_op jit(solution)/shard_map/ppermute | solution.py:23
  54.2 4.5 %collective-permute-done.10.refs_2_.refs_5_.refs_7_.refs_15_ = bf16[128,2048]{1,0:T(8,128)(2,1)S(1)} collective-permute-done((bf16[128,2048]{1,0:T(8,128)(2,1)S(1)}, bf16[128,2048]{1,0:T(8,128)(2,1)S(1)}, u32[]{:S(2)}, u32[]{:S(2)}) %collective-permute-start.10) | collective-permute-done | bytes 524320 | tf_op jit(solution)/shard_map/ppermute | solution.py:23
  58.8 2.5 %shard_map.157.refs_1_ = bf16[256,1024]{1,0:T(8,128)(2,1)S(1)} custom-call(bf16[2,128,2048]{2,1,0:T(8,128)(2,1)S(1)} %bitcast.102, f32[2048,128]{1,0:T(8,128)S(1)} %copy-done.6, f32[2048,128]{1,0:T(8,128)S(1)} %copy-done.7, bf16[128,2048]{1,0:T(8,128)(2,1)S(1)} %collective-permute-done.5.refs_0_.refs_3_.refs_5_.refs_13_, ...), custom_call_target="tpu_custom_call" | custom-call | flops 402653184 | bytes 4194304 | tf_op jit(solution)/shard_map/pallas_call | solution.py:161
  61.4 3.0 %collective-permute-done.11.refs_3_ = bf16[512,1152]{1,0:T(8,128)(2,1)S(1)} collective-permute-done((bf16[512,1152]{1,0:T(8,128)(2,1)}, bf16[512,1152]{1,0:T(8,128)(2,1)S(1)}, u32[]{:S(2)}, u32[]{:S(2)}) %collective-permute-start.11) | collective-permute-done | bytes 1179680 | tf_op jit(solution)/shard_map/ppermute | solution.py:23
  65.0 7.6 %shard_map.158.refs_2_ = bf16[256,1024]{1,0:T(8,128)(2,1)} custom-call(bf16[2,128,2048]{2,1,0:T(8,128)(2,1)} %bitcast.101, bf16[2,128,2048]{2,1,0:T(8,128)(2,1)} %bitcast.107, bf16[2,128,2048]{2,1,0:T(8,128)(2,1)} %bitcast.108, bf16[128,2048]{1,0:T(8,128)(2,1)} %bitcast.113, bf16[128,2048]{1,0:T(8,128)(2,1)} %copy-done.9, bf16[128,2048]{1,0:T(8,128)(2,1)} %copy-done.8, ...), custom_call_target="tpu_custom_call" | custom-call | flops 1207959552 | bytes 4194304 | tf_op jit(solution)/shard_map/pallas_call | solution.py:161
  73.4 1.4 %collective-permute-done.15 = f32[7,128]{1,0:T(8,128)S(1)} collective-permute-done((f32[7,128]{1,0:T(8,128)S(1)}, f32[7,128]{1,0:T(8,128)S(1)}, u32[]{:S(2)}, u32[]{:S(2)}) %collective-permute-start.15) | collective-permute-done | bytes 3616 | tf_op jit(solution)/shard_map/ppermute | solution.py:23
  74.8 1.4 %collective-permute-start.18 = (bf16[256,1024]{1,0:T(8,128)(2,1)}, bf16[256,1024]{1,0:T(8,128)(2,1)S(1)}, u32[]{:S(2)}, u32[]{:S(2)}) collective-permute-start(bf16[256,1024]{1,0:T(8,128)(2,1)} %shard_map.158.refs_2_), channel_id=1, source_target_pairs={{0,2},{1,3},{2,0},{3,1},{4,6},{5,7},{6,4},{7,5},{8,10},{9,11},{10,... | collective-permute-start | bytes 1572872 | tf_op jit(solution)/shard_map/ppermute | solution.py:23
  76.2 1.3 %pad_maximum_fusion.2.refs_0_ = bf16[512,1152]{1,0:T(8,128)(2,1)S(1)} fusion(bf16[256,1152]{1,0:T(8,128)(2,1)} %get-tuple-element.83, bf16[256,1152]{1,0:T(8,128)(2,1)} %get-tuple-element.102), kind=kLoop, calls=%fused_computation.2 | loop fusion | flops 2359296 | bytes 2359296 | tf_op jit(solution)/shard_map/concatenate | solution.py:262
  79.7 2.3 %copy-done = bf16[2048,1152]{1,0:T(8,128)(2,1)S(1)} copy-done((bf16[2048,1152]{1,0:T(8,128)(2,1)S(1)}, bf16[2048,1152]{1,0:T(8,128)(2,1)}, u32[]{:S(2)}) %copy-start) | copy-done | bytes 4718616
  82.0 5.0 %shard_map.159 = f32[2,8,256]{2,1,0:T(8,128)S(1)} custom-call(bf16[2048,1152]{1,0:T(8,128)(2,1)S(1)} %copy-done, f32[2,1152]{1,0:T(2,128)S(1)} %fusion.gain_ref, bf16[512,1152]{1,0:T(8,128)(2,1)S(1)} %pad_maximum_fusion.2.refs_0_, bf16[256,1024]{1,0:T(8,128)(2,1)S(1)} %shard_map.157.refs_1_, bf16[256,1024]{1,0:T(8,128)(2,1)S(1)} %copy-done.5, ...), custom_call_target="tpu_custom_call" | custom-call | flops 2415919104 | bytes 8388608 | tf_op jit(solution)/shard_map/pallas_call | solution.py:216
  87.0 2.7 %collective-permute-done.16 = f32[7,128]{1,0:T(8,128)S(1)} collective-permute-done((f32[7,128]{1,0:T(8,128)S(1)}, f32[7,128]{1,0:T(8,128)S(1)}, u32[]{:S(2)}, u32[]{:S(2)}) %collective-permute-start.16) | collective-permute-done | bytes 3616 | tf_op jit(solution)/shard_map/ppermute | solution.py:23
  90.5 1.2 %collective-permute-done.21.refs_5_ = bf16[256,1024]{1,0:T(8,128)(2,1)S(1)} collective-permute-done((bf16[256,1024]{1,0:T(8,128)(2,1)S(1)}, bf16[256,1024]{1,0:T(8,128)(2,1)S(1)}, u32[]{:S(2)}, u32[]{:S(2)}) %collective-permute-start.21) | collective-permute-done | bytes 524320 | tf_op jit(solution)/shard_map/ppermute | solution.py:23
  91.6 3.7 %shard_map.160 = f32[2,8,256]{2,1,0:T(8,128)S(1)} custom-call(bf16[2048,1152]{1,0:T(8,128)(2,1)S(1)} %copy-done, f32[2,1152]{1,0:T(2,128)S(1)} %fusion.gain_ref, bf16[512,1152]{1,0:T(8,128)(2,1)S(1)} %collective-permute-done.7.refs_0_, bf16[256,1024]{1,0:T(8,128)(2,1)S(1)} %collective-permute-done.19.refs_1_, ...), custom_call_target="tpu_custom_call" | custom-call | flops 2415919104 | bytes 8388608 | tf_op jit(solution)/shard_map/pallas_call | solution.py:216
  97.7 1.6 %collective-permute-done.23 = f32[4,8,256]{2,1,0:T(8,128)S(1)} collective-permute-done((f32[4,8,256]{2,1,0:T(8,128)S(1)}, f32[4,8,256]{2,1,0:T(8,128)S(1)}, u32[]{:S(2)}, u32[]{:S(2)}) %collective-permute-start.23) | collective-permute-done | bytes 32800 | tf_op jit(solution)/shard_map/ppermute | solution.py:23
  101.1 2.9 %collective-permute-done.25 = f32[1,128]{1,0:T(1,128)S(1)} collective-permute-done((f32[1,128]{1,0:T(1,128)S(1)}, f32[1,128]{1,0:T(1,128)S(1)}, u32[]{:S(2)}, u32[]{:S(2)}) %collective-permute-start.25) | collective-permute-done | bytes 544 | tf_op jit(solution)/shard_map/ppermute | solution.py:23
  104.1 1.4 %collective-permute-start.28 = (f32[1,128]{1,0:T(1,128)S(1)}, f32[1,128]{1,0:T(1,128)S(1)}, u32[]{:S(2)}, u32[]{:S(2)}) collective-permute-start(f32[1,128]{1,0:T(1,128)S(1)} %bitcast_add_fusion), channel_id=1, source_target_pairs={{0,24},{4,28},{8,16},{12,20},{16,8},{20,12},{24,0},{28,4},{1,25},{... | collective-permute-start | bytes 1544 | tf_op jit(solution)/shard_map/ppermute | solution.py:23
  105.5 3.0 %collective-permute-start.26 = (f32[1,128]{1,0:T(1,128)S(1)}, f32[1,128]{1,0:T(1,128)S(1)}, u32[]{:S(2)}, u32[]{:S(2)}) collective-permute-start(f32[1,128]{1,0:T(1,128)S(1)} %bitcast_add_fusion), channel_id=1, source_target_pairs={{0,8},{4,12},{8,0},{12,4},{16,24},{20,28},{24,16},{28,20},{1,9},{5... | collective-permute-start | bytes 1544 | tf_op jit(solution)/shard_map/ppermute | solution.py:23
  (114 shorter events, 18.4 us)
Async XLA Ops:
  0.6 15.1 %collective-permute-start.1 = (bf16[128,2048]{1,0:T(8,128)(2,1)}, bf16[128,2048]{1,0:T(8,128)(2,1)S(1)}, u32[]{:S(2)}, u32[]{:S(2)}) collective-permute-start(bf16[128,2048]{1,0:T(8,128)(2,1)} %bitcast.109), channel_id=1, source_target_pairs={{0,4},{4,0},{8,12},{12,8},{16,20},{20,16},{24,28},{28,24},{1,5},{5... | collective-permute-start | bytes 1572872 | tf_op jit(solution)/shard_map/ppermute | solution.py:23
  3.6 13.8 %collective-permute-start = (bf16[128,2048]{1,0:T(8,128)(2,1)}, bf16[128,2048]{1,0:T(8,128)(2,1)S(1)}, u32[]{:S(2)}, u32[]{:S(2)}) collective-permute-start(bf16[128,2048]{1,0:T(8,128)(2,1)} %bitcast.110), channel_id=1, source_target_pairs={{0,16},{4,20},{8,0},{12,4},{16,24},{20,28},{24,8},{28,12},{1,17},{... | collective-permute-start | bytes 1572872 | tf_op jit(solution)/shard_map/ppermute | solution.py:30
  8.8 36.0 %collective-permute-start.7 = (bf16[512,1152]{1,0:T(8,128)(2,1)}, bf16[512,1152]{1,0:T(8,128)(2,1)S(1)}, u32[]{:S(2)}, u32[]{:S(2)}) collective-permute-start(bf16[512,1152]{1,0:T(8,128)(2,1)} %pad_maximum_fusion.1), channel_id=1, source_target_pairs={{0,2},{1,3},{2,0},{3,1},{4,6},{5,7},{6,4},{7,5},{8,10},{9,11},{10,... | collective-permute-start | bytes 3538952 | tf_op jit(solution)/shard_map/ppermute | solution.py:23
  15.8 14.2 %copy-start.8 = (bf16[128,2048]{1,0:T(8,128)(2,1)}, bf16[128,2048]{1,0:T(8,128)(2,1)S(1)}, u32[]{:S(2)}) copy-start(bf16[128,2048]{1,0:T(8,128)(2,1)S(1)} %collective-permute-done.1.refs_2_.refs_7_.refs_10_) | copy-start | bytes 1572868
  17.5 12.5 %collective-permute-start.3 = (bf16[128,2048]{1,0:T(8,128)(2,1)S(1)}, bf16[128,2048]{1,0:T(8,128)(2,1)S(1)}, u32[]{:S(2)}, u32[]{:S(2)}) collective-permute-start(bf16[128,2048]{1,0:T(8,128)(2,1)S(1)} %collective-permute-done.refs_1_.refs_6_.refs_9_), channel_id=1, source_target_pairs={{0,4},{4,0},{8,12},{12,8},{16,20},{20,16},{24,28},{28,24},{1,5},{5... | collective-permute-start | bytes 1572872 | tf_op jit(solution)/shard_map/ppermute | solution.py:23
  18.0 13.0 %collective-permute-start.2 = (bf16[128,2048]{1,0:T(8,128)(2,1)S(1)}, bf16[128,2048]{1,0:T(8,128)(2,1)}, u32[]{:S(2)}, u32[]{:S(2)}) collective-permute-start(bf16[128,2048]{1,0:T(8,128)(2,1)S(1)} %collective-permute-done.refs_1_.refs_6_.refs_9_), channel_id=1, source_target_pairs={{0,16},{4,20},{8,0},{12,4},{16,24},{20,28},{24,8},{28,12},{1,17},{... | collective-permute-start | bytes 1572872 | tf_op jit(solution)/shard_map/ppermute | solution.py:30
  21.3 8.7 %collective-permute-start.4 = (f32[1,128]{1,0:T(1,128)S(1)}, f32[1,128]{1,0:T(1,128)S(1)}, u32[]{:S(2)}, u32[]{:S(2)}) collective-permute-start(f32[1,128]{1,0:T(1,128)S(1)} %compare_select_fusion.1), channel_id=1, source_target_pairs={{0,4},{4,0},{8,12},{12,8},{16,20},{20,16},{24,28},{28,24},{1,5},{5... | collective-permute-start | bytes 1544 | tf_op jit(solution)/shard_map/ppermute | solution.py:23
  31.0 13.8 %collective-permute-start.6 = (bf16[128,2048]{1,0:T(8,128)(2,1)}, bf16[128,2048]{1,0:T(8,128)(2,1)S(1)}, u32[]{:S(2)}, u32[]{:S(2)}) collective-permute-start(bf16[128,2048]{1,0:T(8,128)(2,1)} %collective-permute-done.2.refs_3_.refs_8_.refs_11_), channel_id=1, source_target_pairs={{0,4},{4,0},{8,12},{12,8},{16,20},{20,16},{24,28},{28,24},{1,5},{5... | collective-permute-start | bytes 1572872 | tf_op jit(solution)/shard_map/ppermute | solution.py:23
  32.5 12.3 %collective-permute-start.5 = (bf16[128,2048]{1,0:T(8,128)(2,1)}, bf16[128,2048]{1,0:T(8,128)(2,1)S(1)}, u32[]{:S(2)}, u32[]{:S(2)}) collective-permute-start(bf16[128,2048]{1,0:T(8,128)(2,1)} %collective-permute-done.2.refs_3_.refs_8_.refs_11_), channel_id=1, source_target_pairs={{0,16},{4,20},{8,0},{12,4},{16,24},{20,28},{24,8},{28,12},{1,17},{... | collective-permute-start | bytes 1572872 | tf_op jit(solution)/shard_map/ppermute | solution.py:30
  36.0 28.4 %collective-permute-start.11 = (bf16[512,1152]{1,0:T(8,128)(2,1)}, bf16[512,1152]{1,0:T(8,128)(2,1)S(1)}, u32[]{:S(2)}, u32[]{:S(2)}) collective-permute-start(bf16[512,1152]{1,0:T(8,128)(2,1)} %pad_maximum_fusion), channel_id=1, source_target_pairs={{0,3},{1,2},{2,1},{3,0},{4,7},{5,6},{6,5},{7,4},{8,11},{9,10},{10,... | collective-permute-start | bytes 3538952 | tf_op jit(solution)/shard_map/ppermute | solution.py:23
  36.0 8.8 %collective-permute-start.8 = (f32[1,128]{1,0:T(1,128)S(1)}, f32[1,128]{1,0:T(1,128)S(1)}, u32[]{:S(2)}, u32[]{:S(2)}) collective-permute-start(f32[1,128]{1,0:T(1,128)S(1)} %add.71), channel_id=1, source_target_pairs={{0,8},{4,12},{8,0},{12,4},{16,24},{20,28},{24,16},{28,20},{1,9},{5... | collective-permute-start | bytes 1544 | tf_op jit(solution)/shard_map/ppermute | solution.py:23
  44.8 13.9 %copy-start.2 = (bf16[128,2048]{1,0:T(8,128)(2,1)}, bf16[128,2048]{1,0:T(8,128)(2,1)S(1)}, u32[]{:S(2)}) copy-start(bf16[128,2048]{1,0:T(8,128)(2,1)S(1)} %collective-permute-done.6.refs_1_.refs_4_.refs_6_.refs_14_) | copy-start | bytes 1572868
  44.8 13.9 %copy-start.3 = (bf16[128,2048]{1,0:T(8,128)(2,1)}, bf16[128,2048]{1,0:T(8,128)(2,1)S(1)}, u32[]{:S(2)}) copy-start(bf16[128,2048]{1,0:T(8,128)(2,1)S(1)} %collective-permute-done.5.refs_0_.refs_3_.refs_5_.refs_13_) | copy-start | bytes 1572868
  44.8 13.9 %collective-permute-start.10 = (bf16[128,2048]{1,0:T(8,128)(2,1)S(1)}, bf16[128,2048]{1,0:T(8,128)(2,1)S(1)}, u32[]{:S(2)}, u32[]{:S(2)}) collective-permute-start(bf16[128,2048]{1,0:T(8,128)(2,1)S(1)} %collective-permute-done.5.refs_0_.refs_3_.refs_5_.refs_13_), channel_id=1, source_target_pairs={{0,4},{4,0},{8,12},{12,8},{16,20},{20,16},{24,28},{28,24},{1,5},{5... | collective-permute-start | bytes 1572872 | tf_op jit(solution)/shard_map/ppermute | solution.py:23
  49.5 30.2 %collective-permute-start.12 = (bf16[512,1152]{1,0:T(8,128)(2,1)}, bf16[512,1152]{1,0:T(8,128)(2,1)}, u32[]{:S(2)}, u32[]{:S(2)}) collective-permute-start(bf16[512,1152]{1,0:T(8,128)(2,1)} %pad_maximum_fusion.3), channel_id=1, source_target_pairs={{0,1},{1,0},{2,3},{3,2},{4,5},{5,4},{6,7},{7,6},{8,9},{9,8},{10,11... | collective-permute-start | bytes 3538952 | tf_op jit(solution)/shard_map/ppermute | solution.py:23
  49.5 4.7 %collective-permute-start.9 = (f32[1,128]{1,0:T(1,128)S(1)}, f32[1,128]{1,0:T(1,128)S(1)}, u32[]{:S(2)}, u32[]{:S(2)}) collective-permute-start(f32[1,128]{1,0:T(1,128)S(1)} %add.73), channel_id=1, source_target_pairs={{0,16},{4,20},{8,24},{12,28},{16,0},{20,4},{24,8},{28,12},{1,17},{... | collective-permute-start | bytes 1544 | tf_op jit(solution)/shard_map/ppermute | solution.py:23
  64.4 14.3 %collective-permute-start.19 = (bf16[256,1024]{1,0:T(8,128)(2,1)S(1)}, bf16[256,1024]{1,0:T(8,128)(2,1)S(1)}, u32[]{:S(2)}, u32[]{:S(2)}) collective-permute-start(bf16[256,1024]{1,0:T(8,128)(2,1)S(1)} %shard_map.157.refs_1_), channel_id=1, source_target_pairs={{0,2},{1,3},{2,0},{3,1},{4,6},{5,7},{6,4},{7,5},{8,10},{9,11},{10,... | collective-permute-start | bytes 1572872 | tf_op jit(solution)/shard_map/ppermute | solution.py:23
  65.0 14.7 %collective-permute-start.13 = (bf16[256,1024]{1,0:T(8,128)(2,1)S(1)}, bf16[256,1024]{1,0:T(8,128)(2,1)S(1)}, u32[]{:S(2)}, u32[]{:S(2)}) collective-permute-start(bf16[256,1024]{1,0:T(8,128)(2,1)S(1)} %shard_map.157.refs_1_), channel_id=1, source_target_pairs={{0,1},{1,0},{2,3},{3,2},{4,5},{5,4},{6,7},{7,6},{8,9},{9,8},{10,11... | collective-permute-start | bytes 1572872 | tf_op jit(solution)/shard_map/ppermute | solution.py:23
  72.6 4.9 %collective-permute-start.14 = (bf16[256,1024]{1,0:T(8,128)(2,1)}, bf16[256,1024]{1,0:T(8,128)(2,1)S(1)}, u32[]{:S(2)}, u32[]{:S(2)}) collective-permute-start(bf16[256,1024]{1,0:T(8,128)(2,1)} %shard_map.158.refs_2_), channel_id=1, source_target_pairs={{0,1},{1,0},{2,3},{3,2},{4,5},{5,4},{6,7},{7,6},{8,9},{9,8},{10,11... | collective-permute-start | bytes 1572872 | tf_op jit(solution)/shard_map/ppermute | solution.py:23
  73.2 1.5 %collective-permute-start.15 = (f32[7,128]{1,0:T(8,128)S(1)}, f32[7,128]{1,0:T(8,128)S(1)}, u32[]{:S(2)}, u32[]{:S(2)}) collective-permute-start(f32[7,128]{1,0:T(8,128)S(1)} %select_maximum_fusion), channel_id=1, source_target_pairs={{0,1},{1,0},{2,3},{3,2},{4,5},{5,4},{6,7},{7,6},{8,9},{9,8},{10,11... | collective-permute-start | bytes 10760 | tf_op jit(solution)/shard_map/ppermute | solution.py:23
  74.8 15.0 %collective-permute-start.18 = (bf16[256,1024]{1,0:T(8,128)(2,1)}, bf16[256,1024]{1,0:T(8,128)(2,1)S(1)}, u32[]{:S(2)}, u32[]{:S(2)}) collective-permute-start(bf16[256,1024]{1,0:T(8,128)(2,1)} %shard_map.158.refs_2_), channel_id=1, source_target_pairs={{0,2},{1,3},{2,0},{3,1},{4,6},{5,7},{6,4},{7,5},{8,10},{9,11},{10,... | collective-permute-start | bytes 1572872 | tf_op jit(solution)/shard_map/ppermute | solution.py:23
  77.6 12.1 %collective-permute-start.16 = (f32[7,128]{1,0:T(8,128)S(1)}, f32[7,128]{1,0:T(8,128)S(1)}, u32[]{:S(2)}, u32[]{:S(2)}) collective-permute-start(f32[7,128]{1,0:T(8,128)S(1)} %select_maximum_fusion), channel_id=1, source_target_pairs={{0,2},{1,3},{2,0},{3,1},{4,6},{5,7},{6,4},{7,5},{8,10},{9,11},{10,... | collective-permute-start | bytes 10760 | tf_op jit(solution)/shard_map/ppermute | solution.py:23
  78.6 11.1 %collective-permute-start.17 = (f32[7,128]{1,0:T(8,128)S(1)}, f32[7,128]{1,0:T(8,128)S(1)}, u32[]{:S(2)}, u32[]{:S(2)}) collective-permute-start(f32[7,128]{1,0:T(8,128)S(1)} %collective-permute-done.15), channel_id=1, source_target_pairs={{0,2},{1,3},{2,0},{3,1},{4,6},{5,7},{6,4},{7,5},{8,10},{9,11},{10,... | collective-permute-start | bytes 10760 | tf_op jit(solution)/shard_map/ppermute | solution.py:23
  79.7 10.8 %collective-permute-start.20 = (bf16[256,1024]{1,0:T(8,128)(2,1)S(1)}, bf16[256,1024]{1,0:T(8,128)(2,1)S(1)}, u32[]{:S(2)}, u32[]{:S(2)}) collective-permute-start(bf16[256,1024]{1,0:T(8,128)(2,1)S(1)} %collective-permute-done.19.refs_1_), channel_id=1, source_target_pairs={{0,1},{1,0},{2,3},{3,2},{4,5},{5,4},{6,7},{7,6},{8,9},{9,8},{10,11... | collective-permute-start | bytes 1572872 | tf_op jit(solution)/shard_map/ppermute | solution.py:23
  89.7 1.9 %collective-permute-start.21 = (bf16[256,1024]{1,0:T(8,128)(2,1)S(1)}, bf16[256,1024]{1,0:T(8,128)(2,1)S(1)}, u32[]{:S(2)}, u32[]{:S(2)}) collective-permute-start(bf16[256,1024]{1,0:T(8,128)(2,1)S(1)} %collective-permute-done.18.refs_2_), channel_id=1, source_target_pairs={{0,1},{1,0},{2,3},{3,2},{4,5},{5,4},{6,7},{7,6},{8,9},{9,8},{10,11... | collective-permute-start | bytes 1572872 | tf_op jit(solution)/shard_map/ppermute | solution.py:23
  95.4 4.0 %collective-permute-start.23 = (f32[4,8,256]{2,1,0:T(8,128)S(1)}, f32[4,8,256]{2,1,0:T(8,128)S(1)}, u32[]{:S(2)}, u32[]{:S(2)}) collective-permute-start(f32[4,8,256]{2,1,0:T(8,128)S(1)} %pad_maximum_fusion.4), channel_id=1, source_target_pairs={{0,2},{1,3},{2,0},{3,1},{4,6},{5,7},{6,4},{7,5},{8,10},{9,11},{10,... | collective-permute-start | bytes 98312 | tf_op jit(solution)/shard_map/ppermute | solution.py:23
  96.5 3.7 %collective-permute-start.24 = (f32[4,8,256]{2,1,0:T(8,128)S(1)}, f32[4,8,256]{2,1,0:T(8,128)S(1)}, u32[]{:S(2)}, u32[]{:S(2)}) collective-permute-start(f32[4,8,256]{2,1,0:T(8,128)S(1)} %pad_maximum_fusion.4), channel_id=1, source_target_pairs={{0,3},{1,2},{2,1},{3,0},{4,7},{5,6},{6,5},{7,4},{8,11},{9,10},{10,... | collective-permute-start | bytes 98312 | tf_op jit(solution)/shard_map/ppermute | solution.py:23
  97.0 3.2 %collective-permute-start.22 = (f32[4,8,256]{2,1,0:T(8,128)S(1)}, f32[4,8,256]{2,1,0:T(8,128)S(1)}, u32[]{:S(2)}, u32[]{:S(2)}) collective-permute-start(f32[4,8,256]{2,1,0:T(8,128)S(1)} %pad_maximum_fusion.4), channel_id=1, source_target_pairs={{0,1},{1,0},{2,3},{3,2},{4,5},{5,4},{6,7},{7,6},{8,9},{9,8},{10,11... | collective-permute-start | bytes 98312 | tf_op jit(solution)/shard_map/ppermute | solution.py:23
  100.5 3.6 %collective-permute-start.25 = (f32[1,128]{1,0:T(1,128)S(1)}, f32[1,128]{1,0:T(1,128)S(1)}, u32[]{:S(2)}, u32[]{:S(2)}) collective-permute-start(f32[1,128]{1,0:T(1,128)S(1)} %bitcast.132), channel_id=1, source_target_pairs={{0,4},{4,0},{8,12},{12,8},{16,20},{20,16},{24,28},{28,24},{1,5},{5... | collective-permute-start | bytes 1544 | tf_op jit(solution)/shard_map/ppermute | solution.py:23
  104.1 6.1 %collective-permute-start.28 = (f32[1,128]{1,0:T(1,128)S(1)}, f32[1,128]{1,0:T(1,128)S(1)}, u32[]{:S(2)}, u32[]{:S(2)}) collective-permute-start(f32[1,128]{1,0:T(1,128)S(1)} %bitcast_add_fusion), channel_id=1, source_target_pairs={{0,24},{4,28},{8,16},{12,20},{16,8},{20,12},{24,0},{28,4},{1,25},{... | collective-permute-start | bytes 1544 | tf_op jit(solution)/shard_map/ppermute | solution.py:23
  105.5 4.7 %collective-permute-start.27 = (f32[1,128]{1,0:T(1,128)S(1)}, f32[1,128]{1,0:T(1,128)S(1)}, u32[]{:S(2)}, u32[]{:S(2)}) collective-permute-start(f32[1,128]{1,0:T(1,128)S(1)} %bitcast_add_fusion), channel_id=1, source_target_pairs={{0,16},{4,20},{8,24},{12,28},{16,0},{20,4},{24,8},{28,12},{1,17},{... | collective-permute-start | bytes 1544 | tf_op jit(solution)/shard_map/ppermute | solution.py:23
  105.5 4.7 %collective-permute-start.26 = (f32[1,128]{1,0:T(1,128)S(1)}, f32[1,128]{1,0:T(1,128)S(1)}, u32[]{:S(2)}, u32[]{:S(2)}) collective-permute-start(f32[1,128]{1,0:T(1,128)S(1)} %bitcast_add_fusion), channel_id=1, source_target_pairs={{0,8},{4,12},{8,0},{12,4},{16,24},{20,28},{24,16},{28,20},{1,9},{5... | collective-permute-start | bytes 1544 | tf_op jit(solution)/shard_map/ppermute | solution.py:23
  (16 other events, 137.5 us)
